TPU v7x, 512 devices: a whole 4x4x16 slice. The times are simulated.
512 devices in a mesh: head: 8 (over x_lo, y), ctx: 64 (over z, x_hi, core).
Axes of the slice: x: 4 (x_hi: 2, x_lo: 2; x = x_hi * 2 + x_lo), y: 4, z: 16, core: 2. Of those that a mesh axis runs over, the one named last changes fastest.
Arguments:
- queries: bfloat16 [65536, 1024], P(('ctx', 'head')), may hold values from -10.5 to 10.5
- key_rows: bfloat16 [65536, 1024], P(('ctx', 'head')), may hold values from -10.5 to 10.5
- value_rows: bfloat16 [65536, 1024], P(('ctx', 'head')), may hold values from -40 to 40
- cotangent: bfloat16 [65536, 1024], P(('ctx', 'head')), may hold values from -20 to 20
- block_list: int32 [512, 8], replicated, may hold values from 0 to 511, as said below
Outputs:
- attended: bfloat16 [65536, 1024], P(('ctx', 'head'))
- query_grad: bfloat16 [65536, 1024], P(('ctx', 'head'))
- key_grad: bfloat16 [65536, 1024], P(('ctx', 'head'))
- value_grad: bfloat16 [65536, 1024], P(('ctx', 'head'))
Inputs may be any that keep to these rules, and one draw needn't show every extreme that they name: `block_list`: entry 0 of row a is a itself; the other entries that differ from a are distinct. All rows of one ctx index have the same number of entries that differ from a, at least one; some ctx index has none equal to a past entry 0. Every listed block b satisfies |b // 8 - a // 8| <= 2, and every row lists a block whose distance is exactly 2.
All inputs are finite; a program needn't handle non-finite values.
Results may differ from a plain program's by a relative error of at most 0.038.
Values may be sent and summed in bfloat16 or wider, within the bound.
No kernel may reach another device: no remote copies, remote signals or barrier semaphores. Data moves between devices by JAX's collectives and lax.ppermute only.
A program may use at most 64 MiB of HBM per device.

v0:
```python
import jax
import jax.numpy as jnp
from jax import lax
from jax.sharding import PartitionSpec as P

HEAD_SIZE = 64
BLOCK = 128
REACH = 2


def passed_along(value, axis, steps):
    count = lax.axis_size(axis)
    pairs = [(source, (source + steps) % count) for source in range(count)]
    return lax.ppermute(value, axis, pairs)


def group_size(blocks):
    return max(1, min(blocks, 512 // BLOCK))


def per_device(queries, key_rows, value_rows, cotangent, block_list):
    head_queries, head_keys, head_values, head_grads = (
        lax.all_to_all(queries, "head", split_axis=1, concat_axis=0, tiled=True),
        lax.all_to_all(key_rows, "head", split_axis=1, concat_axis=0, tiled=True),
        lax.all_to_all(value_rows, "head", split_axis=1, concat_axis=0, tiled=True),
        lax.all_to_all(cotangent, "head", split_axis=1, concat_axis=0, tiled=True),
    )
    row_count, columns = head_queries.shape
    heads_local = columns // HEAD_SIZE
    blocks = row_count // BLOCK
    slot_total = block_list.shape[1]
    scaling = HEAD_SIZE ** (-0.5)
    window_size = 2 * REACH + 1
    position = lax.axis_index("ctx")
    listed = lax.dynamic_slice_in_dim(block_list, position * blocks, blocks, 0)
    own_blocks = position * blocks + jnp.arange(blocks, dtype=jnp.int32)
    window_index = listed - (position - REACH) * blocks
    slot_number = jnp.arange(slot_total, dtype=jnp.int32)
    alive_slots = (slot_number[None, :] == 0) | (listed != own_blocks[:, None])
    key_value = jnp.concatenate([head_keys, head_values], axis=1)
    current = passed_along(key_value, "ctx", -REACH)
    visited = [current]
    for repeat in range(2 * REACH):
        current = passed_along(current, "ctx", 1)
        visited.append(current)
    window = jnp.stack(visited[::-1])
    window_blocks = window.reshape(window_size * blocks, BLOCK, 2 * columns)
    per_group = group_size(blocks)
    groups = blocks // per_group
    pairs = per_group * slot_total

    def grouped(array):
        return array.reshape((groups, per_group) + array.shape[1:])

    def as_blocks(array):
        return grouped(array.reshape(blocks, BLOCK, heads_local, HEAD_SIZE))

    def fetch(indices):
        picked = window_blocks[indices]
        layout = indices.shape + (BLOCK, heads_local, HEAD_SIZE)
        return (picked[..., :columns].reshape(layout), picked[..., columns:].reshape(layout))

    def scored(query_group, key_group, alive):
        scores = (
            jnp.einsum(
                "aqhd,ajkhd->ahqjk", query_group, key_group, preferred_element_type=jnp.float32
            )
            * scaling
        )
        return jnp.where(alive[:, None, None, :, None], scores, -jnp.inf)

    def forward(unused, inputs):
        query_group, indices, alive = inputs
        key_group, value_group = fetch(indices)
        scores = scored(query_group, key_group, alive)
        row_max = jnp.max(scores, axis=(3, 4))
        weights = jnp.exp(scores - row_max[..., None, None])
        totals = jnp.sum(weights, axis=(3, 4))
        mixed = jnp.einsum(
            "ahqjk,ajkhd->aqhd",
            weights.astype(jnp.bfloat16),
            value_group,
            preferred_element_type=jnp.float32,
        )
        mixed = mixed / jnp.transpose(totals, (0, 2, 1))[..., None]
        return (unused, (mixed.astype(jnp.bfloat16), row_max + jnp.log(totals)))

    query_groups = as_blocks(head_queries)
    grad_groups = as_blocks(head_grads)
    index_groups = grouped(window_index)
    alive_groups = grouped(alive_slots)
    unused, (mixed_groups, log_totals) = lax.scan(
        forward, jnp.zeros((), jnp.float32), (query_groups, index_groups, alive_groups)
    )
    attended_head = mixed_groups.reshape(row_count, columns)
    attended = lax.all_to_all(attended_head, "head", split_axis=0, concat_axis=1, tiled=True)

    def backward(accum, inputs):
        query_group, grad_group, out_group, log_total, indices, alive = inputs
        key_group, value_group = fetch(indices)
        scores = scored(query_group, key_group, alive)
        recomputed = jnp.exp(scores - log_total[..., None, None])
        recomputed_b = recomputed.astype(jnp.bfloat16)
        value_part = jnp.einsum(
            "ahqjk,aqhd->ajkhd", recomputed_b, grad_group, preferred_element_type=jnp.float32
        )
        dprob = jnp.einsum(
            "aqhd,ajkhd->ahqjk", grad_group, value_group, preferred_element_type=jnp.float32
        )
        delta = jnp.sum(grad_group.astype(jnp.float32) * out_group.astype(jnp.float32), axis=3)
        dscore = recomputed * (dprob - jnp.transpose(delta, (0, 2, 1))[..., None, None])
        dscore_b = dscore.astype(jnp.bfloat16)
        query_part = (
            jnp.einsum("ahqjk,ajkhd->aqhd", dscore_b, key_group, preferred_element_type=jnp.float32)
            * scaling
        ).astype(jnp.bfloat16)
        key_part = (
            jnp.einsum(
                "ahqjk,aqhd->ajkhd", dscore_b, query_group, preferred_element_type=jnp.float32
            )
            * scaling
        )
        terms = jnp.concatenate(
            [key_part.reshape(pairs, BLOCK, columns), value_part.reshape(pairs, BLOCK, columns)],
            axis=2,
        )
        accum = accum.at[indices.reshape(pairs)].add(terms)
        return (accum, query_part)

    initial = jnp.zeros((window_size * blocks, BLOCK, 2 * columns), jnp.float32)
    accum, query_parts = lax.scan(
        backward,
        initial,
        (query_groups, grad_groups, mixed_groups, log_totals, index_groups, alive_groups),
    )
    partials = accum.reshape(window_size, row_count, 2 * columns)
    carried = partials[2 * REACH]
    for level in range(2 * REACH - 1, -1, -1):
        carried = (
            passed_along(carried.astype(jnp.bfloat16), "ctx", 1).astype(carried.dtype)
            + partials[level]
        )
    owned = passed_along(carried.astype(jnp.bfloat16), "ctx", -REACH).astype(carried.dtype)
    key_head = owned[:, :columns].astype(jnp.bfloat16)
    value_head = owned[:, columns:].astype(jnp.bfloat16)
    query_head = query_parts.reshape(row_count, columns)
    query_grad, key_grad, value_grad = (
        lax.all_to_all(query_head, "head", split_axis=0, concat_axis=1, tiled=True),
        lax.all_to_all(key_head, "head", split_axis=0, concat_axis=1, tiled=True),
        lax.all_to_all(value_head, "head", split_axis=0, concat_axis=1, tiled=True),
    )
    return (attended, query_grad, key_grad, value_grad)


def solution(mesh):
    placed = (
        P(("ctx", "head"), None),
        P(("ctx", "head"), None),
        P(("ctx", "head"), None),
        P(("ctx", "head"), None),
        P(),
    )
    return jax.shard_map(
        per_device,
        mesh=mesh,
        in_specs=placed,
        out_specs=(
            P(("ctx", "head"), None),
            P(("ctx", "head"), None),
            P(("ctx", "head"), None),
            P(("ctx", "head"), None),
        ),
        check_vma=False,
    )
```

profile of v0, /device:TPU:4, one launch (start us, length us, event | category | flops | bytes accessed | tf_op | source)
XLA Modules:
  0.0 306.6 jit_solution(13781764974386530441)
XLA Ops:
  2.7 5.1 %all-to-all-start = ((bf16[128,8,128]{2,0,1:T(8,128)(2,1)}), bf16[128,8,128]{2,0,1:T(8,128)(2,1)S(1)}, u32[]{:S(2)}, u32[]{:S(2)}) async-start(bf16[128,8,128]{2,0,1:T(8,128)(2,1)} %copy.89), calls=%async_computation | async-start | bytes 524288 | tf_op jit(solution)/shard_map/all_to_all | solution.py:24
  9.1 5.9 %all-to-all-done = bf16[128,8,128]{2,0,1:T(8,128)(2,1)S(1)} async-done(((bf16[128,8,128]{2,0,1:T(8,128)(2,1)}), bf16[128,8,128]{2,0,1:T(8,128)(2,1)S(1)}, u32[]{:S(2)}, u32[]{:S(2)}) %all-to-all-start) | async-done | bytes 262176 | tf_op jit(solution)/shard_map/all_to_all | solution.py:24
  15.0 9.8 %all_to_all.146 = bf16[128,8,128]{2,0,1:T(8,128)(2,1)S(1)} all-to-all(bf16[128,8,128]{2,0,1:T(8,128)(2,1)S(1)} %copy.91), channel_id=1, replica_groups=mesh['head'=8,'ctx'=64] {'head'}, dimensions={1} | all-to-all | bytes 524288 | tf_op jit(solution)/shard_map/all_to_all | solution.py:25
  24.9 6.0 %collective-permute-start = (bf16[1024,256]{1,0:T(8,128)(2,1)S(1)}, bf16[1024,256]{1,0:T(8,128)(2,1)S(1)}, u32[]{:S(2)}, u32[]{:S(2)}) collective-permute-start(bf16[1024,256]{1,0:T(8,128)(2,1)S(1)} %pad_maximum_fusion.1), channel_id=1, source_target_pairs={{0,62},{1,63},{2,0},{3,1},{4,2},{5,3},{6,4},{7,5},{8,6},{9,7},{10,... | collective-permute-start | bytes 1572872 | tf_op jit(solution)/shard_map/ppermute | solution.py:14
  30.9 9.2 %collective-permute-done = bf16[1024,256]{1,0:T(8,128)(2,1)S(1)} collective-permute-done((bf16[1024,256]{1,0:T(8,128)(2,1)S(1)}, bf16[1024,256]{1,0:T(8,128)(2,1)S(1)}, u32[]{:S(2)}, u32[]{:S(2)}) %collective-permute-start) | collective-permute-done | bytes 524320 | tf_op jit(solution)/shard_map/ppermute | solution.py:14
  42.0 10.2 %collective-permute-done.1 = bf16[1024,256]{1,0:T(8,128)(2,1)S(1)} collective-permute-done((bf16[1024,256]{1,0:T(8,128)(2,1)S(1)}, bf16[1024,256]{1,0:T(8,128)(2,1)S(1)}, u32[]{:S(2)}, u32[]{:S(2)}) %collective-permute-start.1) | collective-permute-done | bytes 524320 | tf_op jit(solution)/shard_map/ppermute | solution.py:14
  55.0 10.1 %collective-permute-done.2 = bf16[1024,256]{1,0:T(8,128)(2,1)S(1)} collective-permute-done((bf16[1024,256]{1,0:T(8,128)(2,1)S(1)}, bf16[1024,256]{1,0:T(8,128)(2,1)S(1)}, u32[]{:S(2)}, u32[]{:S(2)}) %collective-permute-start.2) | collective-permute-done | bytes 524320 | tf_op jit(solution)/shard_map/ppermute | solution.py:14
  72.3 4.8 %collective-permute-done.3 = bf16[1024,256]{1,0:T(8,128)(2,1)S(1)} collective-permute-done((bf16[1024,256]{1,0:T(8,128)(2,1)S(1)}, bf16[1024,256]{1,0:T(8,128)(2,1)S(1)}, u32[]{:S(2)}, u32[]{:S(2)}) %collective-permute-start.3) | collective-permute-done | bytes 524320 | tf_op jit(solution)/shard_map/ppermute | solution.py:14
  79.1 11.4 %collective-permute-done.4 = bf16[1024,256]{1,0:T(8,128)(2,1)S(1)} collective-permute-done((bf16[1024,256]{1,0:T(8,128)(2,1)S(1)}, bf16[1024,256]{1,0:T(8,128)(2,1)S(1)}, u32[]{:S(2)}, u32[]{:S(2)}) %collective-permute-start.4) | collective-permute-done | bytes 524320 | tf_op jit(solution)/shard_map/ppermute | solution.py:14
  97.4 21.6 %while.24 = (s32[]{:T(128)}, bf16[2,4,128,2,64]{2,4,3,1,0:T(8,128)(2,1)S(1)}, f32[2,4,2,128]{3,2,1,0:T(2,128)S(1)}, s32[2,4,8]{2,1,0:T(4,128)S(1)}, bf16[40,128,...) while((s32[]{:T(128)}, ...), condition=%wide.region_3.4_spmd, body=%wide.region_0.3_spmd.sunk | while | flops 280100960 | bytes 48535560 | solution.py:92
  122.8 61.9 %while.25 = (s32[]{:T(128)}, f32[40,128,256]{2,1,0:T(8,128)}, bf16[2,4,128,2,64]{2,4,3,1,0:T(8,128)(2,1)}, s32[2,4,8]{2,1,0:T(4,128)S(1)}, bf16[2,4,128,2,64]{2,...) while((s32[]{:T(128)}, f32[40,128,256]{2,1,0:T(8,128)}, ...), condition=%wide.region_7.8_spmd, body=%wide.region_4.7_spmd.sunk | while | flops 684589248 | bytes 98466568 | solution.py:131
  138.5 5.7 %copy.144 = f32[32,128,256]{2,1,0:T(8,128)} copy(f32[32,128,256]{1,2,0:T(8,128)} %pad_maximum_fusion.3) | data formatting | bytes 8388608 | tf_op jit(solution)/shard_map/while/body/eval_jaxpr/concatenate | solution.py:123
  144.2 9.7 %scatter_fusion = f32[40,128,256]{2,1,0:T(8,128)} fusion(f32[40,128,256]{2,1,0:T(8,128)} %get-tuple-element.315, s32[32]{0:T(128)S(1)} %fusion.111, f32[32,128,256]{2,1,0:T(8,128)} %copy.144), kind=kCustom, calls=%fused_computation.2.clone.1 | custom fusion | flops 1048576 | bytes 12583040 | tf_op jit(solution)/shard_map/while/body/eval_jaxpr/scatter-add | solution.py:127
  169.6 5.7 %copy.144 = f32[32,128,256]{2,1,0:T(8,128)} copy(f32[32,128,256]{1,2,0:T(8,128)} %pad_maximum_fusion.3) | data formatting | bytes 8388608 | tf_op jit(solution)/shard_map/while/body/eval_jaxpr/concatenate | solution.py:123
  175.3 9.4 %scatter_fusion = f32[40,128,256]{2,1,0:T(8,128)} fusion(f32[40,128,256]{2,1,0:T(8,128)} %get-tuple-element.315, s32[32]{0:T(128)S(1)} %fusion.111, f32[32,128,256]{2,1,0:T(8,128)} %copy.144), kind=kCustom, calls=%fused_computation.2.clone.1 | custom fusion | flops 1048576 | bytes 12583040 | tf_op jit(solution)/shard_map/while/body/eval_jaxpr/scatter-add | solution.py:127
  190.4 8.2 %collective-permute-done.5 = bf16[1024,256]{1,0:T(8,128)(2,1)S(1)} collective-permute-done((bf16[1024,256]{1,0:T(8,128)(2,1)S(1)}, bf16[1024,256]{1,0:T(8,128)(2,1)S(1)}, u32[]{:S(2)}, u32[]{:S(2)}) %collective-permute-start.5) | collective-permute-done | bytes 524320 | tf_op jit(solution)/shard_map/ppermute | solution.py:14
  200.9 12.2 %collective-permute-done.6 = bf16[1024,256]{1,0:T(8,128)(2,1)S(1)} collective-permute-done((bf16[1024,256]{1,0:T(8,128)(2,1)S(1)}, bf16[1024,256]{1,0:T(8,128)(2,1)S(1)}, u32[]{:S(2)}, u32[]{:S(2)}) %collective-permute-start.6) | collective-permute-done | bytes 524320 | tf_op jit(solution)/shard_map/ppermute | solution.py:14
  215.2 12.2 %collective-permute-done.7 = bf16[1024,256]{1,0:T(8,128)(2,1)S(1)} collective-permute-done((bf16[1024,256]{1,0:T(8,128)(2,1)S(1)}, bf16[1024,256]{1,0:T(8,128)(2,1)S(1)}, u32[]{:S(2)}, u32[]{:S(2)}) %collective-permute-start.7) | collective-permute-done | bytes 524320 | tf_op jit(solution)/shard_map/ppermute | solution.py:14
  229.4 12.2 %collective-permute-done.8 = bf16[1024,256]{1,0:T(8,128)(2,1)S(1)} collective-permute-done((bf16[1024,256]{1,0:T(8,128)(2,1)S(1)}, bf16[1024,256]{1,0:T(8,128)(2,1)S(1)}, u32[]{:S(2)}, u32[]{:S(2)}) %collective-permute-start.8) | collective-permute-done | bytes 524320 | tf_op jit(solution)/shard_map/ppermute | solution.py:14
  241.7 18.0 %collective-permute-start.9 = (bf16[1024,256]{1,0:T(8,128)(2,1)S(1)}, bf16[1024,256]{1,0:T(8,128)(2,1)S(1)}, u32[]{:S(2)}, u32[]{:S(2)}) collective-permute-start(bf16[1024,256]{1,0:T(8,128)(2,1)S(1)} %fusion.63), channel_id=1, source_target_pairs={{0,62},{1,63},{2,0},{3,1},{4,2},{5,3},{6,4},{7,5},{8,6},{9,7},{10,... | collective-permute-start | bytes 1572872 | tf_op jit(solution)/shard_map/ppermute | solution.py:14
  260.7 6.1 %all-to-all-start.3 = ((bf16[8,128,128]{2,1,0:T(8,128)(2,1)}), bf16[8,128,128]{2,1,0:T(8,128)(2,1)S(1)}, u32[]{:S(2)}, u32[]{:S(2)}) async-start(bf16[8,128,128]{2,1,0:T(8,128)(2,1)} %copy.93), calls=%async_computation.3 | async-start | bytes 524288 | tf_op jit(solution)/shard_map/all_to_all | solution.py:96
  268.5 5.6 %all-to-all-done.3 = bf16[8,128,128]{2,1,0:T(8,128)(2,1)S(1)} async-done(((bf16[8,128,128]{2,1,0:T(8,128)(2,1)}), bf16[8,128,128]{2,1,0:T(8,128)(2,1)S(1)}, u32[]{:S(2)}, u32[]{:S(2)}) %all-to-all-start.3) | async-done | bytes 262176 | tf_op jit(solution)/shard_map/all_to_all | solution.py:96
  278.5 6.7 %all-to-all-done.5 = bf16[8,128,128]{2,1,0:T(8,128)(2,1)S(1)} async-done(((bf16[8,128,128]{2,1,0:T(8,128)(2,1)}), bf16[8,128,128]{2,1,0:T(8,128)(2,1)S(1)}, u32[]{:S(2)}, u32[]{:S(2)}) %all-to-all-start.5) | async-done | bytes 262176 | tf_op jit(solution)/shard_map/all_to_all | solution.py:148
  285.2 9.8 %all_to_all.147 = bf16[8,128,128]{2,1,0:T(8,128)(2,1)S(1)} all-to-all(bf16[8,128,128]{2,1,0:T(8,128)(2,1)S(1)} %bitcast.243), channel_id=1, replica_groups=mesh['head'=8,'ctx'=64] {'head'}, dimensions={0} | all-to-all | bytes 524288 | tf_op jit(solution)/shard_map/all_to_all | solution.py:149
  (145 shorter events, 111.5 us)
Async XLA Ops:
  0.6 70.6 %copy-start = (s32[512,8]{0,1:T(8,128)S(1)}, s32[512,8]{0,1:T(8,128)}, u32[]{:S(2)}) copy-start(s32[512,8]{0,1:T(8,128)} %param.13) | copy-start | bytes 49156
  0.6 66.3 %copy-start.9 = (bf16[128,1024]{1,0:T(8,128)(2,1)S(1)}, bf16[128,1024]{1,0:T(8,128)(2,1)}, u32[]{:S(2)}) copy-start(bf16[128,1024]{1,0:T(8,128)(2,1)} %param.9) | copy-start | bytes 786436
  0.7 70.8 %copy-start.10 = (bf16[128,1024]{1,0:T(8,128)(2,1)S(1)}, bf16[128,1024]{1,0:T(8,128)(2,1)}, u32[]{:S(2)}) copy-start(bf16[128,1024]{1,0:T(8,128)(2,1)} %param.12) | copy-start | bytes 786436
  2.7 12.3 %all-to-all-start = ((bf16[128,8,128]{2,0,1:T(8,128)(2,1)}), bf16[128,8,128]{2,0,1:T(8,128)(2,1)S(1)}, u32[]{:S(2)}, u32[]{:S(2)}) async-start(bf16[128,8,128]{2,0,1:T(8,128)(2,1)} %copy.89), calls=%async_computation | async-start | bytes 524288 | tf_op jit(solution)/shard_map/all_to_all | solution.py:24
  24.9 15.2 %collective-permute-start = (bf16[1024,256]{1,0:T(8,128)(2,1)S(1)}, bf16[1024,256]{1,0:T(8,128)(2,1)S(1)}, u32[]{:S(2)}, u32[]{:S(2)}) collective-permute-start(bf16[1024,256]{1,0:T(8,128)(2,1)S(1)} %pad_maximum_fusion.1), channel_id=1, source_target_pairs={{0,62},{1,63},{2,0},{3,1},{4,2},{5,3},{6,4},{7,5},{8,6},{9,7},{10,... | collective-permute-start | bytes 1572872 | tf_op jit(solution)/shard_map/ppermute | solution.py:14
  40.1 12.1 %collective-permute-start.1 = (bf16[1024,256]{1,0:T(8,128)(2,1)S(1)}, bf16[1024,256]{1,0:T(8,128)(2,1)S(1)}, u32[]{:S(2)}, u32[]{:S(2)}) collective-permute-start(bf16[1024,256]{1,0:T(8,128)(2,1)S(1)} %collective-permute-done), channel_id=1, source_target_pairs={{0,1},{1,2},{2,3},{3,4},{4,5},{5,6},{6,7},{7,8},{8,9},{9,10},{10,1... | collective-permute-start | bytes 1572872 | tf_op jit(solution)/shard_map/ppermute | solution.py:14
  53.1 12.0 %collective-permute-start.2 = (bf16[1024,256]{1,0:T(8,128)(2,1)S(1)}, bf16[1024,256]{1,0:T(8,128)(2,1)S(1)}, u32[]{:S(2)}, u32[]{:S(2)}) collective-permute-start(bf16[1024,256]{1,0:T(8,128)(2,1)S(1)} %collective-permute-done.1), channel_id=1, source_target_pairs={{0,1},{1,2},{2,3},{3,4},{4,5},{5,6},{6,7},{7,8},{8,9},{9,10},{10,1... | collective-permute-start | bytes 1572872 | tf_op jit(solution)/shard_map/ppermute | solution.py:14
  65.1 14.0 %copy-start.7 = (bf16[1024,256]{1,0:T(8,128)(2,1)}, bf16[1024,256]{1,0:T(8,128)(2,1)S(1)}, u32[]{:S(2)}) copy-start(bf16[1024,256]{1,0:T(8,128)(2,1)S(1)} %collective-permute-done.2) | copy-start | bytes 1572868
  65.1 12.0 %collective-permute-start.3 = (bf16[1024,256]{1,0:T(8,128)(2,1)S(1)}, bf16[1024,256]{1,0:T(8,128)(2,1)S(1)}, u32[]{:S(2)}, u32[]{:S(2)}) collective-permute-start(bf16[1024,256]{1,0:T(8,128)(2,1)S(1)} %collective-permute-done.2), channel_id=1, source_target_pairs={{0,1},{1,2},{2,3},{3,4},{4,5},{5,6},{6,7},{7,8},{8,9},{9,10},{10,1... | collective-permute-start | bytes 1572872 | tf_op jit(solution)/shard_map/ppermute | solution.py:14
  67.8 26.0 %all-to-all-start.2 = ((bf16[128,8,128]{0,2,1:T(8,128)(2,1)}), bf16[128,8,128]{0,2,1:T(8,128)(2,1)S(1)}, u32[]{:S(2)}, u32[]{:S(2)}) async-start(bf16[128,8,128]{0,2,1:T(8,128)(2,1)} %bitcast.54), calls=%async_computation.2 | async-start | bytes 524288 | tf_op jit(solution)/shard_map/all_to_all | solution.py:23
  77.0 2.0 copy-start.8
  77.1 13.4 %collective-permute-start.4 = (bf16[1024,256]{1,0:T(8,128)(2,1)S(1)}, bf16[1024,256]{1,0:T(8,128)(2,1)S(1)}, u32[]{:S(2)}, u32[]{:S(2)}) collective-permute-start(bf16[1024,256]{1,0:T(8,128)(2,1)S(1)} %collective-permute-done.3), channel_id=1, source_target_pairs={{0,1},{1,2},{2,3},{3,4},{4,5},{5,6},{6,7},{7,8},{8,9},{9,10},{10,1... | collective-permute-start | bytes 1572872 | tf_op jit(solution)/shard_map/ppermute | solution.py:14
  93.8 25.3 %all-to-all-start.4 = ((bf16[128,8,128]{0,2,1:T(8,128)(2,1)}), bf16[128,8,128]{0,2,1:T(8,128)(2,1)S(1)}, u32[]{:S(2)}, u32[]{:S(2)}) async-start(bf16[128,8,128]{0,2,1:T(8,128)(2,1)} %bitcast.61), calls=%async_computation.4 | async-start | bytes 524288 | tf_op jit(solution)/shard_map/all_to_all | solution.py:26
  144.2 9.7 %copy-start.5 = (bf16[40,128,256]{2,1,0:T(8,128)(2,1)S(1)}, bf16[40,128,256]{2,1,0:T(8,128)(2,1)}, u32[]{:S(2)}) copy-start(bf16[40,128,256]{2,1,0:T(8,128)(2,1)} %copy-done.4) | copy-start | bytes 7864324 | tf_op jit(solution)/shard_map/while
  175.3 9.4 %copy-start.5 = (bf16[40,128,256]{2,1,0:T(8,128)(2,1)S(1)}, bf16[40,128,256]{2,1,0:T(8,128)(2,1)}, u32[]{:S(2)}) copy-start(bf16[40,128,256]{2,1,0:T(8,128)(2,1)} %copy-done.4) | copy-start | bytes 7864324 | tf_op jit(solution)/shard_map/while
  185.9 12.7 %collective-permute-start.5 = (bf16[1024,256]{1,0:T(8,128)(2,1)S(1)}, bf16[1024,256]{1,0:T(8,128)(2,1)S(1)}, u32[]{:S(2)}, u32[]{:S(2)}) collective-permute-start(bf16[1024,256]{1,0:T(8,128)(2,1)S(1)} %bitcast.245), channel_id=1, source_target_pairs={{0,1},{1,2},{2,3},{3,4},{4,5},{5,6},{6,7},{7,8},{8,9},{9,10},{10,1... | collective-permute-start | bytes 1572872 | tf_op jit(solution)/shard_map/ppermute | solution.py:14
  198.8 14.4 %collective-permute-start.6 = (bf16[1024,256]{1,0:T(8,128)(2,1)S(1)}, bf16[1024,256]{1,0:T(8,128)(2,1)S(1)}, u32[]{:S(2)}, u32[]{:S(2)}) collective-permute-start(bf16[1024,256]{1,0:T(8,128)(2,1)S(1)} %fusion.66), channel_id=1, source_target_pairs={{0,1},{1,2},{2,3},{3,4},{4,5},{5,6},{6,7},{7,8},{8,9},{9,10},{10,1... | collective-permute-start | bytes 1572872 | tf_op jit(solution)/shard_map/ppermute | solution.py:14
  213.3 14.1 %collective-permute-start.7 = (bf16[1024,256]{1,0:T(8,128)(2,1)S(1)}, bf16[1024,256]{1,0:T(8,128)(2,1)S(1)}, u32[]{:S(2)}, u32[]{:S(2)}) collective-permute-start(bf16[1024,256]{1,0:T(8,128)(2,1)S(1)} %fusion.65), channel_id=1, source_target_pairs={{0,1},{1,2},{2,3},{3,4},{4,5},{5,6},{6,7},{7,8},{8,9},{9,10},{10,1... | collective-permute-start | bytes 1572872 | tf_op jit(solution)/shard_map/ppermute | solution.py:14
  227.5 14.1 %collective-permute-start.8 = (bf16[1024,256]{1,0:T(8,128)(2,1)S(1)}, bf16[1024,256]{1,0:T(8,128)(2,1)S(1)}, u32[]{:S(2)}, u32[]{:S(2)}) collective-permute-start(bf16[1024,256]{1,0:T(8,128)(2,1)S(1)} %fusion.64), channel_id=1, source_target_pairs={{0,1},{1,2},{2,3},{3,4},{4,5},{5,6},{6,7},{7,8},{8,9},{9,10},{10,1... | collective-permute-start | bytes 1572872 | tf_op jit(solution)/shard_map/ppermute | solution.py:14
  241.7 36.0 %collective-permute-start.9 = (bf16[1024,256]{1,0:T(8,128)(2,1)S(1)}, bf16[1024,256]{1,0:T(8,128)(2,1)S(1)}, u32[]{:S(2)}, u32[]{:S(2)}) collective-permute-start(bf16[1024,256]{1,0:T(8,128)(2,1)S(1)} %fusion.63), channel_id=1, source_target_pairs={{0,62},{1,63},{2,0},{3,1},{4,2},{5,3},{6,4},{7,5},{8,6},{9,7},{10,... | collective-permute-start | bytes 1572872 | tf_op jit(solution)/shard_map/ppermute | solution.py:14
  259.8 46.8 %copy-start.1 = (s32[512,8]{0,1:T(8,128)S(1)}, s32[512,8]{0,1:T(8,128)}, u32[]{:S(2)}) copy-start(s32[512,8]{0,1:T(8,128)} %param.13) | copy-start | bytes 49156
  260.7 13.4 %all-to-all-start.3 = ((bf16[8,128,128]{2,1,0:T(8,128)(2,1)}), bf16[8,128,128]{2,1,0:T(8,128)(2,1)S(1)}, u32[]{:S(2)}, u32[]{:S(2)}) async-start(bf16[8,128,128]{2,1,0:T(8,128)(2,1)} %copy.93), calls=%async_computation.3 | async-start | bytes 524288 | tf_op jit(solution)/shard_map/all_to_all | solution.py:96
  274.1 11.1 %all-to-all-start.5 = ((bf16[8,128,128]{2,1,0:T(8,128)(2,1)}), bf16[8,128,128]{2,1,0:T(8,128)(2,1)S(1)}, u32[]{:S(2)}, u32[]{:S(2)}) async-start(bf16[8,128,128]{2,1,0:T(8,128)(2,1)} %copy.96), calls=%async_computation.5 | async-start | bytes 524288 | tf_op jit(solution)/shard_map/all_to_all | solution.py:148
  295.0 10.6 %all-to-all-start.7 = ((bf16[8,128,128]{2,1,0:T(8,128)(2,1)}), bf16[8,128,128]{2,1,0:T(8,128)(2,1)S(1)}, u32[]{:S(2)}, u32[]{:S(2)}) async-start(bf16[8,128,128]{2,1,0:T(8,128)(2,1)} %bitcast.75), calls=%async_computation.7 | async-start | bytes 524288 | tf_op jit(solution)/shard_map/all_to_all | solution.py:150
  (7 other events, 10.3 us)
where the time goes:
time: 309 us; the launch traced here: 307 us
  waiting for transfers between devices  113 us (37%)
  local copies, waits for them, and re-layouts  65 us (21%)
  starting transfers between devices  64.9 us (21%)
  other arithmetic  27 us (9%)
  blocking collectives  19.6 us (6%)
  matrix products  16.2 us (5%)
    ppermute x10, waiting for transfers between devices, passed_along(): return lax.ppermute(value, axis, pairs)  90.5 us
    ppermute x10, starting transfers between devices, passed_along(): return lax.ppermute(value, axis, pairs)  39.6 us
    gather x8, local copies, waits for them, and re-layouts, fetch(): picked = window_blocks[indices]  21 us
    scatter-add x2, other arithmetic, backward(): accum = accum.at[indices.reshape(pairs)].add(terms)  19.1 us
    concatenate x2, local copies, waits for them, and re-layouts, backward(): jnp.concatenate([key_part.reshape(pairs, BLOCK, columns), value_part.resh...  11.4 us
    unnamed x25, local copies, waits for them, and re-layouts  9.89 us
    all_to_all x1, blocking collectives, per_device(): lax.all_to_all(value_rows, 'head', split_axis=1, concat_axis=0, tiled=True)  9.8 us
    all_to_all x1, blocking collectives, per_device(): lax.all_to_all(key_head, 'head', split_axis=0, concat_axis=1, tiled=True)  9.79 us
  transfers between devices with their start and end apart: 16, of which 13 were waited for; matrix products, arithmetic and copies ran while one was open for 11% of the time, Pallas kernels for 0%

commit v1 on v0

v1 whole, which is shorter than its diff:
```python
import jax
import jax.numpy as jnp
import numpy as np
from jax import lax
from jax.experimental import pallas as pl
from jax.experimental.pallas import tpu as pltpu
from jax.sharding import Mesh, PartitionSpec as P

HEADS = 16
HEAD_SIZE = 64
BLOCK = 128
WIDTH = 2 * HEAD_SIZE
SCALING = HEAD_SIZE ** (-0.5)
PLANE = 32
HALF = PLANE // 2
SLOTS = 8
AXES = ("x_hi", "core", "x_lo", "y")
VMEM_LIMIT = 40 * 1024 * 1024


def lane_pair(left, right, odd):
    start = HEAD_SIZE if odd else 0
    return jnp.concatenate(
        [left[:, start : start + HEAD_SIZE], right[:, start : start + HEAD_SIZE]], axis=1
    )


def slot_of(head, core):
    return (head // 8) * 16 + core * 8 + head % 8


def pack_kernel(place, q_ref, k_ref, v_ref, g_ref, out_ref):
    x_hi = place[1]
    for pair in range(HEADS // 2):
        columns = slice(pair * WIDTH, (pair + 1) * WIDTH)
        q, k, v, g = q_ref[:, columns], k_ref[:, columns], v_ref[:, columns], g_ref[:, columns]
        for odd in range(2):
            head = 2 * pair + odd
            out_ref[slot_of(head, x_hi)] = lane_pair(k, v, odd)
            out_ref[slot_of(head, 1 - x_hi)] = lane_pair(q, g, odd)


def unpack_kernel(place, in_ref, o_ref, dq_ref, dk_ref, dv_ref):
    x_hi = place[1]
    for pair in range(HEADS // 2):
        columns = slice(pair * WIDTH, (pair + 1) * WIDTH)
        even, odd = 2 * pair, 2 * pair + 1
        kv0, kv1 = in_ref[slot_of(even, x_hi)], in_ref[slot_of(odd, x_hi)]
        qo0, qo1 = in_ref[slot_of(even, 1 - x_hi)], in_ref[slot_of(odd, 1 - x_hi)]
        dk_ref[:, columns] = lane_pair(kv0, kv1, 0)
        dv_ref[:, columns] = lane_pair(kv0, kv1, 1)
        dq_ref[:, columns] = lane_pair(qo0, qo1, 0)
        o_ref[:, columns] = lane_pair(qo0, qo1, 1)


def attention_kernel(
    place, index, alive, qg_ref, own_ref, mate_ref, halo_ref,
    qo_ref, own_out, mate_out, halo_out, window, accum, sems,
):
    core = place[0]
    own_at = 2 * core
    halo_at = 2 - own_at
    copies = [
        pltpu.make_async_copy(own_ref, window.at[pl.ds(own_at * HALF, HALF)], sems.at[0]),
        pltpu.make_async_copy(mate_ref, window.at[pl.ds(HALF, HALF)], sems.at[1]),
        pltpu.make_async_copy(halo_ref, window.at[pl.ds(halo_at * HALF, HALF)], sems.at[2]),
    ]
    for copy in copies:
        copy.start()
    accum[...] = jnp.zeros_like(accum)
    for copy in copies:
        copy.wait()
    lane = lax.broadcasted_iota(jnp.int32, (BLOCK, WIDTH), 1)
    left = lane < HEAD_SIZE

    def step(i, carry):
        qg = qg_ref[i]
        zero = jnp.zeros_like(qg)
        rows = jnp.concatenate(
            [jnp.where(left, qg * jnp.bfloat16(SCALING), zero), jnp.where(left, zero, qg)], axis=0
        )
        listed = [index[i, s] for s in range(SLOTS)]
        kv = jnp.concatenate([window[b] for b in listed], axis=0)
        both = lax.dot_general(
            rows, kv, (((1,), (1,)), ((), ())), preferred_element_type=jnp.float32
        )
        scores = jnp.concatenate(
            [
                jnp.where(
                    alive[i, s] > 0, both[:BLOCK, s * BLOCK : (s + 1) * BLOCK], -jnp.inf
                )
                for s in range(SLOTS)
            ],
            axis=1,
        )
        dprob = both[BLOCK:]
        row_max = jnp.max(scores, axis=1, keepdims=True)
        weights = jnp.exp(scores - row_max)
        totals = jnp.sum(weights, axis=1, keepdims=True)
        probs = weights * (1.0 / totals)
        terms = probs * dprob
        delta = jnp.sum(terms, axis=1, keepdims=True)
        dscore = terms - probs * delta
        stacked = jnp.concatenate(
            [dscore.astype(jnp.bfloat16), probs.astype(jnp.bfloat16)], axis=0
        )
        mixed = jnp.dot(stacked, kv, preferred_element_type=jnp.float32)
        qo_ref[i] = jnp.where(left, mixed[:BLOCK] * SCALING, mixed[BLOCK:]).astype(jnp.bfloat16)
        grads = lax.dot_general(
            stacked, rows, (((0,), (0,)), ((), ())), preferred_element_type=jnp.float32
        )
        for s in range(SLOTS):
            accum[listed[s]] += grads[s * BLOCK : (s + 1) * BLOCK]
        return carry

    lax.fori_loop(0, HALF, step, 0)
    own_out[...] = accum[pl.ds(own_at * HALF, HALF)]
    mate_out[...] = accum[HALF : 2 * HALF].astype(jnp.bfloat16)
    halo_out[...] = accum[pl.ds(halo_at * HALF, HALF)].astype(jnp.bfloat16)


def sum_kernel(place, qo_ref, own_ref, mate_ref, halo_ref, out_ref):
    core = place[0]
    total = own_ref[...] + mate_ref[...].astype(jnp.float32) + halo_ref[...].astype(jnp.float32)
    out_ref[pl.ds(core * HALF, HALF)] = total.astype(jnp.bfloat16)
    out_ref[pl.ds((1 - core) * HALF, HALF)] = qo_ref[...]


SMEM = pl.BlockSpec(memory_space=pltpu.SMEM)
VMEM = pl.BlockSpec(memory_space=pltpu.VMEM)
ANY = pl.BlockSpec(memory_space=pl.ANY)
PARAMS = pltpu.CompilerParams(vmem_limit_bytes=VMEM_LIMIT)


def moved(value, axes, target):
    sizes = [lax.axis_size(a) for a in axes]
    pairs = []
    for source in range(int(np.prod(sizes))):
        spot = [int(t) for t in np.unravel_index(source, sizes)]
        pairs.append((source, int(np.ravel_multi_index(target(*spot), sizes))))
    return lax.ppermute(value, axes, pairs)


def to_mate(value):
    return moved(value, ("core",), lambda c: (1 - c,))


def per_device(queries, key_rows, value_rows, cotangent, block_list):
    depth = lax.axis_size("z")
    core, x_hi, z = lax.axis_index("core"), lax.axis_index("x_hi"), lax.axis_index("z")
    place = jnp.stack([core, x_hi]).astype(jnp.int32)
    packed = pl.pallas_call(
        pack_kernel,
        out_shape=jax.ShapeDtypeStruct((PLANE, BLOCK, WIDTH), jnp.bfloat16),
        in_specs=[SMEM] + [VMEM] * 4,
        out_specs=VMEM,
        compiler_params=PARAMS,
        name="pack",
    )(place, queries, key_rows, value_rows, cotangent)
    received = lax.all_to_all(packed, AXES, 0, 0, tiled=True)
    key_value = lax.dynamic_slice_in_dim(received, core * HALF, HALF, 0)
    query_grad_rows = lax.dynamic_slice_in_dim(received, (1 - core) * HALF, HALF, 0)
    mate = to_mate(key_value)
    halo = moved(
        key_value, ("z", "core"), lambda z, c: ((z + (1 if c else depth - 1)) % depth, c)
    )
    first_query = z * PLANE + (1 - core) * HALF
    first_key = z * PLANE - core * HALF
    listed = lax.dynamic_slice_in_dim(block_list, first_query, HALF, 0)
    own_blocks = first_query + jnp.arange(HALF, dtype=jnp.int32)
    alive = (jnp.arange(SLOTS)[None, :] == 0) | (listed != own_blocks[:, None])
    index = listed - first_key
    half = (HALF, BLOCK, WIDTH)
    query_out, own_part, mate_part, halo_part = pl.pallas_call(
        attention_kernel,
        out_shape=[
            jax.ShapeDtypeStruct(half, jnp.bfloat16),
            jax.ShapeDtypeStruct(half, jnp.float32),
            jax.ShapeDtypeStruct(half, jnp.bfloat16),
            jax.ShapeDtypeStruct(half, jnp.bfloat16),
        ],
        in_specs=[SMEM] * 3 + [VMEM] + [ANY] * 3,
        out_specs=[VMEM] * 4,
        scratch_shapes=[
            pltpu.VMEM((3 * HALF, BLOCK, WIDTH), jnp.bfloat16),
            pltpu.VMEM((3 * HALF, BLOCK, WIDTH), jnp.float32),
            pltpu.SemaphoreType.DMA((3,)),
        ],
        compiler_params=PARAMS,
        name="attention",
    )(place, index, alive.astype(jnp.int32), query_grad_rows, key_value, mate, halo)
    mate_sum = to_mate(mate_part)
    halo_sum = moved(
        halo_part, ("z", "core"), lambda z, c: ((z + (depth - 1 if c else 1)) % depth, c)
    )
    outgoing = pl.pallas_call(
        sum_kernel,
        out_shape=jax.ShapeDtypeStruct((PLANE, BLOCK, WIDTH), jnp.bfloat16),
        in_specs=[SMEM] + [VMEM] * 4,
        out_specs=VMEM,
        compiler_params=PARAMS,
        name="total",
    )(place, query_out, own_part, mate_sum, halo_sum)
    returned = lax.all_to_all(outgoing, AXES, 0, 0, tiled=True)
    rows = jax.ShapeDtypeStruct(queries.shape, jnp.bfloat16)
    return pl.pallas_call(
        unpack_kernel,
        out_shape=[rows] * 4,
        in_specs=[SMEM, VMEM],
        out_specs=[VMEM] * 4,
        compiler_params=PARAMS,
        name="unpack",
    )(place, returned)


def solution(mesh):
    fine = Mesh(mesh.devices.reshape(2, 4, 16, 2, 2), ("x_lo", "y", "z", "x_hi", "core"))
    rows = P(("z", "x_hi", "core", "x_lo", "y"), None)
    return jax.shard_map(
        per_device,
        mesh=fine,
        in_specs=(rows,) * 4 + (P(),),
        out_specs=(rows,) * 4,
        check_vma=False,
    )
```

time: 309 us -> 105 us (0.34)
  the two profiles are of different devices: /device:TPU:4 before, /device:TPU:1 now
where the time goes in v1:
time: 105 us; the launch traced here: 104 us
  starting transfers between devices  29.7 us (28%)
  waiting for transfers between devices  26.5 us (25%)
  blocking collectives  21.9 us (21%)
  Pallas kernels  21.4 us (20%)
  local copies, waits for them, and re-layouts  4.03 us (4%)
    all_to_all x1, blocking collectives, per_device(): returned = lax.all_to_all(outgoing, AXES, 0, 0, tiled=True)  21.9 us
    ppermute x4, starting transfers between devices, moved(): return lax.ppermute(value, axes, pairs)  19.2 us
    pallas_call x1, Pallas kernels, per_device(): pl.pallas_call(attention_kernel, out_shape=[jax.ShapeDtypeStruct(half, jn...  16.9 us
    all_to_all x1, waiting for transfers between devices, per_device(): received = lax.all_to_all(packed, AXES, 0, 0, tiled=True)  16.2 us
    all_to_all x1, starting transfers between devices, per_device(): received = lax.all_to_all(packed, AXES, 0, 0, tiled=True)  10.5 us
    ppermute x4, waiting for transfers between devices, moved(): return lax.ppermute(value, axes, pairs)  10.2 us
    unnamed x11, local copies, waits for them, and re-layouts  3.88 us
  transfers between devices with their start and end apart: 5, of which 3 were waited for; matrix products, arithmetic and copies ran while one was open for 0% of the time, Pallas kernels for 0%

profile of v1, /device:TPU:1, one launch (start us, length us, event | category | flops | bytes accessed | tf_op | source)
XLA Modules:
  0.0 104.4 jit_solution(2584248282943100907)
XLA Ops:
  0.6 0.0 copy-start
  0.7 0.1 pad_add_fusion.place
  0.7 0.9 copy-done.1
  1.7 0.9 copy-done.2
  2.6 0.9 copy-done.3
  3.6 0.9 copy-done.4
  4.5 1.9 %pack.1 = bf16[32,128,128]{2,1,0:T(8,128)(2,1)} custom-call(s32[2]{0:T(128)S(1)} %pad_add_fusion.place, bf16[128,1024]{1,0:T(8,128)(2,1)S(1)} %copy-done.1, bf16[128,1024]{1,0:T(8,128)(2,1)S(1)} %copy-done.2, bf16[128,1024]{1,0:T(8,128)(2,1)S(1)} %copy-done.3, bf16[128,1024]{1,0:T(8,128)(2,1)S(1)} %copy-done.4), custom_call_target="tpu_custom_call" | custom-call | tf_op jit(solution)/shard_map/pack/pallas_call | solution.py:152
  6.4 10.5 %all-to-all-start = ((bf16[32,128,128]{2,1,0:T(8,128)(2,1)}), bf16[32,128,128]{2,1,0:T(8,128)(2,1)S(1)}, u32[]{:S(2)}, u32[]{:S(2)}) async-start(bf16[32,128,128]{2,1,0:T(8,128)(2,1)} %pack.1), calls=%async_computation | async-start | bytes 2097152 | tf_op jit(solution)/shard_map/all_to_all | solution.py:160
  16.9 0.1 constant_dynamic-slice_fusion.2
  17.0 0.1 copy.10
  17.1 16.2 %all-to-all-done = bf16[32,128,128]{2,1,0:T(8,128)(2,1)S(1)} async-done(((bf16[32,128,128]{2,1,0:T(8,128)(2,1)}), bf16[32,128,128]{2,1,0:T(8,128)(2,1)S(1)}, u32[]{:S(2)}, u32[]{:S(2)}) %all-to-all-start) | async-done | bytes 1048608 | tf_op jit(solution)/shard_map/all_to_all | solution.py:160
  33.3 0.1 constant_dynamic-slice_fusion
  33.4 1.9 %collective-permute-start.1 = (bf16[16,128,128]{2,1,0:T(8,128)(2,1)S(1)}, bf16[16,128,128]{2,1,0:T(8,128)(2,1)S(1)}, u32[]{:S(2)}, u32[]{:S(2)}) collective-permute-start(bf16[16,128,128]{2,1,0:T(8,128)(2,1)S(1)} %get-tuple-element.12.own_ref), channel_id=1, source_target_pairs={{0,60},{1,5},{4,0},{5,9},{8,4},{9,13},{12,8},{13,17},{16,12},{17,2... | collective-permute-start | bytes 1572872 | tf_op jit(solution)/shard_map/ppermute | solution.py:141
  35.3 9.5 %collective-permute-start = (bf16[16,128,128]{2,1,0:T(8,128)(2,1)S(1)}, bf16[16,128,128]{2,1,0:T(8,128)(2,1)S(1)}, u32[]{:S(2)}, u32[]{:S(2)}) collective-permute-start(bf16[16,128,128]{2,1,0:T(8,128)(2,1)S(1)} %get-tuple-element.12.own_ref), channel_id=1, source_target_pairs={{0,1},{1,0},{2,3},{3,2},{4,5},{5,4},{6,7},{7,6},{8,9},{9,8},{10,11... | collective-permute-start | bytes 1572872 | tf_op jit(solution)/shard_map/ppermute | solution.py:141
  44.9 0.1 or_convert_fusion.alive
  45.0 4.1 %collective-permute-done.1.halo_ref = bf16[16,128,128]{2,1,0:T(8,128)(2,1)S(1)} collective-permute-done((bf16[16,128,128]{2,1,0:T(8,128)(2,1)S(1)}, bf16[16,128,128]{2,1,0:T(8,128)(2,1)S(1)}, u32[]{:S(2)}, u32[]{:S(2)}) %collective-permute-start.1) | collective-permute-done | bytes 524320 | tf_op jit(solution)/shard_map/ppermute | solution.py:141
  49.1 0.0 collective-permute-done.mate_ref
  49.1 16.9 %attention.1 = (bf16[16,128,128]{2,1,0:T(8,128)(2,1)S(1)}, f32[16,128,128]{2,1,0:T(8,128)S(1)}, bf16[16,128,128]{2,1,0:T(8,128)(2,1)S(1)}, bf16[16,128,128]{2,1,0:T(8,128)(2,1)S(1)}) custom-call(s32[2]{0:T(128)S(1)} %pad_add_fusion.place, s32[16,8]{1,0:T(8,128)S(1)} %broadcast_subtract_fusion.index, s32[16,8]{1,0:T(8,128)S(1)} %or_convert_fusion.alive, ...), custom_call_target="tpu_custom_call" | custom-call | tf_op jit(solution)/shard_map/attention/pallas_call | solution.py:174
  66.0 2.4 %collective-permute-start.2 = (bf16[16,128,128]{2,1,0:T(8,128)(2,1)S(1)}, bf16[16,128,128]{2,1,0:T(8,128)(2,1)S(1)}, u32[]{:S(2)}, u32[]{:S(2)}) collective-permute-start(bf16[16,128,128]{2,1,0:T(8,128)(2,1)S(1)} %get-tuple-element.10), channel_id=1, source_target_pairs={{0,1},{1,0},{2,3},{3,2},{4,5},{5,4},{6,7},{7,6},{8,9},{9,8},{10,11... | collective-permute-start | bytes 1572872 | tf_op jit(solution)/shard_map/ppermute | solution.py:141
  68.4 5.4 %collective-permute-start.3 = (bf16[16,128,128]{2,1,0:T(8,128)(2,1)S(1)}, bf16[16,128,128]{2,1,0:T(8,128)(2,1)S(1)}, u32[]{:S(2)}, u32[]{:S(2)}) collective-permute-start(bf16[16,128,128]{2,1,0:T(8,128)(2,1)S(1)} %get-tuple-element.11), channel_id=1, source_target_pairs={{0,4},{1,61},{4,8},{5,1},{8,12},{9,5},{12,16},{13,9},{16,20},{17,1... | collective-permute-start | bytes 1572872 | tf_op jit(solution)/shard_map/ppermute | solution.py:141
  73.8 6.1 %collective-permute-done.3.halo_ref = bf16[16,128,128]{2,1,0:T(8,128)(2,1)S(1)} collective-permute-done((bf16[16,128,128]{2,1,0:T(8,128)(2,1)S(1)}, bf16[16,128,128]{2,1,0:T(8,128)(2,1)S(1)}, u32[]{:S(2)}, u32[]{:S(2)}) %collective-permute-start.3) | collective-permute-done | bytes 524320 | tf_op jit(solution)/shard_map/ppermute | solution.py:141
  79.9 0.7 total.1
  80.7 21.9 %all_to_all.10.in_ref = bf16[32,128,128]{2,1,0:T(8,128)(2,1)S(1)} all-to-all(bf16[32,128,128]{2,1,0:T(8,128)(2,1)S(1)} %total.1), channel_id=1, replica_groups=mesh['x_lo'=2,'y'=4,'z'=16,'x_hi'=2,'core'=2] {'x_hi','core','x_lo','y'}, dimensions={0} | all-to-all | bytes 2097152 | tf_op jit(solution)/shard_map/all_to_all | solution.py:204
  102.6 1.9 %unpack.1 = (bf16[128,1024]{1,0:T(8,128)(2,1)}, bf16[128,1024]{1,0:T(8,128)(2,1)}, bf16[128,1024]{1,0:T(8,128)(2,1)}, bf16[128,1024]{1,0:T(8,128)(2,1)}) custom-call(s32[2]{0:T(128)S(1)} %pad_add_fusion.place, bf16[32,128,128]{2,1,0:T(8,128)(2,1)S(1)} %all_to_all.10.in_ref), custom_call_target="tpu_custom_call" | custom-call | tf_op jit(solution)/shard_map/unpack/pallas_call | solution.py:206
  (9 shorter events, 0.0 us)
Async XLA Ops:
  0.6 16.3 %copy-start = (s32[512,8]{0,1:T(8,128)S(1)}, s32[512,8]{0,1:T(8,128)}, u32[]{:S(2)}) copy-start(s32[512,8]{0,1:T(8,128)} %param.9) | copy-start | bytes 49156
  0.7 1.0 copy-start.1
  1.7 0.9 copy-start.2
  2.6 0.9 copy-start.3
  3.6 0.9 copy-start.4
  6.4 26.9 %all-to-all-start = ((bf16[32,128,128]{2,1,0:T(8,128)(2,1)}), bf16[32,128,128]{2,1,0:T(8,128)(2,1)S(1)}, u32[]{:S(2)}, u32[]{:S(2)}) async-start(bf16[32,128,128]{2,1,0:T(8,128)(2,1)} %pack.1), calls=%async_computation | async-start | bytes 2097152 | tf_op jit(solution)/shard_map/all_to_all | solution.py:160
  33.4 15.7 %collective-permute-start.1 = (bf16[16,128,128]{2,1,0:T(8,128)(2,1)S(1)}, bf16[16,128,128]{2,1,0:T(8,128)(2,1)S(1)}, u32[]{:S(2)}, u32[]{:S(2)}) collective-permute-start(bf16[16,128,128]{2,1,0:T(8,128)(2,1)S(1)} %get-tuple-element.12.own_ref), channel_id=1, source_target_pairs={{0,60},{1,5},{4,0},{5,9},{8,4},{9,13},{12,8},{13,17},{16,12},{17,2... | collective-permute-start | bytes 1572872 | tf_op jit(solution)/shard_map/ppermute | solution.py:141
  35.3 13.8 %collective-permute-start = (bf16[16,128,128]{2,1,0:T(8,128)(2,1)S(1)}, bf16[16,128,128]{2,1,0:T(8,128)(2,1)S(1)}, u32[]{:S(2)}, u32[]{:S(2)}) collective-permute-start(bf16[16,128,128]{2,1,0:T(8,128)(2,1)S(1)} %get-tuple-element.12.own_ref), channel_id=1, source_target_pairs={{0,1},{1,0},{2,3},{3,2},{4,5},{5,4},{6,7},{7,6},{8,9},{9,8},{10,11... | collective-permute-start | bytes 1572872 | tf_op jit(solution)/shard_map/ppermute | solution.py:141
  66.0 7.8 %collective-permute-start.2 = (bf16[16,128,128]{2,1,0:T(8,128)(2,1)S(1)}, bf16[16,128,128]{2,1,0:T(8,128)(2,1)S(1)}, u32[]{:S(2)}, u32[]{:S(2)}) collective-permute-start(bf16[16,128,128]{2,1,0:T(8,128)(2,1)S(1)} %get-tuple-element.10), channel_id=1, source_target_pairs={{0,1},{1,0},{2,3},{3,2},{4,5},{5,4},{6,7},{7,6},{8,9},{9,8},{10,11... | collective-permute-start | bytes 1572872 | tf_op jit(solution)/shard_map/ppermute | solution.py:141
  68.4 11.5 %collective-permute-start.3 = (bf16[16,128,128]{2,1,0:T(8,128)(2,1)S(1)}, bf16[16,128,128]{2,1,0:T(8,128)(2,1)S(1)}, u32[]{:S(2)}, u32[]{:S(2)}) collective-permute-start(bf16[16,128,128]{2,1,0:T(8,128)(2,1)S(1)} %get-tuple-element.11), channel_id=1, source_target_pairs={{0,4},{1,61},{4,8},{5,1},{8,12},{9,5},{12,16},{13,9},{16,20},{17,1... | collective-permute-start | bytes 1572872 | tf_op jit(solution)/shard_map/ppermute | solution.py:141

commit v2 on v1

--- a/solution.py
+++ b/solution.py
@@ -16,6 +16,10 @@
 SLOTS = 8
 AXES = ("x_hi", "core", "x_lo", "y")
 VMEM_LIMIT = 40 * 1024 * 1024
+KEYS = SLOTS * BLOCK
+CHUNK = 16
+PART = 256
+PARTS = HEADS * HEAD_SIZE // PART
 
 
 def lane_pair(left, right, odd):
@@ -29,9 +33,25 @@
     return (head // 8) * 16 + core * 8 + head % 8
 
 
-def pack_kernel(place, q_ref, k_ref, v_ref, g_ref, out_ref):
+def pack_kernel(place, q_hbm, k_hbm, v_hbm, g_hbm, out_ref, q_ref, k_ref, v_ref, g_ref, sems):
     x_hi = place[1]
+    parts = [slice(p * PART, (p + 1) * PART) for p in range(PARTS)]
+    copies = [
+        [
+            pltpu.make_async_copy(source.at[:, part], target.at[:, part], sems.at[p, n])
+            for n, (source, target) in enumerate(
+                ((k_hbm, k_ref), (v_hbm, v_ref), (q_hbm, q_ref), (g_hbm, g_ref))
+            )
+        ]
+        for p, part in enumerate(parts)
+    ]
+    for group in copies:
+        for copy in group:
+            copy.start()
     for pair in range(HEADS // 2):
+        if pair * WIDTH % PART == 0:
+            for copy in copies[pair * WIDTH // PART]:
+                copy.wait()
         columns = slice(pair * WIDTH, (pair + 1) * WIDTH)
         q, k, v, g = q_ref[:, columns], k_ref[:, columns], v_ref[:, columns], g_ref[:, columns]
         for odd in range(2):
@@ -40,8 +60,11 @@
             out_ref[slot_of(head, 1 - x_hi)] = lane_pair(q, g, odd)
 
 
-def unpack_kernel(place, in_ref, o_ref, dq_ref, dk_ref, dv_ref):
+def unpack_kernel(
+    place, in_ref, o_hbm, dq_hbm, dk_hbm, dv_hbm, o_ref, dq_ref, dk_ref, dv_ref, sems
+):
     x_hi = place[1]
+    copies = []
     for pair in range(HEADS // 2):
         columns = slice(pair * WIDTH, (pair + 1) * WIDTH)
         even, odd = 2 * pair, 2 * pair + 1
@@ -51,11 +74,23 @@
         dv_ref[:, columns] = lane_pair(kv0, kv1, 1)
         dq_ref[:, columns] = lane_pair(qo0, qo1, 0)
         o_ref[:, columns] = lane_pair(qo0, qo1, 1)
+        if (pair + 1) * WIDTH % PART == 0:
+            p = pair * WIDTH // PART
+            part = slice(p * PART, (p + 1) * PART)
+            for n, (source, target) in enumerate(
+                ((o_ref, o_hbm), (dq_ref, dq_hbm), (dk_ref, dk_hbm), (dv_ref, dv_hbm))
+            ):
+                copy = pltpu.make_async_copy(source.at[:, part], target.at[:, part], sems.at[p, n])
+                copy.start()
+                copies.append(copy)
+    for copy in copies:
+        copy.wait()
 
 
 def attention_kernel(
     place, index, alive, qg_ref, own_ref, mate_ref, halo_ref,
-    qo_ref, own_out, mate_out, halo_out, window, accum, sems,
+    qo_ref, own_out, mate_out, halo_out,
+    window, accum, both_even, both_odd, pair_even, pair_odd, sems,
 ):
     core = place[0]
     own_at = 2 * core
@@ -68,55 +103,72 @@
     for copy in copies:
         copy.start()
     accum[...] = jnp.zeros_like(accum)
+    pair_odd[...] = jnp.zeros_like(pair_odd)
     for copy in copies:
         copy.wait()
-    lane = lax.broadcasted_iota(jnp.int32, (BLOCK, WIDTH), 1)
-    left = lane < HEAD_SIZE
-
-    def step(i, carry):
+    left = lax.broadcasted_iota(jnp.int32, (BLOCK, WIDTH), 1) < HEAD_SIZE
+
+    def listed_rows(i):
+        return jnp.concatenate([window[index[i, s]] for s in range(SLOTS)], axis=0)
+
+    def query_rows(i):
         qg = qg_ref[i]
         zero = jnp.zeros_like(qg)
-        rows = jnp.concatenate(
+        return jnp.concatenate(
             [jnp.where(left, qg * jnp.bfloat16(SCALING), zero), jnp.where(left, zero, qg)], axis=0
         )
-        listed = [index[i, s] for s in range(SLOTS)]
-        kv = jnp.concatenate([window[b] for b in listed], axis=0)
-        both = lax.dot_general(
-            rows, kv, (((1,), (1,)), ((), ())), preferred_element_type=jnp.float32
+
+    def products(i, both):
+        both[...] = lax.dot_general(
+            query_rows(i), listed_rows(i), (((1,), (1,)), ((), ())),
+            preferred_element_type=jnp.float32,
         )
-        scores = jnp.concatenate(
-            [
-                jnp.where(
-                    alive[i, s] > 0, both[:BLOCK, s * BLOCK : (s + 1) * BLOCK], -jnp.inf
-                )
-                for s in range(SLOTS)
-            ],
-            axis=1,
-        )
-        dprob = both[BLOCK:]
-        row_max = jnp.max(scores, axis=1, keepdims=True)
-        weights = jnp.exp(scores - row_max)
-        totals = jnp.sum(weights, axis=1, keepdims=True)
-        probs = weights * (1.0 / totals)
-        terms = probs * dprob
-        delta = jnp.sum(terms, axis=1, keepdims=True)
-        dscore = terms - probs * delta
-        stacked = jnp.concatenate(
-            [dscore.astype(jnp.bfloat16), probs.astype(jnp.bfloat16)], axis=0
-        )
-        mixed = jnp.dot(stacked, kv, preferred_element_type=jnp.float32)
+
+    def weigh(i, both, pair):
+        live = [alive[i, s] > 0 for s in range(SLOTS)]
+        for r in range(0, BLOCK, CHUNK):
+            scores = jnp.concatenate(
+                [
+                    jnp.where(live[s], both[r : r + CHUNK, s * BLOCK : (s + 1) * BLOCK], -jnp.inf)
+                    for s in range(SLOTS)
+                ],
+                axis=1,
+            )
+            dprob = both[BLOCK + r : BLOCK + r + CHUNK]
+            weights = jnp.exp(scores - jnp.max(scores, axis=1, keepdims=True))
+            probs = weights * (1.0 / jnp.sum(weights, axis=1, keepdims=True))
+            terms = probs * dprob
+            dscore = terms - probs * jnp.sum(terms, axis=1, keepdims=True)
+            pair[r : r + CHUNK] = dscore.astype(jnp.bfloat16)
+            pair[BLOCK + r : BLOCK + r + CHUNK] = probs.astype(jnp.bfloat16)
+
+    def results(i, pair):
+        stacked = pair[...]
+        mixed = jnp.dot(stacked, listed_rows(i), preferred_element_type=jnp.float32)
         qo_ref[i] = jnp.where(left, mixed[:BLOCK] * SCALING, mixed[BLOCK:]).astype(jnp.bfloat16)
         grads = lax.dot_general(
-            stacked, rows, (((0,), (0,)), ((), ())), preferred_element_type=jnp.float32
+            stacked, query_rows(i), (((0,), (0,)), ((), ())), preferred_element_type=jnp.float32
         )
         for s in range(SLOTS):
-            accum[listed[s]] += grads[s * BLOCK : (s + 1) * BLOCK]
+            accum[index[i, s]] += grads[s * BLOCK : (s + 1) * BLOCK]
+
+    products(0, both_even)
+
+    def step(j, carry):
+        even, odd = 2 * j, 2 * j + 1
+        products(odd, both_odd)
+        weigh(even, both_even, pair_even)
+        results(jnp.maximum(even - 1, 0), pair_odd)
+        products(jnp.minimum(even + 2, HALF - 1), both_even)
+        weigh(odd, both_odd, pair_odd)
+        results(even, pair_even)
         return carry
 
-    lax.fori_loop(0, HALF, step, 0)
+    lax.fori_loop(0, HALF // 2, step, 0)
+    results(HALF - 1, pair_odd)
+    halo_out[...] = accum[pl.ds(halo_at * HALF, HALF)].astype(jnp.bfloat16)
+    mate_out[...] = accum[HALF : 2 * HALF].astype(jnp.bfloat16)
     own_out[...] = accum[pl.ds(own_at * HALF, HALF)]
-    mate_out[...] = accum[HALF : 2 * HALF].astype(jnp.bfloat16)
-    halo_out[...] = accum[pl.ds(halo_at * HALF, HALF)].astype(jnp.bfloat16)
 
 
 def sum_kernel(place, qo_ref, own_ref, mate_ref, halo_ref, out_ref):
@@ -130,6 +182,7 @@
 VMEM = pl.BlockSpec(memory_space=pltpu.VMEM)
 ANY = pl.BlockSpec(memory_space=pl.ANY)
 PARAMS = pltpu.CompilerParams(vmem_limit_bytes=VMEM_LIMIT)
+EDGE_PARAMS = pltpu.CompilerParams(vmem_limit_bytes=60 * 1024 * 1024)
 
 
 def moved(value, axes, target):
@@ -152,9 +205,11 @@
     packed = pl.pallas_call(
         pack_kernel,
         out_shape=jax.ShapeDtypeStruct((PLANE, BLOCK, WIDTH), jnp.bfloat16),
-        in_specs=[SMEM] + [VMEM] * 4,
+        in_specs=[SMEM] + [ANY] * 4,
         out_specs=VMEM,
-        compiler_params=PARAMS,
+        scratch_shapes=[pltpu.VMEM(queries.shape, jnp.bfloat16)] * 4
+        + [pltpu.SemaphoreType.DMA((PARTS, 4))],
+        compiler_params=EDGE_PARAMS,
         name="pack",
     )(place, queries, key_rows, value_rows, cotangent)
     received = lax.all_to_all(packed, AXES, 0, 0, tiled=True)
@@ -184,6 +239,10 @@
         scratch_shapes=[
             pltpu.VMEM((3 * HALF, BLOCK, WIDTH), jnp.bfloat16),
             pltpu.VMEM((3 * HALF, BLOCK, WIDTH), jnp.float32),
+            pltpu.VMEM((2 * BLOCK, KEYS), jnp.float32),
+            pltpu.VMEM((2 * BLOCK, KEYS), jnp.float32),
+            pltpu.VMEM((2 * BLOCK, KEYS), jnp.bfloat16),
+            pltpu.VMEM((2 * BLOCK, KEYS), jnp.bfloat16),
             pltpu.SemaphoreType.DMA((3,)),
         ],
         compiler_params=PARAMS,
@@ -207,7 +266,9 @@
         unpack_kernel,
         out_shape=[rows] * 4,
         in_specs=[SMEM, VMEM],
-        out_specs=[VMEM] * 4,
+        out_specs=[ANY] * 4,
+        scratch_shapes=[pltpu.VMEM(queries.shape, jnp.bfloat16)] * 4
+        + [pltpu.SemaphoreType.DMA((PARTS, 4))],
         compiler_params=PARAMS,
         name="unpack",
     )(place, returned)

time: 105 us -> 97.2 us (0.926)
  Pallas kernels: 21.4 us -> 17.1 us
  local copies, waits for them, and re-layouts: 4.03 us -> 0.24 us
    pallas_call x1, Pallas kernels: 16.9 us -> 11.3 us  [per_device(): pl.pallas_call(attention_kernel, out_shape=[jax.ShapeDtypeStruct(half, jn...]
    unnamed x11 -> x5, local copies, waits for them, and re-layouts: 3.88 us -> 0.09 us
    pallas_call x1, Pallas kernels: 1.86 us -> 3.27 us  [per_device(): pl.pallas_call(pack_kernel, out_shape=jax.ShapeDtypeStruct((PLANE, BLOCK,...]
where the time goes in v2:
time: 97.2 us; the launch traced here: 96.8 us
  starting transfers between devices  29.7 us (31%)
  waiting for transfers between devices  26.5 us (27%)
  blocking collectives  21.9 us (23%)
  Pallas kernels  17.1 us (18%)
    all_to_all x1, blocking collectives, per_device(): returned = lax.all_to_all(outgoing, AXES, 0, 0, tiled=True)  21.9 us
    ppermute x4, starting transfers between devices, moved(): return lax.ppermute(value, axes, pairs)  19.2 us
    all_to_all x1, waiting for transfers between devices, per_device(): received = lax.all_to_all(packed, AXES, 0, 0, tiled=True)  16.2 us
    pallas_call x1, Pallas kernels, per_device(): pl.pallas_call(attention_kernel, out_shape=[jax.ShapeDtypeStruct(half, jn...  11.3 us
    all_to_all x1, starting transfers between devices, per_device(): received = lax.all_to_all(packed, AXES, 0, 0, tiled=True)  10.5 us
    ppermute x4, waiting for transfers between devices, moved(): return lax.ppermute(value, axes, pairs)  10.2 us
    pallas_call x1, Pallas kernels, per_device(): pl.pallas_call(pack_kernel, out_shape=jax.ShapeDtypeStruct((PLANE, BLOCK,...  3.27 us
  transfers between devices with their start and end apart: 5, of which 3 were waited for; matrix products, arithmetic and copies ran while one was open for 0% of the time, Pallas kernels for 0%

profile of v2, /device:TPU:1, one launch (start us, length us, event | category | flops | bytes accessed | tf_op | source)
XLA Modules:
  0.0 96.8 jit_solution(3032075122843989373)
XLA Ops:
  0.6 0.0 copy-start
  0.7 0.6 pad_add_fusion.place
  1.2 3.3 %pack.1 = bf16[32,128,128]{2,1,0:T(8,128)(2,1)} custom-call(s32[2]{0:T(128)} %pad_add_fusion.place, bf16[128,1024]{1,0:T(8,128)(2,1)} %q_hbm.1, bf16[128,1024]{1,0:T(8,128)(2,1)} %k_hbm.1, bf16[128,1024]{1,0:T(8,128)(2,1)} %v_hbm.1, bf16[128,1024]{1,0:T(8,128)(2,1)} %g_hbm.1), custom_call_target="tpu_custom_call" | custom-call | tf_op jit(solution)/shard_map/pack/pallas_call | solution.py:205
  4.5 10.5 %all-to-all-start = ((bf16[32,128,128]{2,1,0:T(8,128)(2,1)}), bf16[32,128,128]{2,1,0:T(8,128)(2,1)S(1)}, u32[]{:S(2)}, u32[]{:S(2)}) async-start(bf16[32,128,128]{2,1,0:T(8,128)(2,1)} %pack.1), calls=%async_computation | async-start | bytes 2097152 | tf_op jit(solution)/shard_map/all_to_all | solution.py:215
  15.1 0.0 copy-done
  15.1 0.1 constant_dynamic-slice_fusion.2
  15.1 0.1 copy.10
  15.2 16.2 %all-to-all-done = bf16[32,128,128]{2,1,0:T(8,128)(2,1)S(1)} async-done(((bf16[32,128,128]{2,1,0:T(8,128)(2,1)}), bf16[32,128,128]{2,1,0:T(8,128)(2,1)S(1)}, u32[]{:S(2)}, u32[]{:S(2)}) %all-to-all-start) | async-done | bytes 1048608 | tf_op jit(solution)/shard_map/all_to_all | solution.py:215
  31.5 0.1 constant_dynamic-slice_fusion
  31.5 1.9 %collective-permute-start.1 = (bf16[16,128,128]{2,1,0:T(8,128)(2,1)S(1)}, bf16[16,128,128]{2,1,0:T(8,128)(2,1)S(1)}, u32[]{:S(2)}, u32[]{:S(2)}) collective-permute-start(bf16[16,128,128]{2,1,0:T(8,128)(2,1)S(1)} %get-tuple-element.12.own_ref), channel_id=1, source_target_pairs={{0,60},{1,5},{4,0},{5,9},{8,4},{9,13},{12,8},{13,17},{16,12},{17,2... | collective-permute-start | bytes 1572872 | tf_op jit(solution)/shard_map/ppermute | solution.py:194
  33.5 9.5 %collective-permute-start = (bf16[16,128,128]{2,1,0:T(8,128)(2,1)S(1)}, bf16[16,128,128]{2,1,0:T(8,128)(2,1)S(1)}, u32[]{:S(2)}, u32[]{:S(2)}) collective-permute-start(bf16[16,128,128]{2,1,0:T(8,128)(2,1)S(1)} %get-tuple-element.12.own_ref), channel_id=1, source_target_pairs={{0,1},{1,0},{2,3},{3,2},{4,5},{5,4},{6,7},{7,6},{8,9},{9,8},{10,11... | collective-permute-start | bytes 1572872 | tf_op jit(solution)/shard_map/ppermute | solution.py:194
  43.0 0.1 or_convert_fusion.alive
  43.1 0.0 copy-start.1
  43.1 4.1 %collective-permute-done.1.halo_ref = bf16[16,128,128]{2,1,0:T(8,128)(2,1)S(1)} collective-permute-done((bf16[16,128,128]{2,1,0:T(8,128)(2,1)S(1)}, bf16[16,128,128]{2,1,0:T(8,128)(2,1)S(1)}, u32[]{:S(2)}, u32[]{:S(2)}) %collective-permute-start.1) | collective-permute-done | bytes 524320 | tf_op jit(solution)/shard_map/ppermute | solution.py:194
  47.2 0.0 collective-permute-done.mate_ref
  47.2 0.0 copy-done.1
  47.2 11.3 %attention.1 = (bf16[16,128,128]{2,1,0:T(8,128)(2,1)S(1)}, f32[16,128,128]{2,1,0:T(8,128)S(1)}, bf16[16,128,128]{2,1,0:T(8,128)(2,1)S(1)}, bf16[16,128,128]{2,1,0:T(8,128)(2,1)S(1)}) custom-call(s32[2]{0:T(128)S(1)} %copy-done.1, s32[16,8]{1,0:T(8,128)S(1)} %broadcast_subtract_fusion.index, s32[16,8]{1,0:T(8,128)S(1)} %or_convert_fusion.alive, ...), custom_call_target="tpu_custom_call" | custom-call | tf_op jit(solution)/shard_map/attention/pallas_call | solution.py:229
  58.5 2.4 %collective-permute-start.2 = (bf16[16,128,128]{2,1,0:T(8,128)(2,1)S(1)}, bf16[16,128,128]{2,1,0:T(8,128)(2,1)S(1)}, u32[]{:S(2)}, u32[]{:S(2)}) collective-permute-start(bf16[16,128,128]{2,1,0:T(8,128)(2,1)S(1)} %get-tuple-element.10), channel_id=1, source_target_pairs={{0,1},{1,0},{2,3},{3,2},{4,5},{5,4},{6,7},{7,6},{8,9},{9,8},{10,11... | collective-permute-start | bytes 1572872 | tf_op jit(solution)/shard_map/ppermute | solution.py:194
  61.0 5.3 %collective-permute-start.3 = (bf16[16,128,128]{2,1,0:T(8,128)(2,1)S(1)}, bf16[16,128,128]{2,1,0:T(8,128)(2,1)S(1)}, u32[]{:S(2)}, u32[]{:S(2)}) collective-permute-start(bf16[16,128,128]{2,1,0:T(8,128)(2,1)S(1)} %get-tuple-element.11), channel_id=1, source_target_pairs={{0,4},{1,61},{4,8},{5,1},{8,12},{9,5},{12,16},{13,9},{16,20},{17,1... | collective-permute-start | bytes 1572872 | tf_op jit(solution)/shard_map/ppermute | solution.py:194
  66.3 0.0 collective-permute-done.2.mate_ref
  66.3 6.1 %collective-permute-done.3.halo_ref = bf16[16,128,128]{2,1,0:T(8,128)(2,1)S(1)} collective-permute-done((bf16[16,128,128]{2,1,0:T(8,128)(2,1)S(1)}, bf16[16,128,128]{2,1,0:T(8,128)(2,1)S(1)}, u32[]{:S(2)}, u32[]{:S(2)}) %collective-permute-start.3) | collective-permute-done | bytes 524320 | tf_op jit(solution)/shard_map/ppermute | solution.py:194
  72.4 0.7 total.1
  73.2 21.9 %all_to_all.10.in_ref = bf16[32,128,128]{2,1,0:T(8,128)(2,1)S(1)} all-to-all(bf16[32,128,128]{2,1,0:T(8,128)(2,1)S(1)} %total.1), channel_id=1, replica_groups=mesh['x_lo'=2,'y'=4,'z'=16,'x_hi'=2,'core'=2] {'x_hi','core','x_lo','y'}, dimensions={0} | all-to-all | bytes 2097152 | tf_op jit(solution)/shard_map/all_to_all | solution.py:263
  95.0 1.8 %unpack.1 = (bf16[128,1024]{1,0:T(8,128)(2,1)}, bf16[128,1024]{1,0:T(8,128)(2,1)}, bf16[128,1024]{1,0:T(8,128)(2,1)}, bf16[128,1024]{1,0:T(8,128)(2,1)}) custom-call(s32[2]{0:T(128)S(1)} %copy-done.1, bf16[32,128,128]{2,1,0:T(8,128)(2,1)S(1)} %all_to_all.10.in_ref), custom_call_target="tpu_custom_call" | custom-call | tf_op jit(solution)/shard_map/unpack/pallas_call | solution.py:265
  (3 shorter events, 0.0 us)
Async XLA Ops:
  0.6 14.4 %copy-start = (s32[512,8]{0,1:T(8,128)S(1)}, s32[512,8]{0,1:T(8,128)}, u32[]{:S(2)}) copy-start(s32[512,8]{0,1:T(8,128)} %param.9) | copy-start | bytes 49156
  4.5 26.9 %all-to-all-start = ((bf16[32,128,128]{2,1,0:T(8,128)(2,1)}), bf16[32,128,128]{2,1,0:T(8,128)(2,1)S(1)}, u32[]{:S(2)}, u32[]{:S(2)}) async-start(bf16[32,128,128]{2,1,0:T(8,128)(2,1)} %pack.1), calls=%async_computation | async-start | bytes 2097152 | tf_op jit(solution)/shard_map/all_to_all | solution.py:215
  31.5 15.7 %collective-permute-start.1 = (bf16[16,128,128]{2,1,0:T(8,128)(2,1)S(1)}, bf16[16,128,128]{2,1,0:T(8,128)(2,1)S(1)}, u32[]{:S(2)}, u32[]{:S(2)}) collective-permute-start(bf16[16,128,128]{2,1,0:T(8,128)(2,1)S(1)} %get-tuple-element.12.own_ref), channel_id=1, source_target_pairs={{0,60},{1,5},{4,0},{5,9},{8,4},{9,13},{12,8},{13,17},{16,12},{17,2... | collective-permute-start | bytes 1572872 | tf_op jit(solution)/shard_map/ppermute | solution.py:194
  33.5 13.8 %collective-permute-start = (bf16[16,128,128]{2,1,0:T(8,128)(2,1)S(1)}, bf16[16,128,128]{2,1,0:T(8,128)(2,1)S(1)}, u32[]{:S(2)}, u32[]{:S(2)}) collective-permute-start(bf16[16,128,128]{2,1,0:T(8,128)(2,1)S(1)} %get-tuple-element.12.own_ref), channel_id=1, source_target_pairs={{0,1},{1,0},{2,3},{3,2},{4,5},{5,4},{6,7},{7,6},{8,9},{9,8},{10,11... | collective-permute-start | bytes 1572872 | tf_op jit(solution)/shard_map/ppermute | solution.py:194
  43.1 4.1 %copy-start.1 = (s32[2]{0:T(128)S(1)}, s32[2]{0:T(128)}, u32[]{:S(2)}) copy-start(s32[2]{0:T(128)} %pad_add_fusion.place) | copy-start | bytes 28
  58.5 7.8 %collective-permute-start.2 = (bf16[16,128,128]{2,1,0:T(8,128)(2,1)S(1)}, bf16[16,128,128]{2,1,0:T(8,128)(2,1)S(1)}, u32[]{:S(2)}, u32[]{:S(2)}) collective-permute-start(bf16[16,128,128]{2,1,0:T(8,128)(2,1)S(1)} %get-tuple-element.10), channel_id=1, source_target_pairs={{0,1},{1,0},{2,3},{3,2},{4,5},{5,4},{6,7},{7,6},{8,9},{9,8},{10,11... | collective-permute-start | bytes 1572872 | tf_op jit(solution)/shard_map/ppermute | solution.py:194
  61.0 11.4 %collective-permute-start.3 = (bf16[16,128,128]{2,1,0:T(8,128)(2,1)S(1)}, bf16[16,128,128]{2,1,0:T(8,128)(2,1)S(1)}, u32[]{:S(2)}, u32[]{:S(2)}) collective-permute-start(bf16[16,128,128]{2,1,0:T(8,128)(2,1)S(1)} %get-tuple-element.11), channel_id=1, source_target_pairs={{0,4},{1,61},{4,8},{5,1},{8,12},{9,5},{12,16},{13,9},{16,20},{17,1... | collective-permute-start | bytes 1572872 | tf_op jit(solution)/shard_map/ppermute | solution.py:194

commit v3 on v2

--- a/solution.py
+++ b/solution.py
@@ -15,8 +15,11 @@
 HALF = PLANE // 2
 SLOTS = 8
 AXES = ("x_hi", "core", "x_lo", "y")
-VMEM_LIMIT = 40 * 1024 * 1024
-KEYS = SLOTS * BLOCK
+VMEM_LIMIT = 24 * 1024 * 1024
+PAIR = 2 * BLOCK
+SPARE = 6
+LISTED = HALF * SLOTS + 8
+LOWEST = -1e30
 CHUNK = 16
 PART = 256
 PARTS = HEADS * HEAD_SIZE // PART
@@ -87,93 +90,225 @@
         copy.wait()
 
 
-def attention_kernel(
-    place, index, alive, qg_ref, own_ref, mate_ref, halo_ref,
-    qo_ref, own_out, mate_out, halo_out,
-    window, accum, both_even, both_odd, pair_even, pair_odd, sems,
+def plan_kernel(index, alive, place, local_out, halo_out, count_out):
+    plane_at = place[0] * HALF
+    halo_at = (1 - place[0]) * PLANE
+
+    def padded(out, spot):
+        out[0, spot] = -1
+        return spot + spot % 2
+
+    def per_query(i, spots):
+        local, halo = spots
+        for s in range(SLOTS):
+            block, live = index[i, s], alive[i, s]
+            here = block - plane_at
+            inside = jnp.where((here >= 0) & (here < PLANE), live, 0)
+            local_out[0, local] = here
+            local_out[1, local] = i
+            halo_out[0, halo] = block - halo_at
+            halo_out[1, halo] = i
+            local = local + inside
+            halo = halo + live - inside
+        return padded(local_out, local), padded(halo_out, halo)
+
+    local, halo = lax.fori_loop(0, HALF, per_query, (jnp.int32(0), jnp.int32(0)))
+    for out, spot in ((local_out, local), (halo_out, halo)):
+        for extra in range(SPARE):
+            out[0, spot + extra] = -1
+            out[1, spot + extra] = HALF - 1
+    count_out[0] = local // 2
+    count_out[1] = halo // 2
+
+
+def left_lanes():
+    return lax.broadcasted_iota(jnp.int32, (BLOCK, WIDTH), 1) < HEAD_SIZE
+
+
+def query_rows(queries, tasks, t, left):
+    qg = queries[tasks[1, 2 * t]]
+    zero = jnp.zeros_like(qg)
+    return jnp.concatenate(
+        [jnp.where(left, qg * jnp.bfloat16(SCALING), zero), jnp.where(left, zero, qg)], axis=0
+    )
+
+
+def pair_of(tasks, t):
+    blocks = [tasks[0, 2 * t], tasks[0, 2 * t + 1]]
+    return [jnp.maximum(b, 0) for b in blocks], [b >= 0 for b in blocks]
+
+
+def listed_rows(window, tasks, t):
+    return jnp.concatenate([window[b] for b in pair_of(tasks, t)[0]], axis=0)
+
+
+def products(queries, window, tasks, t, left, both):
+    both[...] = lax.dot_general(
+        query_rows(queries, tasks, t, left), listed_rows(window, tasks, t),
+        (((1,), (1,)), ((), ())), preferred_element_type=jnp.float32,
+    )
+
+
+def pair_scores(both, live, r):
+    return [
+        jnp.where(live[s], both[r : r + CHUNK, s * BLOCK : (s + 1) * BLOCK], -jnp.inf)
+        for s in range(2)
+    ]
+
+
+def statistics(queries, window, tasks, count, stats, both_even, both_odd):
+    left = left_lanes()
+
+    def gather(t, both):
+        t_query = tasks[1, 2 * t]
+        live = pair_of(tasks, t)[1]
+        for r in range(0, BLOCK, CHUNK):
+            rows = slice(r, r + CHUNK)
+            first, second = pair_scores(both, live, r)
+            dprobs = both[BLOCK + r : BLOCK + r + CHUNK]
+            old = stats[0, t_query, rows]
+            top = jnp.maximum(old, jnp.maximum(first, second))
+            kept = jnp.exp(old - top)
+            w0, w1 = jnp.exp(first - top), jnp.exp(second - top)
+            stats[0, t_query, rows] = top
+            stats[1, t_query, rows] = stats[1, t_query, rows] * kept + w0 + w1
+            stats[2, t_query, rows] = (
+                stats[2, t_query, rows] * kept + w0 * dprobs[:, :BLOCK] + w1 * dprobs[:, BLOCK:]
+            )
+
+    products(queries, window, tasks, 0, left, both_even)
+
+    def step(j, carry):
+        even, odd = 2 * j, 2 * j + 1
+        products(queries, window, tasks, odd, left, both_odd)
+        gather(even, both_even)
+        products(queries, window, tasks, odd + 1, left, both_even)
+        gather(odd, both_odd)
+        return carry
+
+    lax.fori_loop(0, (count + 1) // 2, step, 0)
+
+
+def gradients(
+    queries, window, tasks, count, ends, mixed, accum, both_even, both_odd, pair_even, pair_odd
+):
+    left = left_lanes()
+    pair_odd[...] = jnp.zeros_like(pair_odd)
+
+    def weigh(t, both, pair):
+        t_query = tasks[1, 2 * t]
+        live = pair_of(tasks, t)[1]
+        for r in range(0, BLOCK, CHUNK):
+            rows = slice(r, r + CHUNK)
+            log_totals, delta = ends[0, t_query, rows], ends[1, t_query, rows]
+            for s, scores in enumerate(pair_scores(both, live, r)):
+                columns = slice(s * BLOCK, (s + 1) * BLOCK)
+                probs = jnp.exp(scores - log_totals)
+                dscore = probs * (both[BLOCK + r : BLOCK + r + CHUNK, columns] - delta)
+                pair[rows, columns] = dscore.astype(jnp.bfloat16)
+                pair[BLOCK + r : BLOCK + r + CHUNK, columns] = probs.astype(jnp.bfloat16)
+
+    def results(t, pair):
+        t_query = tasks[1, 2 * t]
+        stacked = pair[...]
+        both = jnp.dot(stacked, listed_rows(window, tasks, t), preferred_element_type=jnp.float32)
+        mixed[t_query] += jnp.where(left, both[:BLOCK] * SCALING, both[BLOCK:])
+        grads = lax.dot_general(
+            stacked, query_rows(queries, tasks, t, left), (((0,), (0,)), ((), ())),
+            preferred_element_type=jnp.float32,
+        )
+        for s, block in enumerate(pair_of(tasks, t)[0]):
+            accum[block] += grads[s * BLOCK : (s + 1) * BLOCK]
+
+    products(queries, window, tasks, 0, left, both_even)
+
+    def step(j, carry):
+        even, odd = 2 * j, 2 * j + 1
+        products(queries, window, tasks, odd, left, both_odd)
+        weigh(even, both_even, pair_even)
+        results(jnp.maximum(even - 1, 0), pair_odd)
+        products(queries, window, tasks, odd + 1, left, both_even)
+        weigh(odd, both_odd, pair_odd)
+        results(even, pair_even)
+        return carry
+
+    steps = (count + 1) // 2
+    lax.fori_loop(0, steps, step, 0)
+    results(jnp.maximum(2 * steps - 1, 0), pair_odd)
+
+
+def local_statistics_kernel(
+    place, tasks, counts, queries, own_ref, mate_ref, stats, plane, both_even, both_odd, sems
 ):
     core = place[0]
-    own_at = 2 * core
-    halo_at = 2 - own_at
     copies = [
-        pltpu.make_async_copy(own_ref, window.at[pl.ds(own_at * HALF, HALF)], sems.at[0]),
-        pltpu.make_async_copy(mate_ref, window.at[pl.ds(HALF, HALF)], sems.at[1]),
-        pltpu.make_async_copy(halo_ref, window.at[pl.ds(halo_at * HALF, HALF)], sems.at[2]),
+        pltpu.make_async_copy(own_ref, plane.at[pl.ds(core * HALF, HALF)], sems.at[0]),
+        pltpu.make_async_copy(mate_ref, plane.at[pl.ds((1 - core) * HALF, HALF)], sems.at[1]),
     ]
     for copy in copies:
         copy.start()
-    accum[...] = jnp.zeros_like(accum)
-    pair_odd[...] = jnp.zeros_like(pair_odd)
+    stats[0] = jnp.full(stats.shape[1:], LOWEST, jnp.float32)
+    stats[1] = jnp.zeros(stats.shape[1:], jnp.float32)
+    stats[2] = jnp.zeros(stats.shape[1:], jnp.float32)
     for copy in copies:
         copy.wait()
-    left = lax.broadcasted_iota(jnp.int32, (BLOCK, WIDTH), 1) < HEAD_SIZE
-
-    def listed_rows(i):
-        return jnp.concatenate([window[index[i, s]] for s in range(SLOTS)], axis=0)
-
-    def query_rows(i):
-        qg = qg_ref[i]
-        zero = jnp.zeros_like(qg)
-        return jnp.concatenate(
-            [jnp.where(left, qg * jnp.bfloat16(SCALING), zero), jnp.where(left, zero, qg)], axis=0
-        )
-
-    def products(i, both):
-        both[...] = lax.dot_general(
-            query_rows(i), listed_rows(i), (((1,), (1,)), ((), ())),
-            preferred_element_type=jnp.float32,
-        )
-
-    def weigh(i, both, pair):
-        live = [alive[i, s] > 0 for s in range(SLOTS)]
-        for r in range(0, BLOCK, CHUNK):
-            scores = jnp.concatenate(
-                [
-                    jnp.where(live[s], both[r : r + CHUNK, s * BLOCK : (s + 1) * BLOCK], -jnp.inf)
-                    for s in range(SLOTS)
-                ],
-                axis=1,
-            )
-            dprob = both[BLOCK + r : BLOCK + r + CHUNK]
-            weights = jnp.exp(scores - jnp.max(scores, axis=1, keepdims=True))
-            probs = weights * (1.0 / jnp.sum(weights, axis=1, keepdims=True))
-            terms = probs * dprob
-            dscore = terms - probs * jnp.sum(terms, axis=1, keepdims=True)
-            pair[r : r + CHUNK] = dscore.astype(jnp.bfloat16)
-            pair[BLOCK + r : BLOCK + r + CHUNK] = probs.astype(jnp.bfloat16)
-
-    def results(i, pair):
-        stacked = pair[...]
-        mixed = jnp.dot(stacked, listed_rows(i), preferred_element_type=jnp.float32)
-        qo_ref[i] = jnp.where(left, mixed[:BLOCK] * SCALING, mixed[BLOCK:]).astype(jnp.bfloat16)
-        grads = lax.dot_general(
-            stacked, query_rows(i), (((0,), (0,)), ((), ())), preferred_element_type=jnp.float32
-        )
-        for s in range(SLOTS):
-            accum[index[i, s]] += grads[s * BLOCK : (s + 1) * BLOCK]
-
-    products(0, both_even)
-
-    def step(j, carry):
-        even, odd = 2 * j, 2 * j + 1
-        products(odd, both_odd)
-        weigh(even, both_even, pair_even)
-        results(jnp.maximum(even - 1, 0), pair_odd)
-        products(jnp.minimum(even + 2, HALF - 1), both_even)
-        weigh(odd, both_odd, pair_odd)
-        results(even, pair_even)
+    statistics(queries, plane, tasks, counts[0], stats, both_even, both_odd)
+
+
+def halo_kernel(
+    tasks, counts, queries, halo_ref, stats_in, ends, mixed, halo_out,
+    stats, accum, both_even, both_odd, pair_even, pair_odd, sem,
+):
+    copy = pltpu.make_async_copy(stats_in, stats, sem)
+    copy.start()
+    accum[...] = jnp.zeros_like(accum)
+    mixed[...] = jnp.zeros_like(mixed)
+    copy.wait()
+    statistics(queries, halo_ref, tasks, counts[1], stats, both_even, both_odd)
+
+    def finish(i, carry):
+        lane_max = stats[0, i]
+        row_max = jnp.max(lane_max, axis=1, keepdims=True)
+        kept = jnp.exp(lane_max - row_max)
+        totals = jnp.sum(stats[1, i] * kept, axis=1, keepdims=True)
+        delta = jnp.sum(stats[2, i] * kept, axis=1, keepdims=True) / totals
+        ends[0, i] = jnp.broadcast_to(row_max + jnp.log(totals), (BLOCK, WIDTH))
+        ends[1, i] = jnp.broadcast_to(delta, (BLOCK, WIDTH))
         return carry
 
-    lax.fori_loop(0, HALF // 2, step, 0)
-    results(HALF - 1, pair_odd)
-    halo_out[...] = accum[pl.ds(halo_at * HALF, HALF)].astype(jnp.bfloat16)
-    mate_out[...] = accum[HALF : 2 * HALF].astype(jnp.bfloat16)
-    own_out[...] = accum[pl.ds(own_at * HALF, HALF)]
-
-
-def sum_kernel(place, qo_ref, own_ref, mate_ref, halo_ref, out_ref):
+    lax.fori_loop(0, HALF, finish, 0)
+    gradients(
+        queries, halo_ref, tasks, counts[1], ends, mixed, accum,
+        both_even, both_odd, pair_even, pair_odd,
+    )
+    halo_out[...] = accum[...].astype(jnp.bfloat16)
+
+
+def local_gradients_kernel(
+    place, tasks, counts, queries, plane, ends, mixed_in, qo_ref, own_out, mate_out,
+    mixed, accum, both_even, both_odd, pair_even, pair_odd, sem,
+):
     core = place[0]
-    total = own_ref[...] + mate_ref[...].astype(jnp.float32) + halo_ref[...].astype(jnp.float32)
+    copy = pltpu.make_async_copy(mixed_in, mixed, sem)
+    copy.start()
+    accum[...] = jnp.zeros_like(accum)
+    copy.wait()
+    gradients(
+        queries, plane, tasks, counts[0], ends, mixed, accum,
+        both_even, both_odd, pair_even, pair_odd,
+    )
+    qo_ref[...] = mixed[...].astype(jnp.bfloat16)
+    mate_out[...] = accum[pl.ds((1 - core) * HALF, HALF)].astype(jnp.bfloat16)
+    own_out[...] = accum[pl.ds(core * HALF, HALF)]
+
+
+def halo_sum_kernel(own_ref, halo_ref, out_ref):
+    out_ref[...] = own_ref[...] + halo_ref[...].astype(jnp.float32)
+
+
+def sum_kernel(place, qo_ref, own_ref, mate_ref, out_ref):
+    core = place[0]
+    total = own_ref[...] + mate_ref[...].astype(jnp.float32)
     out_ref[pl.ds(core * HALF, HALF)] = total.astype(jnp.bfloat16)
     out_ref[pl.ds((1 - core) * HALF, HALF)] = qo_ref[...]
 
@@ -196,6 +331,80 @@
 
 def to_mate(value):
     return moved(value, ("core",), lambda c: (1 - c,))
+
+
+def cost(pairs):
+    flops = pairs * 2 * PAIR * PAIR * WIDTH
+    return pl.CostEstimate(flops=flops, bytes_accessed=1 << 20, transcendentals=pairs * BLOCK * PAIR)
+
+
+HALF_BF16 = jax.ShapeDtypeStruct((HALF, BLOCK, WIDTH), jnp.bfloat16)
+HALF_F32 = jax.ShapeDtypeStruct((HALF, BLOCK, WIDTH), jnp.float32)
+TASKS = jax.ShapeDtypeStruct((2, LISTED), jnp.int32)
+BOTHS = [pltpu.VMEM((PAIR, PAIR), jnp.float32)] * 2
+PAIRS = [pltpu.VMEM((PAIR, PAIR), jnp.bfloat16)] * 2
+
+
+def attention_in(place, index, alive, queries, own, mate):
+    local_tasks, halo_tasks, counts = pl.pallas_call(
+        plan_kernel,
+        out_shape=[TASKS, TASKS, jax.ShapeDtypeStruct((2,), jnp.int32)],
+        in_specs=[SMEM] * 3,
+        out_specs=[SMEM] * 3,
+        name="plan",
+    )(index, alive, place)
+    stats, plane = pl.pallas_call(
+        local_statistics_kernel,
+        out_shape=[
+            jax.ShapeDtypeStruct((3, HALF, BLOCK, WIDTH), jnp.float32),
+            jax.ShapeDtypeStruct((PLANE, BLOCK, WIDTH), jnp.bfloat16),
+        ],
+        in_specs=[SMEM] * 3 + [VMEM] + [ANY] * 2,
+        out_specs=[VMEM] * 2,
+        scratch_shapes=BOTHS + [pltpu.SemaphoreType.DMA((2,))],
+        compiler_params=PARAMS,
+        cost_estimate=cost(64),
+        name="local_statistics",
+    )(place, local_tasks, counts, queries, own, mate)
+    return local_tasks, halo_tasks, counts, stats, plane
+
+
+def attention_halo(tasks, counts, queries, halo, stats):
+    return pl.pallas_call(
+        halo_kernel,
+        out_shape=[jax.ShapeDtypeStruct((2, HALF, BLOCK, WIDTH), jnp.float32), HALF_F32, HALF_BF16],
+        in_specs=[SMEM] * 2 + [VMEM] * 2 + [ANY],
+        out_specs=[VMEM] * 3,
+        scratch_shapes=[
+            pltpu.VMEM((3, HALF, BLOCK, WIDTH), jnp.float32),
+            pltpu.VMEM((HALF, BLOCK, WIDTH), jnp.float32),
+        ]
+        + BOTHS
+        + PAIRS
+        + [pltpu.SemaphoreType.DMA],
+        compiler_params=PARAMS,
+        cost_estimate=cost(64),
+        name="halo",
+    )(tasks, counts, queries, halo, stats)
+
+
+def attention_out(place, tasks, counts, queries, plane, ends, mixed):
+    return pl.pallas_call(
+        local_gradients_kernel,
+        out_shape=[HALF_BF16, HALF_F32, HALF_BF16],
+        in_specs=[SMEM] * 3 + [VMEM] * 3 + [ANY],
+        out_specs=[VMEM] * 3,
+        scratch_shapes=[
+            pltpu.VMEM((HALF, BLOCK, WIDTH), jnp.float32),
+            pltpu.VMEM((PLANE, BLOCK, WIDTH), jnp.float32),
+        ]
+        + BOTHS
+        + PAIRS
+        + [pltpu.SemaphoreType.DMA],
+        compiler_params=PARAMS,
+        cost_estimate=cost(128),
+        name="local_gradients",
+    )(place, tasks, counts, queries, plane, ends, mixed)
 
 
 def per_device(queries, key_rows, value_rows, cotangent, block_list):
@@ -225,41 +434,33 @@
     own_blocks = first_query + jnp.arange(HALF, dtype=jnp.int32)
     alive = (jnp.arange(SLOTS)[None, :] == 0) | (listed != own_blocks[:, None])
     index = listed - first_key
-    half = (HALF, BLOCK, WIDTH)
-    query_out, own_part, mate_part, halo_part = pl.pallas_call(
-        attention_kernel,
-        out_shape=[
-            jax.ShapeDtypeStruct(half, jnp.bfloat16),
-            jax.ShapeDtypeStruct(half, jnp.float32),
-            jax.ShapeDtypeStruct(half, jnp.bfloat16),
-            jax.ShapeDtypeStruct(half, jnp.bfloat16),
-        ],
-        in_specs=[SMEM] * 3 + [VMEM] + [ANY] * 3,
-        out_specs=[VMEM] * 4,
-        scratch_shapes=[
-            pltpu.VMEM((3 * HALF, BLOCK, WIDTH), jnp.bfloat16),
-            pltpu.VMEM((3 * HALF, BLOCK, WIDTH), jnp.float32),
-            pltpu.VMEM((2 * BLOCK, KEYS), jnp.float32),
-            pltpu.VMEM((2 * BLOCK, KEYS), jnp.float32),
-            pltpu.VMEM((2 * BLOCK, KEYS), jnp.bfloat16),
-            pltpu.VMEM((2 * BLOCK, KEYS), jnp.bfloat16),
-            pltpu.SemaphoreType.DMA((3,)),
-        ],
-        compiler_params=PARAMS,
-        name="attention",
-    )(place, index, alive.astype(jnp.int32), query_grad_rows, key_value, mate, halo)
-    mate_sum = to_mate(mate_part)
+    local_tasks, halo_tasks, counts, stats, plane = attention_in(
+        place, index, alive.astype(jnp.int32), query_grad_rows, key_value, mate
+    )
+    ends, mixed, halo_part = attention_halo(halo_tasks, counts, query_grad_rows, halo, stats)
     halo_sum = moved(
         halo_part, ("z", "core"), lambda z, c: ((z + (depth - 1 if c else 1)) % depth, c)
     )
+    query_out, own_part, mate_part = attention_out(
+        place, local_tasks, counts, query_grad_rows, plane, ends, mixed
+    )
+    mate_sum = to_mate(mate_part)
+    own_sum = pl.pallas_call(
+        halo_sum_kernel,
+        out_shape=HALF_F32,
+        in_specs=[VMEM] * 2,
+        out_specs=VMEM,
+        compiler_params=PARAMS,
+        name="halo_total",
+    )(own_part, halo_sum)
     outgoing = pl.pallas_call(
         sum_kernel,
         out_shape=jax.ShapeDtypeStruct((PLANE, BLOCK, WIDTH), jnp.bfloat16),
-        in_specs=[SMEM] + [VMEM] * 4,
+        in_specs=[SMEM] + [VMEM] * 3,
         out_specs=VMEM,
         compiler_params=PARAMS,
         name="total",
-    )(place, query_out, own_part, mate_sum, halo_sum)
+    )(place, query_out, own_sum, mate_sum)
     returned = lax.all_to_all(outgoing, AXES, 0, 0, tiled=True)
     rows = jax.ShapeDtypeStruct(queries.shape, jnp.bfloat16)
     return pl.pallas_call(

time: 97.2 us -> 99.8 us (1.027)
  Pallas kernels: 17.1 us -> 31.1 us
  waiting for transfers between devices: 26.5 us -> 19.4 us
  starting transfers between devices: 29.7 us -> 23.8 us
  local copies, waits for them, and re-layouts: 0.24 us -> 1.61 us
  other arithmetic: 0.67 us -> 1.9 us
  blocking collectives: 21.9 us -> 20.7 us
    pallas_call x1 -> x5, Pallas kernels: 11.3 us -> 25.2 us  [the longest x1 10.8 us: attention_out(): pl.pallas_call(local_gradients_kernel, out_shape=[HALF_BF16, HALF_F32, HA...]
    ppermute x4, waiting for transfers between devices: 10.2 us -> 3.21 us  [moved(): return lax.ppermute(value, axes, pairs)]
    ppermute x4, starting transfers between devices: 19.2 us -> 13.2 us  [moved(): return lax.ppermute(value, axes, pairs)]
    unnamed x5 -> x11, local copies, waits for them, and re-layouts: 0.09 us -> 1.43 us
    all_to_all x1, blocking collectives: 21.9 us -> 20.7 us  [per_device(): returned = lax.all_to_all(outgoing, AXES, 0, 0, tiled=True)]
  transfers between devices with their start and end apart: 5 -> 5, of which waited for: 3 -> 3; matrix products, arithmetic and copies ran while one was open for 0% -> 1% of each run, Pallas kernels for 0% -> 21%
where the time goes in v3:
time: 99.8 us; the launch traced here: 99.3 us
  Pallas kernels  31.1 us (31%)
  starting transfers between devices  23.8 us (24%)
  blocking collectives  20.7 us (21%)
  waiting for transfers between devices  19.4 us (19%)
  other arithmetic  1.9 us (2%)
  local copies, waits for them, and re-layouts  1.61 us (2%)
    all_to_all x1, blocking collectives, per_device(): returned = lax.all_to_all(outgoing, AXES, 0, 0, tiled=True)  20.7 us
    all_to_all x1, waiting for transfers between devices, per_device(): received = lax.all_to_all(packed, AXES, 0, 0, tiled=True)  16.2 us
    ppermute x4, starting transfers between devices, moved(): return lax.ppermute(value, axes, pairs)  13.2 us
    pallas_call x1, Pallas kernels, attention_out(): pl.pallas_call(local_gradients_kernel, out_shape=[HALF_BF16, HALF_F32, HA...  10.8 us
    all_to_all x1, starting transfers between devices, per_device(): received = lax.all_to_all(packed, AXES, 0, 0, tiled=True)  10.5 us
    pallas_call x1, Pallas kernels, attention_in(): pl.pallas_call(local_statistics_kernel, out_shape=[jax.ShapeDtypeStruct((...  6.9 us
    pallas_call x1, Pallas kernels, attention_halo(): pl.pallas_call(halo_kernel, out_shape=[jax.ShapeDtypeStruct((2, HALF, BLO...  4.72 us
    pallas_call x1, Pallas kernels, per_device(): pl.pallas_call(pack_kernel, out_shape=jax.ShapeDtypeStruct((PLANE, BLOCK,...  3.42 us
  transfers between devices with their start and end apart: 5, of which 3 were waited for; matrix products, arithmetic and copies ran while one was open for 1% of the time, Pallas kernels for 21%

profile of v3, /device:TPU:1, one launch (start us, length us, event | category | flops | bytes accessed | tf_op | source)
XLA Modules:
  0.0 99.3 jit_solution(4928538071989495632)
XLA Ops:
  0.7 0.6 pad_add_fusion.place
  1.3 3.4 %pack.1 = bf16[32,128,128]{2,1,0:T(8,128)(2,1)} custom-call(s32[2]{0:T(128)} %pad_add_fusion.place, bf16[128,1024]{1,0:T(8,128)(2,1)} %q_hbm.1, bf16[128,1024]{1,0:T(8,128)(2,1)} %k_hbm.1, bf16[128,1024]{1,0:T(8,128)(2,1)} %v_hbm.1, bf16[128,1024]{1,0:T(8,128)(2,1)} %g_hbm.1), custom_call_target="tpu_custom_call" | custom-call | tf_op jit(solution)/shard_map/pack/pallas_call | solution.py:414
  4.7 10.5 %all-to-all-start = ((bf16[32,128,128]{2,1,0:T(8,128)(2,1)}), bf16[32,128,128]{2,1,0:T(8,128)(2,1)S(1)}, u32[]{:S(2)}, u32[]{:S(2)}) async-start(bf16[32,128,128]{2,1,0:T(8,128)(2,1)} %pack.1), calls=%async_computation | async-start | bytes 2097152 | tf_op jit(solution)/shard_map/all_to_all | solution.py:424
  15.2 0.1 constant_dynamic-slice_fusion.2
  15.4 16.2 %all-to-all-done = bf16[32,128,128]{2,1,0:T(8,128)(2,1)S(1)} async-done(((bf16[32,128,128]{2,1,0:T(8,128)(2,1)}), bf16[32,128,128]{2,1,0:T(8,128)(2,1)S(1)}, u32[]{:S(2)}, u32[]{:S(2)}) %all-to-all-start) | async-done | bytes 1048608 | tf_op jit(solution)/shard_map/all_to_all | solution.py:424
  31.6 0.1 constant_dynamic-slice_fusion
  31.8 2.1 %collective-permute-start = (bf16[16,128,128]{2,1,0:T(8,128)(2,1)S(1)}, bf16[16,128,128]{2,1,0:T(8,128)(2,1)S(1)}, u32[]{:S(2)}, u32[]{:S(2)}) collective-permute-start(bf16[16,128,128]{2,1,0:T(8,128)(2,1)S(1)} %get-tuple-element.26.own_ref), channel_id=1, source_target_pairs={{0,1},{1,0},{2,3},{3,2},{4,5},{5,4},{6,7},{7,6},{8,9},{9,8},{10,11... | collective-permute-start | bytes 1572872 | tf_op jit(solution)/shard_map/ppermute | solution.py:329
  33.8 1.9 %collective-permute-start.1 = (bf16[16,128,128]{2,1,0:T(8,128)(2,1)S(1)}, bf16[16,128,128]{2,1,0:T(8,128)(2,1)S(1)}, u32[]{:S(2)}, u32[]{:S(2)}) collective-permute-start(bf16[16,128,128]{2,1,0:T(8,128)(2,1)S(1)} %get-tuple-element.26.own_ref), channel_id=1, source_target_pairs={{0,60},{1,5},{4,0},{5,9},{8,4},{9,13},{12,8},{13,17},{16,12},{17,2... | collective-permute-start | bytes 1572872 | tf_op jit(solution)/shard_map/ppermute | solution.py:329
  35.8 0.6 broadcast_subtract_fusion.index
  36.4 0.7 or_convert_fusion.alive
  37.0 2.7 %plan.1 = (s32[2,136]{1,0:T(2,128)}, s32[2,136]{1,0:T(2,128)}, s32[2]{0:T(128)}) custom-call(s32[16,8]{1,0:T(8,128)} %broadcast_subtract_fusion.index, s32[16,8]{1,0:T(8,128)} %or_convert_fusion.alive, s32[2]{0:T(128)} %pad_add_fusion.place), custom_call_target="tpu_custom_call" | custom-call | tf_op jit(solution)/shard_map/plan/pallas_call | solution.py:349
  39.8 0.7 copy-done.3
  40.5 0.7 copy-done.4
  41.2 6.9 %local_statistics.1 = (f32[3,16,128,128]{3,2,1,0:T(8,128)S(1)}, bf16[32,128,128]{2,1,0:T(8,128)(2,1)S(1)}) custom-call(s32[2]{0:T(128)S(1)} %copy-done.1, s32[2,136]{1,0:T(2,128)S(1)} %copy-done.4, s32[2]{0:T(128)S(1)} %copy-done.3, bf16[16,128,128]{2,1,0:T(8,128)(2,1)S(1)} %get-tuple-element.27.queries, ...), custom_call_target="tpu_custom_call" | custom-call | flops 1073741824 | bytes 1048576 | tf_op jit(solution)/shard_map/local_statistics/pallas_call | solution.py:356
  48.1 1.4 %collective-permute-done.1.halo_ref = bf16[16,128,128]{2,1,0:T(8,128)(2,1)S(1)} collective-permute-done((bf16[16,128,128]{2,1,0:T(8,128)(2,1)S(1)}, bf16[16,128,128]{2,1,0:T(8,128)(2,1)S(1)}, u32[]{:S(2)}, u32[]{:S(2)}) %collective-permute-start.1) | collective-permute-done | bytes 524320 | tf_op jit(solution)/shard_map/ppermute | solution.py:329
  49.5 4.7 %halo.1 = (f32[2,16,128,128]{3,2,1,0:T(8,128)S(1)}, f32[16,128,128]{2,1,0:T(8,128)S(1)}, bf16[16,128,128]{2,1,0:T(8,128)(2,1)S(1)}) custom-call(s32[2,136]{1,0:T(2,128)S(1)} %copy-done.2, s32[2]{0:T(128)S(1)} %copy-done.3, bf16[16,128,128]{2,1,0:T(8,128)(2,1)S(1)} %get-tuple-element.27.queries, bf16[16,128,128]{2,1,0:T(8,128)(2,1)S(1)} %collective-permute-done.1.halo_ref, ...), custom_call_target="tpu_custom_call" | custom-call | flops 1073741824 | bytes 1048576 | tf_op jit(solution)/shard_map/halo/pallas_call | solution.py:373
  54.2 7.3 %collective-permute-start.2 = (bf16[16,128,128]{2,1,0:T(8,128)(2,1)S(1)}, bf16[16,128,128]{2,1,0:T(8,128)(2,1)S(1)}, u32[]{:S(2)}, u32[]{:S(2)}) collective-permute-start(bf16[16,128,128]{2,1,0:T(8,128)(2,1)S(1)} %get-tuple-element.24), channel_id=1, source_target_pairs={{0,4},{1,61},{4,8},{5,1},{8,12},{9,5},{12,16},{13,9},{16,20},{17,1... | collective-permute-start | bytes 1572872 | tf_op jit(solution)/shard_map/ppermute | solution.py:329
  61.6 10.8 %local_gradients.1 = (bf16[16,128,128]{2,1,0:T(8,128)(2,1)S(1)}, f32[16,128,128]{2,1,0:T(8,128)S(1)}, bf16[16,128,128]{2,1,0:T(8,128)(2,1)S(1)}) custom-call(s32[2]{0:T(128)S(1)} %copy-done.1, s32[2,136]{1,0:T(2,128)S(1)} %copy-done.4, s32[2]{0:T(128)S(1)} %copy-done.3, bf16[16,128,128]{2,1,0:T(8,128)(2,1)S(1)} %get-tuple-element.27.queries, ...), custom_call_target="tpu_custom_call" | custom-call | flops 2147483648 | bytes 1048576 | tf_op jit(solution)/shard_map/local_gradients/pallas_call | solution.py:392
  72.3 1.9 %collective-permute-start.3 = (bf16[16,128,128]{2,1,0:T(8,128)(2,1)S(1)}, bf16[16,128,128]{2,1,0:T(8,128)(2,1)S(1)}, u32[]{:S(2)}, u32[]{:S(2)}) collective-permute-start(bf16[16,128,128]{2,1,0:T(8,128)(2,1)S(1)} %get-tuple-element.25), channel_id=1, source_target_pairs={{0,1},{1,0},{2,3},{3,2},{4,5},{5,4},{6,7},{7,6},{8,9},{9,8},{10,11... | collective-permute-start | bytes 1572872 | tf_op jit(solution)/shard_map/ppermute | solution.py:329
  74.3 0.1 halo_total.1.own_ref
  74.4 1.8 %collective-permute-done.3.mate_ref = bf16[16,128,128]{2,1,0:T(8,128)(2,1)S(1)} collective-permute-done((bf16[16,128,128]{2,1,0:T(8,128)(2,1)S(1)}, bf16[16,128,128]{2,1,0:T(8,128)(2,1)S(1)}, u32[]{:S(2)}, u32[]{:S(2)}) %collective-permute-start.3) | collective-permute-done | bytes 524320 | tf_op jit(solution)/shard_map/ppermute | solution.py:329
  76.1 0.7 total.1
  76.9 20.7 %all_to_all.10.in_ref = bf16[32,128,128]{2,1,0:T(8,128)(2,1)S(1)} all-to-all(bf16[32,128,128]{2,1,0:T(8,128)(2,1)S(1)} %total.1), channel_id=1, replica_groups=mesh['x_lo'=2,'y'=4,'z'=16,'x_hi'=2,'core'=2] {'x_hi','core','x_lo','y'}, dimensions={0} | all-to-all | bytes 2097152 | tf_op jit(solution)/shard_map/all_to_all | solution.py:464
  97.5 1.8 %unpack.1 = (bf16[128,1024]{1,0:T(8,128)(2,1)}, bf16[128,1024]{1,0:T(8,128)(2,1)}, bf16[128,1024]{1,0:T(8,128)(2,1)}, bf16[128,1024]{1,0:T(8,128)(2,1)}) custom-call(s32[2]{0:T(128)S(1)} %copy-done.1, bf16[32,128,128]{2,1,0:T(8,128)(2,1)S(1)} %all_to_all.10.in_ref), custom_call_target="tpu_custom_call" | custom-call | tf_op jit(solution)/shard_map/unpack/pallas_call | solution.py:466
  (13 shorter events, 0.1 us)
Async XLA Ops:
  0.6 14.6 %copy-start = (s32[512,8]{0,1:T(8,128)S(1)}, s32[512,8]{0,1:T(8,128)}, u32[]{:S(2)}) copy-start(s32[512,8]{0,1:T(8,128)} %param.9) | copy-start | bytes 49156
  1.3 38.5 %copy-start.1 = (s32[2]{0:T(128)S(1)}, s32[2]{0:T(128)}, u32[]{:S(2)}) copy-start(s32[2]{0:T(128)} %pad_add_fusion.place) | copy-start | bytes 28
  4.7 26.9 %all-to-all-start = ((bf16[32,128,128]{2,1,0:T(8,128)(2,1)}), bf16[32,128,128]{2,1,0:T(8,128)(2,1)S(1)}, u32[]{:S(2)}, u32[]{:S(2)}) async-start(bf16[32,128,128]{2,1,0:T(8,128)(2,1)} %pack.1), calls=%async_computation | async-start | bytes 2097152 | tf_op jit(solution)/shard_map/all_to_all | solution.py:424
  31.8 8.1 %collective-permute-start = (bf16[16,128,128]{2,1,0:T(8,128)(2,1)S(1)}, bf16[16,128,128]{2,1,0:T(8,128)(2,1)S(1)}, u32[]{:S(2)}, u32[]{:S(2)}) collective-permute-start(bf16[16,128,128]{2,1,0:T(8,128)(2,1)S(1)} %get-tuple-element.26.own_ref), channel_id=1, source_target_pairs={{0,1},{1,0},{2,3},{3,2},{4,5},{5,4},{6,7},{7,6},{8,9},{9,8},{10,11... | collective-permute-start | bytes 1572872 | tf_op jit(solution)/shard_map/ppermute | solution.py:329
  33.8 15.7 %collective-permute-start.1 = (bf16[16,128,128]{2,1,0:T(8,128)(2,1)S(1)}, bf16[16,128,128]{2,1,0:T(8,128)(2,1)S(1)}, u32[]{:S(2)}, u32[]{:S(2)}) collective-permute-start(bf16[16,128,128]{2,1,0:T(8,128)(2,1)S(1)} %get-tuple-element.26.own_ref), channel_id=1, source_target_pairs={{0,60},{1,5},{4,0},{5,9},{8,4},{9,13},{12,8},{13,17},{16,12},{17,2... | collective-permute-start | bytes 1572872 | tf_op jit(solution)/shard_map/ppermute | solution.py:329
  39.8 9.7 %copy-start.2 = (s32[2,136]{1,0:T(2,128)S(1)}, s32[2,136]{1,0:T(2,128)}, u32[]{:S(2)}) copy-start(s32[2,136]{1,0:T(2,128)} %get-tuple-element.18.tasks) | copy-start | bytes 3268
  39.8 0.7 copy-start.3
  40.5 0.7 copy-start.4
  54.2 20.0 %collective-permute-start.2 = (bf16[16,128,128]{2,1,0:T(8,128)(2,1)S(1)}, bf16[16,128,128]{2,1,0:T(8,128)(2,1)S(1)}, u32[]{:S(2)}, u32[]{:S(2)}) collective-permute-start(bf16[16,128,128]{2,1,0:T(8,128)(2,1)S(1)} %get-tuple-element.24), channel_id=1, source_target_pairs={{0,4},{1,61},{4,8},{5,1},{8,12},{9,5},{12,16},{13,9},{16,20},{17,1... | collective-permute-start | bytes 1572872 | tf_op jit(solution)/shard_map/ppermute | solution.py:329
  72.3 3.8 %collective-permute-start.3 = (bf16[16,128,128]{2,1,0:T(8,128)(2,1)S(1)}, bf16[16,128,128]{2,1,0:T(8,128)(2,1)S(1)}, u32[]{:S(2)}, u32[]{:S(2)}) collective-permute-start(bf16[16,128,128]{2,1,0:T(8,128)(2,1)S(1)} %get-tuple-element.25), channel_id=1, source_target_pairs={{0,1},{1,0},{2,3},{3,2},{4,5},{5,4},{6,7},{7,6},{8,9},{9,8},{10,11... | collective-permute-start | bytes 1572872 | tf_op jit(solution)/shard_map/ppermute | solution.py:329

commit v4 on v2

--- a/solution.py
+++ b/solution.py
@@ -18,6 +18,7 @@
 VMEM_LIMIT = 40 * 1024 * 1024
 KEYS = SLOTS * BLOCK
 CHUNK = 16
+LANES = 128
 PART = 256
 PARTS = HEADS * HEAD_SIZE // PART
 
@@ -33,37 +34,49 @@
     return (head // 8) * 16 + core * 8 + head % 8
 
 
-def pack_kernel(place, q_hbm, k_hbm, v_hbm, g_hbm, out_ref, q_ref, k_ref, v_ref, g_ref, sems):
-    x_hi = place[1]
+def pack_kernel(
+    q_hbm, k_hbm, v_hbm, g_hbm, out_hbm, q_ref, k_ref, v_ref, g_ref, out_ref, in_sems, out_sems
+):
+    x_hi = lax.axis_index("x_hi")
     parts = [slice(p * PART, (p + 1) * PART) for p in range(PARTS)]
-    copies = [
+    arrivals = [
         [
-            pltpu.make_async_copy(source.at[:, part], target.at[:, part], sems.at[p, n])
+            pltpu.make_async_copy(source.at[:, part], target.at[:, part], in_sems.at[p, n])
             for n, (source, target) in enumerate(
                 ((k_hbm, k_ref), (v_hbm, v_ref), (q_hbm, q_ref), (g_hbm, g_ref))
             )
         ]
         for p, part in enumerate(parts)
     ]
-    for group in copies:
+    for group in arrivals:
         for copy in group:
             copy.start()
-    for pair in range(HEADS // 2):
-        if pair * WIDTH % PART == 0:
-            for copy in copies[pair * WIDTH // PART]:
-                copy.wait()
-        columns = slice(pair * WIDTH, (pair + 1) * WIDTH)
-        q, k, v, g = q_ref[:, columns], k_ref[:, columns], v_ref[:, columns], g_ref[:, columns]
-        for odd in range(2):
-            head = 2 * pair + odd
-            out_ref[slot_of(head, x_hi)] = lane_pair(k, v, odd)
-            out_ref[slot_of(head, 1 - x_hi)] = lane_pair(q, g, odd)
+    departures = []
+    for p in range(PARTS):
+        for copy in arrivals[p]:
+            copy.wait()
+        heads = PART // HEAD_SIZE
+        for head in range(p * heads, (p + 1) * heads):
+            columns = slice(head // 2 * WIDTH, (head // 2 + 1) * WIDTH)
+            out_ref[slot_of(head, x_hi)] = lane_pair(
+                k_ref[:, columns], v_ref[:, columns], head % 2
+            )
+            out_ref[slot_of(head, 1 - x_hi)] = lane_pair(
+                q_ref[:, columns], g_ref[:, columns], head % 2
+            )
+        for n in range(2):
+            slots = pl.ds(slot_of(p * heads, n), heads)
+            copy = pltpu.make_async_copy(out_ref.at[slots], out_hbm.at[slots], out_sems.at[p, n])
+            copy.start()
+            departures.append(copy)
+    for copy in departures:
+        copy.wait()
 
 
 def unpack_kernel(
-    place, in_ref, o_hbm, dq_hbm, dk_hbm, dv_hbm, o_ref, dq_ref, dk_ref, dv_ref, sems
+    in_ref, o_hbm, dq_hbm, dk_hbm, dv_hbm, o_ref, dq_ref, dk_ref, dv_ref, sems
 ):
-    x_hi = place[1]
+    x_hi = lax.axis_index("x_hi")
     copies = []
     for pair in range(HEADS // 2):
         columns = slice(pair * WIDTH, (pair + 1) * WIDTH)
@@ -87,29 +100,54 @@
         copy.wait()
 
 
+def split_kernel(in_ref, kv_ref, qg_ref):
+    core = lax.axis_index("core")
+    kv_ref[...] = in_ref[pl.ds(core * HALF, HALF)]
+    qg_ref[...] = in_ref[pl.ds((1 - core) * HALF, HALF)]
+
+
 def attention_kernel(
-    place, index, alive, qg_ref, own_ref, mate_ref, halo_ref,
+    list_hbm, qg_ref, own_ref, mate_ref, halo_ref,
     qo_ref, own_out, mate_out, halo_out,
-    window, accum, both_even, both_odd, pair_even, pair_odd, sems,
+    window, accum, both_even, both_odd, pair_even, pair_odd, listed, table, sem,
 ):
-    core = place[0]
-    own_at = 2 * core
-    halo_at = 2 - own_at
-    copies = [
-        pltpu.make_async_copy(own_ref, window.at[pl.ds(own_at * HALF, HALF)], sems.at[0]),
-        pltpu.make_async_copy(mate_ref, window.at[pl.ds(HALF, HALF)], sems.at[1]),
-        pltpu.make_async_copy(halo_ref, window.at[pl.ds(halo_at * HALF, HALF)], sems.at[2]),
-    ]
-    for copy in copies:
-        copy.start()
+    core, z = lax.axis_index("core"), lax.axis_index("z")
+    own_at = 2 * core * HALF
+    halo_at = 2 * HALF - own_at
+    first_query = z * PLANE + (1 - core) * HALF
+    first_key = z * PLANE - core * HALF
+    lanes = listed.shape[1]
+    at = lax.div(first_query, lanes) * lanes
+    copy = pltpu.make_async_copy(
+        list_hbm.at[:, pl.ds(pl.multiple_of(at, lanes), lanes)], listed, sem
+    )
+    copy.start()
+    window[pl.ds(own_at, HALF)] = own_ref[...]
+    window[HALF : 2 * HALF] = mate_ref[...]
+    window[pl.ds(halo_at, HALF)] = halo_ref[...]
     accum[...] = jnp.zeros_like(accum)
     pair_odd[...] = jnp.zeros_like(pair_odd)
-    for copy in copies:
-        copy.wait()
+    copy.wait()
+
+    def note(i, carry):
+        for s in range(SLOTS):
+            block = listed[s, first_query - at + i]
+            dead = (block == first_query + i) if s else False
+            table[i, s] = jnp.where(dead, -1, block - first_key)
+        return carry
+
+    lax.fori_loop(0, HALF, note, 0)
+
+    def blocks_of(i):
+        return [
+            jnp.where(table[i, s] < 0, table[i, 0], table[i, s]) if s else table[i, 0]
+            for s in range(SLOTS)
+        ]
+
     left = lax.broadcasted_iota(jnp.int32, (BLOCK, WIDTH), 1) < HEAD_SIZE
 
     def listed_rows(i):
-        return jnp.concatenate([window[index[i, s]] for s in range(SLOTS)], axis=0)
+        return jnp.concatenate([window[b] for b in blocks_of(i)], axis=0)
 
     def query_rows(i):
         qg = qg_ref[i]
@@ -125,7 +163,7 @@
         )
 
     def weigh(i, both, pair):
-        live = [alive[i, s] > 0 for s in range(SLOTS)]
+        live = [table[i, s] >= 0 for s in range(SLOTS)]
         for r in range(0, BLOCK, CHUNK):
             scores = jnp.concatenate(
                 [
@@ -149,8 +187,8 @@
         grads = lax.dot_general(
             stacked, query_rows(i), (((0,), (0,)), ((), ())), preferred_element_type=jnp.float32
         )
-        for s in range(SLOTS):
-            accum[index[i, s]] += grads[s * BLOCK : (s + 1) * BLOCK]
+        for s, block in enumerate(blocks_of(i)):
+            accum[block] += grads[s * BLOCK : (s + 1) * BLOCK]
 
     products(0, both_even)
 
@@ -166,19 +204,22 @@
 
     lax.fori_loop(0, HALF // 2, step, 0)
     results(HALF - 1, pair_odd)
-    halo_out[...] = accum[pl.ds(halo_at * HALF, HALF)].astype(jnp.bfloat16)
+    halo_out[...] = accum[pl.ds(halo_at, HALF)].astype(jnp.bfloat16)
     mate_out[...] = accum[HALF : 2 * HALF].astype(jnp.bfloat16)
-    own_out[...] = accum[pl.ds(own_at * HALF, HALF)]
-
-
-def sum_kernel(place, qo_ref, own_ref, mate_ref, halo_ref, out_ref):
-    core = place[0]
-    total = own_ref[...] + mate_ref[...].astype(jnp.float32) + halo_ref[...].astype(jnp.float32)
+    own_out[...] = accum[pl.ds(own_at, HALF)]
+
+
+def halo_sum_kernel(own_ref, halo_ref, out_ref):
+    out_ref[...] = own_ref[...] + halo_ref[...].astype(jnp.float32)
+
+
+def sum_kernel(qo_ref, own_ref, mate_ref, out_ref):
+    core = lax.axis_index("core")
+    total = own_ref[...] + mate_ref[...].astype(jnp.float32)
     out_ref[pl.ds(core * HALF, HALF)] = total.astype(jnp.bfloat16)
     out_ref[pl.ds((1 - core) * HALF, HALF)] = qo_ref[...]
 
 
-SMEM = pl.BlockSpec(memory_space=pltpu.SMEM)
 VMEM = pl.BlockSpec(memory_space=pltpu.VMEM)
 ANY = pl.BlockSpec(memory_space=pl.ANY)
 PARAMS = pltpu.CompilerParams(vmem_limit_bytes=VMEM_LIMIT)
@@ -200,32 +241,35 @@
 
 def per_device(queries, key_rows, value_rows, cotangent, block_list):
     depth = lax.axis_size("z")
-    core, x_hi, z = lax.axis_index("core"), lax.axis_index("x_hi"), lax.axis_index("z")
-    place = jnp.stack([core, x_hi]).astype(jnp.int32)
+    plane = jax.ShapeDtypeStruct((PLANE, BLOCK, WIDTH), jnp.bfloat16)
     packed = pl.pallas_call(
         pack_kernel,
-        out_shape=jax.ShapeDtypeStruct((PLANE, BLOCK, WIDTH), jnp.bfloat16),
-        in_specs=[SMEM] + [ANY] * 4,
-        out_specs=VMEM,
+        out_shape=plane,
+        in_specs=[ANY] * 4,
+        out_specs=ANY,
         scratch_shapes=[pltpu.VMEM(queries.shape, jnp.bfloat16)] * 4
-        + [pltpu.SemaphoreType.DMA((PARTS, 4))],
+        + [
+            pltpu.VMEM(plane.shape, jnp.bfloat16),
+            pltpu.SemaphoreType.DMA((PARTS, 4)),
+            pltpu.SemaphoreType.DMA((PARTS, 2)),
+        ],
         compiler_params=EDGE_PARAMS,
         name="pack",
-    )(place, queries, key_rows, value_rows, cotangent)
+    )(queries, key_rows, value_rows, cotangent)
     received = lax.all_to_all(packed, AXES, 0, 0, tiled=True)
-    key_value = lax.dynamic_slice_in_dim(received, core * HALF, HALF, 0)
-    query_grad_rows = lax.dynamic_slice_in_dim(received, (1 - core) * HALF, HALF, 0)
+    half = (HALF, BLOCK, WIDTH)
+    key_value, query_grad_rows = pl.pallas_call(
+        split_kernel,
+        out_shape=[jax.ShapeDtypeStruct(half, jnp.bfloat16)] * 2,
+        in_specs=[VMEM],
+        out_specs=[VMEM] * 2,
+        compiler_params=PARAMS,
+        name="split",
+    )(received)
     mate = to_mate(key_value)
     halo = moved(
         key_value, ("z", "core"), lambda z, c: ((z + (1 if c else depth - 1)) % depth, c)
     )
-    first_query = z * PLANE + (1 - core) * HALF
-    first_key = z * PLANE - core * HALF
-    listed = lax.dynamic_slice_in_dim(block_list, first_query, HALF, 0)
-    own_blocks = first_query + jnp.arange(HALF, dtype=jnp.int32)
-    alive = (jnp.arange(SLOTS)[None, :] == 0) | (listed != own_blocks[:, None])
-    index = listed - first_key
-    half = (HALF, BLOCK, WIDTH)
     query_out, own_part, mate_part, halo_part = pl.pallas_call(
         attention_kernel,
         out_shape=[
@@ -234,7 +278,7 @@
             jax.ShapeDtypeStruct(half, jnp.bfloat16),
             jax.ShapeDtypeStruct(half, jnp.bfloat16),
         ],
-        in_specs=[SMEM] * 3 + [VMEM] + [ANY] * 3,
+        in_specs=[ANY] + [VMEM] * 4,
         out_specs=[VMEM] * 4,
         scratch_shapes=[
             pltpu.VMEM((3 * HALF, BLOCK, WIDTH), jnp.bfloat16),
@@ -243,35 +287,45 @@
             pltpu.VMEM((2 * BLOCK, KEYS), jnp.float32),
             pltpu.VMEM((2 * BLOCK, KEYS), jnp.bfloat16),
             pltpu.VMEM((2 * BLOCK, KEYS), jnp.bfloat16),
-            pltpu.SemaphoreType.DMA((3,)),
+            pltpu.SMEM((SLOTS, LANES), jnp.int32),
+            pltpu.SMEM((HALF, SLOTS), jnp.int32),
+            pltpu.SemaphoreType.DMA,
         ],
         compiler_params=PARAMS,
         name="attention",
-    )(place, index, alive.astype(jnp.int32), query_grad_rows, key_value, mate, halo)
+    )(block_list.T, query_grad_rows, key_value, mate, halo)
     mate_sum = to_mate(mate_part)
     halo_sum = moved(
         halo_part, ("z", "core"), lambda z, c: ((z + (depth - 1 if c else 1)) % depth, c)
     )
+    own_sum = pl.pallas_call(
+        halo_sum_kernel,
+        out_shape=jax.ShapeDtypeStruct(half, jnp.float32),
+        in_specs=[VMEM] * 2,
+        out_specs=VMEM,
+        compiler_params=PARAMS,
+        name="halo_total",
+    )(own_part, halo_sum)
     outgoing = pl.pallas_call(
         sum_kernel,
-        out_shape=jax.ShapeDtypeStruct((PLANE, BLOCK, WIDTH), jnp.bfloat16),
-        in_specs=[SMEM] + [VMEM] * 4,
+        out_shape=plane,
+        in_specs=[VMEM] * 3,
         out_specs=VMEM,
         compiler_params=PARAMS,
         name="total",
-    )(place, query_out, own_part, mate_sum, halo_sum)
+    )(query_out, own_sum, mate_sum)
     returned = lax.all_to_all(outgoing, AXES, 0, 0, tiled=True)
     rows = jax.ShapeDtypeStruct(queries.shape, jnp.bfloat16)
     return pl.pallas_call(
         unpack_kernel,
         out_shape=[rows] * 4,
-        in_specs=[SMEM, VMEM],
+        in_specs=[VMEM],
         out_specs=[ANY] * 4,
         scratch_shapes=[pltpu.VMEM(queries.shape, jnp.bfloat16)] * 4
         + [pltpu.SemaphoreType.DMA((PARTS, 4))],
         compiler_params=PARAMS,
         name="unpack",
-    )(place, returned)
+    )(returned)
 
 
 def solution(mesh):

time: 97.2 us -> 92.4 us (0.951)
  blocking collectives: 21.9 us -> 50.5 us
  waiting for transfers between devices: 26.5 us -> 8.85 us
  starting transfers between devices: 29.7 us -> 17.1 us
  Pallas kernels: 17.1 us -> 14.8 us
    all_to_all x0 -> x1, blocking collectives: none -> 26.9 us  [per_device(): received = lax.all_to_all(packed, AXES, 0, 0, tiled=True)]
    all_to_all x1 -> x0, waiting for transfers between devices: 16.2 us -> none  [per_device(): received = lax.all_to_all(packed, AXES, 0, 0, tiled=True)]
    all_to_all x1 -> x0, starting transfers between devices: 10.5 us -> none  [per_device(): received = lax.all_to_all(packed, AXES, 0, 0, tiled=True)]
    ppermute x4, starting transfers between devices: 19.2 us -> 17.1 us  [moved(): return lax.ppermute(value, axes, pairs)]
    pallas_call x3 -> x5, Pallas kernels: 5.8 us -> 3.95 us  [the longest x1 2.44 us: per_device(): pl.pallas_call(pack_kernel, out_shape=plane, in_specs=[ANY] * 4, out_spec...]
    all_to_all x1, blocking collectives: 21.9 us -> 23.6 us  [per_device(): returned = lax.all_to_all(outgoing, AXES, 0, 0, tiled=True)]
    ppermute x4, waiting for transfers between devices: 10.2 us -> 8.85 us  [moved(): return lax.ppermute(value, axes, pairs)]
  transfers between devices with their start and end apart: 5 -> 4, of which waited for: 3 -> 2; matrix products, arithmetic and copies ran while one was open for 0% -> 0% of each run, Pallas kernels for 0% -> 0%
where the time goes in v4:
time: 92.4 us; the launch traced here: 91.9 us
  blocking collectives  50.5 us (55%)
  starting transfers between devices  17.1 us (19%)
  Pallas kernels  14.8 us (16%)
  waiting for transfers between devices  8.85 us (10%)
    all_to_all x1, blocking collectives, per_device(): received = lax.all_to_all(packed, AXES, 0, 0, tiled=True)  26.9 us
    all_to_all x1, blocking collectives, per_device(): returned = lax.all_to_all(outgoing, AXES, 0, 0, tiled=True)  23.6 us
    ppermute x4, starting transfers between devices, moved(): return lax.ppermute(value, axes, pairs)  17.1 us
    pallas_call x1, Pallas kernels, per_device(): pl.pallas_call(attention_kernel, out_shape=[jax.ShapeDtypeStruct(half, jn...  10.8 us
    ppermute x4, waiting for transfers between devices, moved(): return lax.ppermute(value, axes, pairs)  8.85 us
    pallas_call x1, Pallas kernels, per_device(): pl.pallas_call(pack_kernel, out_shape=plane, in_specs=[ANY] * 4, out_spec...  2.44 us
  transfers between devices with their start and end apart: 4, of which 2 were waited for; matrix products, arithmetic and copies ran while one was open for 0% of the time, Pallas kernels for 0%

profile of v4, /device:TPU:1, one launch (start us, length us, event | category | flops | bytes accessed | tf_op | source)
XLA Modules:
  0.0 91.9 jit_solution(11047144025361589315)
XLA Ops:
  0.6 2.4 %pack.1 = bf16[32,128,128]{2,1,0:T(8,128)(2,1)} custom-call(bf16[128,1024]{1,0:T(8,128)(2,1)} %q_hbm.1, bf16[128,1024]{1,0:T(8,128)(2,1)} %k_hbm.1, bf16[128,1024]{1,0:T(8,128)(2,1)} %v_hbm.1, bf16[128,1024]{1,0:T(8,128)(2,1)} %g_hbm.1), custom_call_target="tpu_custom_call" | custom-call | tf_op jit(solution)/shard_map/pack/pallas_call | solution.py:245
  3.1 26.9 %all_to_all.10.in_ref = bf16[32,128,128]{2,1,0:T(8,128)(2,1)S(1)} all-to-all(bf16[32,128,128]{2,1,0:T(8,128)(2,1)} %pack.1), channel_id=1, replica_groups=mesh['x_lo'=2,'y'=4,'z'=16,'x_hi'=2,'core'=2] {'x_hi','core','x_lo','y'}, dimensions={0} | all-to-all | bytes 2097152 | tf_op jit(solution)/shard_map/all_to_all | solution.py:259
  30.0 0.0 copy-start
  30.0 0.1 split.1
  30.1 1.9 %collective-permute-start.1 = (bf16[16,128,128]{2,1,0:T(8,128)(2,1)S(1)}, bf16[16,128,128]{2,1,0:T(8,128)(2,1)S(1)}, u32[]{:S(2)}, u32[]{:S(2)}) collective-permute-start(bf16[16,128,128]{2,1,0:T(8,128)(2,1)S(1)} %get-tuple-element.11.own_ref), channel_id=1, source_target_pairs={{0,60},{1,5},{4,0},{5,9},{8,4},{9,13},{12,8},{13,17},{16,12},{17,2... | collective-permute-start | bytes 1572872 | tf_op jit(solution)/shard_map/ppermute | solution.py:235
  32.0 9.5 %collective-permute-start = (bf16[16,128,128]{2,1,0:T(8,128)(2,1)S(1)}, bf16[16,128,128]{2,1,0:T(8,128)(2,1)S(1)}, u32[]{:S(2)}, u32[]{:S(2)}) collective-permute-start(bf16[16,128,128]{2,1,0:T(8,128)(2,1)S(1)} %get-tuple-element.11.own_ref), channel_id=1, source_target_pairs={{0,1},{1,0},{2,3},{3,2},{4,5},{5,4},{6,7},{7,6},{8,9},{9,8},{10,11... | collective-permute-start | bytes 1572872 | tf_op jit(solution)/shard_map/ppermute | solution.py:235
  41.6 4.2 %collective-permute-done.1.halo_ref = bf16[16,128,128]{2,1,0:T(8,128)(2,1)S(1)} collective-permute-done((bf16[16,128,128]{2,1,0:T(8,128)(2,1)S(1)}, bf16[16,128,128]{2,1,0:T(8,128)(2,1)S(1)}, u32[]{:S(2)}, u32[]{:S(2)}) %collective-permute-start.1) | collective-permute-done | bytes 524320 | tf_op jit(solution)/shard_map/ppermute | solution.py:235
  45.8 0.0 collective-permute-done.mate_ref
  45.8 0.0 copy-done
  45.8 10.8 %attention.1 = (bf16[16,128,128]{2,1,0:T(8,128)(2,1)S(1)}, f32[16,128,128]{2,1,0:T(8,128)S(1)}, bf16[16,128,128]{2,1,0:T(8,128)(2,1)S(1)}, bf16[16,128,128]{2,1,0:T(8,128)(2,1)S(1)}) custom-call(s32[8,512]{1,0:T(8,128)S(1)} %bitcast.1, bf16[16,128,128]{2,1,0:T(8,128)(2,1)S(1)} %get-tuple-element.10.qg_ref, ...), custom_call_target="tpu_custom_call" | custom-call | tf_op jit(solution)/shard_map/attention/pallas_call | solution.py:273
  56.6 3.7 %collective-permute-start.2 = (bf16[16,128,128]{2,1,0:T(8,128)(2,1)S(1)}, bf16[16,128,128]{2,1,0:T(8,128)(2,1)S(1)}, u32[]{:S(2)}, u32[]{:S(2)}) collective-permute-start(bf16[16,128,128]{2,1,0:T(8,128)(2,1)S(1)} %get-tuple-element.14), channel_id=1, source_target_pairs={{0,4},{1,61},{4,8},{5,1},{8,12},{9,5},{12,16},{13,9},{16,20},{17,1... | collective-permute-start | bytes 1572872 | tf_op jit(solution)/shard_map/ppermute | solution.py:235
  60.3 1.9 %collective-permute-start.3 = (bf16[16,128,128]{2,1,0:T(8,128)(2,1)S(1)}, bf16[16,128,128]{2,1,0:T(8,128)(2,1)S(1)}, u32[]{:S(2)}, u32[]{:S(2)}) collective-permute-start(bf16[16,128,128]{2,1,0:T(8,128)(2,1)S(1)} %get-tuple-element.15), channel_id=1, source_target_pairs={{0,1},{1,0},{2,3},{3,2},{4,5},{5,4},{6,7},{7,6},{8,9},{9,8},{10,11... | collective-permute-start | bytes 1572872 | tf_op jit(solution)/shard_map/ppermute | solution.py:235
  62.3 4.6 %collective-permute-done.2.halo_ref = bf16[16,128,128]{2,1,0:T(8,128)(2,1)S(1)} collective-permute-done((bf16[16,128,128]{2,1,0:T(8,128)(2,1)S(1)}, bf16[16,128,128]{2,1,0:T(8,128)(2,1)S(1)}, u32[]{:S(2)}, u32[]{:S(2)}) %collective-permute-start.2) | collective-permute-done | bytes 524320 | tf_op jit(solution)/shard_map/ppermute | solution.py:235
  66.9 0.1 halo_total.1.own_ref
  67.0 0.0 collective-permute-done.3.mate_ref
  67.0 0.1 total.1
  67.1 23.6 %all_to_all.11.in_ref = bf16[32,128,128]{2,1,0:T(8,128)(2,1)S(1)} all-to-all(bf16[32,128,128]{2,1,0:T(8,128)(2,1)S(1)} %total.1), channel_id=1, replica_groups=mesh['x_lo'=2,'y'=4,'z'=16,'x_hi'=2,'core'=2] {'x_hi','core','x_lo','y'}, dimensions={0} | all-to-all | bytes 2097152 | tf_op jit(solution)/shard_map/all_to_all | solution.py:317
  90.7 1.2 %unpack.1 = (bf16[128,1024]{1,0:T(8,128)(2,1)}, bf16[128,1024]{1,0:T(8,128)(2,1)}, bf16[128,1024]{1,0:T(8,128)(2,1)}, bf16[128,1024]{1,0:T(8,128)(2,1)}) custom-call(bf16[32,128,128]{2,1,0:T(8,128)(2,1)S(1)} %all_to_all.11.in_ref), custom_call_target="tpu_custom_call" | custom-call | tf_op jit(solution)/shard_map/unpack/pallas_call | solution.py:319
Async XLA Ops:
  30.0 15.8 %copy-start = (s32[512,8]{0,1:T(8,128)S(1)}, s32[512,8]{0,1:T(8,128)}, u32[]{:S(2)}) copy-start(s32[512,8]{0,1:T(8,128)} %param.9) | copy-start | bytes 49156
  30.1 15.7 %collective-permute-start.1 = (bf16[16,128,128]{2,1,0:T(8,128)(2,1)S(1)}, bf16[16,128,128]{2,1,0:T(8,128)(2,1)S(1)}, u32[]{:S(2)}, u32[]{:S(2)}) collective-permute-start(bf16[16,128,128]{2,1,0:T(8,128)(2,1)S(1)} %get-tuple-element.11.own_ref), channel_id=1, source_target_pairs={{0,60},{1,5},{4,0},{5,9},{8,4},{9,13},{12,8},{13,17},{16,12},{17,2... | collective-permute-start | bytes 1572872 | tf_op jit(solution)/shard_map/ppermute | solution.py:235
  32.0 13.8 %collective-permute-start = (bf16[16,128,128]{2,1,0:T(8,128)(2,1)S(1)}, bf16[16,128,128]{2,1,0:T(8,128)(2,1)S(1)}, u32[]{:S(2)}, u32[]{:S(2)}) collective-permute-start(bf16[16,128,128]{2,1,0:T(8,128)(2,1)S(1)} %get-tuple-element.11.own_ref), channel_id=1, source_target_pairs={{0,1},{1,0},{2,3},{3,2},{4,5},{5,4},{6,7},{7,6},{8,9},{9,8},{10,11... | collective-permute-start | bytes 1572872 | tf_op jit(solution)/shard_map/ppermute | solution.py:235
  56.6 10.2 %collective-permute-start.2 = (bf16[16,128,128]{2,1,0:T(8,128)(2,1)S(1)}, bf16[16,128,128]{2,1,0:T(8,128)(2,1)S(1)}, u32[]{:S(2)}, u32[]{:S(2)}) collective-permute-start(bf16[16,128,128]{2,1,0:T(8,128)(2,1)S(1)} %get-tuple-element.14), channel_id=1, source_target_pairs={{0,4},{1,61},{4,8},{5,1},{8,12},{9,5},{12,16},{13,9},{16,20},{17,1... | collective-permute-start | bytes 1572872 | tf_op jit(solution)/shard_map/ppermute | solution.py:235
  60.3 6.6 %collective-permute-start.3 = (bf16[16,128,128]{2,1,0:T(8,128)(2,1)S(1)}, bf16[16,128,128]{2,1,0:T(8,128)(2,1)S(1)}, u32[]{:S(2)}, u32[]{:S(2)}) collective-permute-start(bf16[16,128,128]{2,1,0:T(8,128)(2,1)S(1)} %get-tuple-element.15), channel_id=1, source_target_pairs={{0,1},{1,0},{2,3},{3,2},{4,5},{5,4},{6,7},{7,6},{8,9},{9,8},{10,11... | collective-permute-start | bytes 1572872 | tf_op jit(solution)/shard_map/ppermute | solution.py:235

commit v5 on v4

--- a/solution.py
+++ b/solution.py
@@ -13,6 +13,7 @@
 SCALING = HEAD_SIZE ** (-0.5)
 PLANE = 32
 HALF = PLANE // 2
+QUARTER = HALF // 2
 SLOTS = 8
 AXES = ("x_hi", "core", "x_lo", "y")
 VMEM_LIMIT = 40 * 1024 * 1024
@@ -100,21 +101,45 @@
         copy.wait()
 
 
-def split_kernel(in_ref, kv_ref, qg_ref):
+def split_kernel(in_ref, kv_ref, qg_ref, near_ref, far_ref):
     core = lax.axis_index("core")
-    kv_ref[...] = in_ref[pl.ds(core * HALF, HALF)]
+    kv_at = core * HALF
+    kv_ref[...] = in_ref[pl.ds(kv_at, HALF)]
     qg_ref[...] = in_ref[pl.ds((1 - core) * HALF, HALF)]
-
-
-def attention_kernel(
-    list_hbm, qg_ref, own_ref, mate_ref, halo_ref,
-    qo_ref, own_out, mate_out, halo_out,
-    window, accum, both_even, both_odd, pair_even, pair_odd, listed, table, sem,
+    near_ref[...] = in_ref[pl.ds(kv_at + core * QUARTER, QUARTER)]
+    far_ref[...] = in_ref[pl.ds(kv_at + (1 - core) * QUARTER, QUARTER)]
+
+
+def near_kernel(list_hbm, qg_ref, own_ref, mate_ref, near_ref, qo_ref, sums, *scratch):
+    sums[...] = jnp.zeros_like(sums)
+    core = lax.axis_index("core")
+    attend(core, list_hbm, qg_ref, own_ref, mate_ref, (near_ref,), qo_ref, sums, *scratch)
+
+
+def far_kernel(
+    list_hbm, qg_ref, own_ref, mate_ref, near_ref, far_ref, sums_ref,
+    qo_ref, own_out, mate_out, halo_out, sums, *scratch,
+):
+    sums[...] = sums_ref[...]
+    core = lax.axis_index("core")
+    attend(
+        1 - core, list_hbm, qg_ref, own_ref, mate_ref, (near_ref, far_ref), qo_ref, sums, *scratch
+    )
+    own_at = 2 * core * HALF
+    halo_out[...] = sums[pl.ds(2 * HALF - own_at, HALF)].astype(jnp.bfloat16)
+    mate_out[...] = sums[HALF : 2 * HALF].astype(jnp.bfloat16)
+    own_out[...] = sums[pl.ds(own_at, HALF)]
+
+
+def attend(
+    group, list_hbm, qg_ref, own_ref, mate_ref, halo_refs, qo_ref, accum,
+    window, both_even, both_odd, pair_even, pair_odd, listed, table, sem,
 ):
     core, z = lax.axis_index("core"), lax.axis_index("z")
     own_at = 2 * core * HALF
     halo_at = 2 * HALF - own_at
-    first_query = z * PLANE + (1 - core) * HALF
+    first = group * QUARTER
+    first_query = z * PLANE + (1 - core) * HALF + first
     first_key = z * PLANE - core * HALF
     lanes = listed.shape[1]
     at = lax.div(first_query, lanes) * lanes
@@ -124,8 +149,8 @@
     copy.start()
     window[pl.ds(own_at, HALF)] = own_ref[...]
     window[HALF : 2 * HALF] = mate_ref[...]
-    window[pl.ds(halo_at, HALF)] = halo_ref[...]
-    accum[...] = jnp.zeros_like(accum)
+    for side, halo_ref in zip((core, 1 - core), halo_refs):
+        window[pl.ds(halo_at + side * QUARTER, QUARTER)] = halo_ref[...]
     pair_odd[...] = jnp.zeros_like(pair_odd)
     copy.wait()
 
@@ -136,7 +161,7 @@
             table[i, s] = jnp.where(dead, -1, block - first_key)
         return carry
 
-    lax.fori_loop(0, HALF, note, 0)
+    lax.fori_loop(0, QUARTER, note, 0)
 
     def blocks_of(i):
         return [
@@ -150,7 +175,7 @@
         return jnp.concatenate([window[b] for b in blocks_of(i)], axis=0)
 
     def query_rows(i):
-        qg = qg_ref[i]
+        qg = qg_ref[first + i]
         zero = jnp.zeros_like(qg)
         return jnp.concatenate(
             [jnp.where(left, qg * jnp.bfloat16(SCALING), zero), jnp.where(left, zero, qg)], axis=0
@@ -197,27 +222,26 @@
         products(odd, both_odd)
         weigh(even, both_even, pair_even)
         results(jnp.maximum(even - 1, 0), pair_odd)
-        products(jnp.minimum(even + 2, HALF - 1), both_even)
+        products(jnp.minimum(even + 2, QUARTER - 1), both_even)
         weigh(odd, both_odd, pair_odd)
         results(even, pair_even)
         return carry
 
-    lax.fori_loop(0, HALF // 2, step, 0)
-    results(HALF - 1, pair_odd)
-    halo_out[...] = accum[pl.ds(halo_at, HALF)].astype(jnp.bfloat16)
-    mate_out[...] = accum[HALF : 2 * HALF].astype(jnp.bfloat16)
-    own_out[...] = accum[pl.ds(own_at, HALF)]
+    lax.fori_loop(0, QUARTER // 2, step, 0)
+    results(QUARTER - 1, pair_odd)
 
 
 def halo_sum_kernel(own_ref, halo_ref, out_ref):
     out_ref[...] = own_ref[...] + halo_ref[...].astype(jnp.float32)
 
 
-def sum_kernel(qo_ref, own_ref, mate_ref, out_ref):
+def sum_kernel(near_ref, far_ref, own_ref, mate_ref, out_ref):
     core = lax.axis_index("core")
     total = own_ref[...] + mate_ref[...].astype(jnp.float32)
     out_ref[pl.ds(core * HALF, HALF)] = total.astype(jnp.bfloat16)
-    out_ref[pl.ds((1 - core) * HALF, HALF)] = qo_ref[...]
+    query_at = (1 - core) * HALF
+    out_ref[pl.ds(query_at + core * QUARTER, QUARTER)] = near_ref[...]
+    out_ref[pl.ds(query_at + (1 - core) * QUARTER, QUARTER)] = far_ref[...]
 
 
 VMEM = pl.BlockSpec(memory_space=pltpu.VMEM)
@@ -258,42 +282,67 @@
     )(queries, key_rows, value_rows, cotangent)
     received = lax.all_to_all(packed, AXES, 0, 0, tiled=True)
     half = (HALF, BLOCK, WIDTH)
-    key_value, query_grad_rows = pl.pallas_call(
+    quarter = (QUARTER, BLOCK, WIDTH)
+    sums = (3 * HALF, BLOCK, WIDTH)
+    key_value, query_grad_rows, near_part, far_part = pl.pallas_call(
         split_kernel,
-        out_shape=[jax.ShapeDtypeStruct(half, jnp.bfloat16)] * 2,
+        out_shape=[jax.ShapeDtypeStruct(half, jnp.bfloat16)] * 2
+        + [jax.ShapeDtypeStruct(quarter, jnp.bfloat16)] * 2,
         in_specs=[VMEM],
-        out_specs=[VMEM] * 2,
+        out_specs=[VMEM] * 4,
         compiler_params=PARAMS,
         name="split",
     )(received)
+
+    def inward(value):
+        return moved(value, ("z", "core"), lambda z, c: ((z + (1 if c else depth - 1)) % depth, c))
+
+    near = inward(near_part)
     mate = to_mate(key_value)
-    halo = moved(
-        key_value, ("z", "core"), lambda z, c: ((z + (1 if c else depth - 1)) % depth, c)
-    )
-    query_out, own_part, mate_part, halo_part = pl.pallas_call(
-        attention_kernel,
+    far = inward(far_part)
+    scratch = [
+        pltpu.VMEM(sums, jnp.bfloat16),
+        pltpu.VMEM((2 * BLOCK, KEYS), jnp.float32),
+        pltpu.VMEM((2 * BLOCK, KEYS), jnp.float32),
+        pltpu.VMEM((2 * BLOCK, KEYS), jnp.bfloat16),
+        pltpu.VMEM((2 * BLOCK, KEYS), jnp.bfloat16),
+        pltpu.SMEM((SLOTS, LANES), jnp.int32),
+        pltpu.SMEM((QUARTER, SLOTS), jnp.int32),
+        pltpu.SemaphoreType.DMA,
+    ]
+    work = pl.CostEstimate(
+        flops=QUARTER * 6 * 2 * BLOCK * KEYS * WIDTH,
+        bytes_accessed=1 << 20,
+        transcendentals=QUARTER * BLOCK * KEYS,
+    )
+    query_near, near_sums = pl.pallas_call(
+        near_kernel,
         out_shape=[
-            jax.ShapeDtypeStruct(half, jnp.bfloat16),
+            jax.ShapeDtypeStruct(quarter, jnp.bfloat16),
+            jax.ShapeDtypeStruct(sums, jnp.float32),
+        ],
+        in_specs=[ANY] + [VMEM] * 4,
+        out_specs=[VMEM] * 2,
+        scratch_shapes=scratch,
+        compiler_params=PARAMS,
+        cost_estimate=work,
+        name="near",
+    )(block_list.T, query_grad_rows, key_value, mate, near)
+    query_far, own_part, mate_part, halo_part = pl.pallas_call(
+        far_kernel,
+        out_shape=[
+            jax.ShapeDtypeStruct(quarter, jnp.bfloat16),
             jax.ShapeDtypeStruct(half, jnp.float32),
             jax.ShapeDtypeStruct(half, jnp.bfloat16),
             jax.ShapeDtypeStruct(half, jnp.bfloat16),
         ],
-        in_specs=[ANY] + [VMEM] * 4,
+        in_specs=[ANY] + [VMEM] * 6,
         out_specs=[VMEM] * 4,
-        scratch_shapes=[
-            pltpu.VMEM((3 * HALF, BLOCK, WIDTH), jnp.bfloat16),
-            pltpu.VMEM((3 * HALF, BLOCK, WIDTH), jnp.float32),
-            pltpu.VMEM((2 * BLOCK, KEYS), jnp.float32),
-            pltpu.VMEM((2 * BLOCK, KEYS), jnp.float32),
-            pltpu.VMEM((2 * BLOCK, KEYS), jnp.bfloat16),
-            pltpu.VMEM((2 * BLOCK, KEYS), jnp.bfloat16),
-            pltpu.SMEM((SLOTS, LANES), jnp.int32),
-            pltpu.SMEM((HALF, SLOTS), jnp.int32),
-            pltpu.SemaphoreType.DMA,
-        ],
-        compiler_params=PARAMS,
-        name="attention",
-    )(block_list.T, query_grad_rows, key_value, mate, halo)
+        scratch_shapes=[pltpu.VMEM(sums, jnp.float32)] + scratch,
+        compiler_params=PARAMS,
+        cost_estimate=work,
+        name="far",
+    )(block_list.T, query_grad_rows, key_value, mate, near, far, near_sums)
     mate_sum = to_mate(mate_part)
     halo_sum = moved(
         halo_part, ("z", "core"), lambda z, c: ((z + (depth - 1 if c else 1)) % depth, c)
@@ -309,11 +358,11 @@
     outgoing = pl.pallas_call(
         sum_kernel,
         out_shape=plane,
-        in_specs=[VMEM] * 3,
+        in_specs=[VMEM] * 4,
         out_specs=VMEM,
         compiler_params=PARAMS,
         name="total",
-    )(query_out, own_sum, mate_sum)
+    )(query_near, query_far, own_sum, mate_sum)
     returned = lax.all_to_all(outgoing, AXES, 0, 0, tiled=True)
     rows = jax.ShapeDtypeStruct(queries.shape, jnp.bfloat16)
     return pl.pallas_call(

time: 92.4 us -> 93.2 us (level)
  starting transfers between devices: 17.1 us -> 12.8 us
  waiting for transfers between devices: 8.85 us -> 12.4 us
  Pallas kernels: 14.8 us -> 16.4 us
    ppermute x4 -> x5, starting transfers between devices: 17.1 us -> 12.8 us  [moved(): return lax.ppermute(value, axes, pairs)]
    ppermute x4 -> x5, waiting for transfers between devices: 8.85 us -> 12.4 us  [moved(): return lax.ppermute(value, axes, pairs)]
    pallas_call x2 -> x3, Pallas kernels: 11 us -> 12.5 us  [the longest x1 6.29 us: per_device(): pl.pallas_call(far_kernel, out_shape=[jax.ShapeDtypeStruct(quarter, jnp.b...]
  transfers between devices with their start and end apart: 4 -> 5, of which waited for: 2 -> 2; matrix products, arithmetic and copies ran while one was open for 0% -> 0% of each run, Pallas kernels for 0% -> 7%
where the time goes in v5:
time: 93.2 us; the launch traced here: 92.8 us
  blocking collectives  50.5 us (54%)
  Pallas kernels  16.4 us (18%)
  starting transfers between devices  12.8 us (14%)
  waiting for transfers between devices  12.4 us (13%)
    all_to_all x1, blocking collectives, per_device(): received = lax.all_to_all(packed, AXES, 0, 0, tiled=True)  26.9 us
    all_to_all x1, blocking collectives, per_device(): returned = lax.all_to_all(outgoing, AXES, 0, 0, tiled=True)  23.6 us
    ppermute x5, starting transfers between devices, moved(): return lax.ppermute(value, axes, pairs)  12.8 us
    ppermute x5, waiting for transfers between devices, moved(): return lax.ppermute(value, axes, pairs)  12.4 us
    pallas_call x1, Pallas kernels, per_device(): pl.pallas_call(far_kernel, out_shape=[jax.ShapeDtypeStruct(quarter, jnp.b...  6.29 us
    pallas_call x1, Pallas kernels, per_device(): pl.pallas_call(near_kernel, out_shape=[jax.ShapeDtypeStruct(quarter, jnp....  6.07 us
    pallas_call x1, Pallas kernels, per_device(): pl.pallas_call(pack_kernel, out_shape=plane, in_specs=[ANY] * 4, out_spec...  2.44 us
  transfers between devices with their start and end apart: 5, of which 2 were waited for; matrix products, arithmetic and copies ran while one was open for 0% of the time, Pallas kernels for 7%

profile of v5, /device:TPU:1, one launch (start us, length us, event | category | flops | bytes accessed | tf_op | source)
XLA Modules:
  0.0 92.8 jit_solution(18249411396409302866)
XLA Ops:
  0.6 0.0 copy-start
  0.6 2.4 %pack.1 = bf16[32,128,128]{2,1,0:T(8,128)(2,1)} custom-call(bf16[128,1024]{1,0:T(8,128)(2,1)} %q_hbm.1, bf16[128,1024]{1,0:T(8,128)(2,1)} %k_hbm.1, bf16[128,1024]{1,0:T(8,128)(2,1)} %v_hbm.1, bf16[128,1024]{1,0:T(8,128)(2,1)} %g_hbm.1), custom_call_target="tpu_custom_call" | custom-call | tf_op jit(solution)/shard_map/pack/pallas_call | solution.py:269
  3.1 26.9 %all_to_all.10.in_ref = bf16[32,128,128]{2,1,0:T(8,128)(2,1)S(1)} all-to-all(bf16[32,128,128]{2,1,0:T(8,128)(2,1)} %pack.1), channel_id=1, replica_groups=mesh['x_lo'=2,'y'=4,'z'=16,'x_hi'=2,'core'=2] {'x_hi','core','x_lo','y'}, dimensions={0} | all-to-all | bytes 2097152 | tf_op jit(solution)/shard_map/all_to_all | solution.py:283
  30.0 0.1 split.1
  30.1 2.1 %collective-permute-start = (bf16[16,128,128]{2,1,0:T(8,128)(2,1)S(1)}, bf16[16,128,128]{2,1,0:T(8,128)(2,1)S(1)}, u32[]{:S(2)}, u32[]{:S(2)}) collective-permute-start(bf16[16,128,128]{2,1,0:T(8,128)(2,1)S(1)} %get-tuple-element.15.own_ref), channel_id=1, source_target_pairs={{0,1},{1,0},{2,3},{3,2},{4,5},{5,4},{6,7},{7,6},{8,9},{9,8},{10,11... | collective-permute-start | bytes 1572872 | tf_op jit(solution)/shard_map/ppermute | solution.py:259
  32.2 1.9 %collective-permute-start.1 = (bf16[8,128,128]{2,1,0:T(8,128)(2,1)S(1)}, bf16[8,128,128]{2,1,0:T(8,128)(2,1)S(1)}, u32[]{:S(2)}, u32[]{:S(2)}) collective-permute-start(bf16[8,128,128]{2,1,0:T(8,128)(2,1)S(1)} %get-tuple-element.16), channel_id=1, source_target_pairs={{0,60},{1,5},{4,0},{5,9},{8,4},{9,13},{12,8},{13,17},{16,12},{17,2... | collective-permute-start | bytes 786440 | tf_op jit(solution)/shard_map/ppermute | solution.py:259
  34.1 3.2 %collective-permute-start.2 = (bf16[8,128,128]{2,1,0:T(8,128)(2,1)S(1)}, bf16[8,128,128]{2,1,0:T(8,128)(2,1)S(1)}, u32[]{:S(2)}, u32[]{:S(2)}) collective-permute-start(bf16[8,128,128]{2,1,0:T(8,128)(2,1)S(1)} %get-tuple-element.18), channel_id=1, source_target_pairs={{0,60},{1,5},{4,0},{5,9},{8,4},{9,13},{12,8},{13,17},{16,12},{17,2... | collective-permute-start | bytes 786440 | tf_op jit(solution)/shard_map/ppermute | solution.py:259
  37.3 7.8 %collective-permute-done.1.near_ref = bf16[8,128,128]{2,1,0:T(8,128)(2,1)S(1)} collective-permute-done((bf16[8,128,128]{2,1,0:T(8,128)(2,1)S(1)}, bf16[8,128,128]{2,1,0:T(8,128)(2,1)S(1)}, u32[]{:S(2)}, u32[]{:S(2)}) %collective-permute-start.1) | collective-permute-done | bytes 262176 | tf_op jit(solution)/shard_map/ppermute | solution.py:259
  45.1 0.0 collective-permute-done.mate_ref
  45.1 0.0 copy-done
  45.1 6.1 %near.1 = (bf16[8,128,128]{2,1,0:T(8,128)(2,1)S(1)}, f32[48,128,128]{2,1,0:T(8,128)S(1)}) custom-call(s32[8,512]{1,0:T(8,128)S(1)} %bitcast.1, bf16[16,128,128]{2,1,0:T(8,128)(2,1)S(1)} %get-tuple-element.14.qg_ref, bf16[16,128,128]{2,1,0:T(8,128)(2,1)S(1)} %get-tuple-element.15.own_ref, bf16[16,128,128]{2,1,0:T(8,128)(2,1)S(1)} %collective-permute-done.mate_ref, ...), custom_call_target="tpu_custom_call" | custom-call | flops 1610612736 | bytes 1048576 | tf_op jit(solution)/shard_map/near/pallas_call | solution.py:318
  51.1 0.0 collective-permute-done.2.far_ref
  51.2 6.3 %far.1 = (bf16[8,128,128]{2,1,0:T(8,128)(2,1)S(1)}, f32[16,128,128]{2,1,0:T(8,128)S(1)}, bf16[16,128,128]{2,1,0:T(8,128)(2,1)S(1)}, bf16[16,128,128]{2,1,0:T(8,128)(2,1)S(1)}) custom-call(s32[8,512]{1,0:T(8,128)S(1)} %bitcast.2, bf16[16,128,128]{2,1,0:T(8,128)(2,1)S(1)} %get-tuple-element.14.qg_ref, bf16[16,128,128]{2,1,0:T(8,128)(2,1)S(1)} %get-tuple-element.15.own_ref, ...), custom_call_target="tpu_custom_call" | custom-call | flops 1610612736 | bytes 1048576 | tf_op jit(solution)/shard_map/far/pallas_call | solution.py:331
  57.5 3.7 %collective-permute-start.3 = (bf16[16,128,128]{2,1,0:T(8,128)(2,1)S(1)}, bf16[16,128,128]{2,1,0:T(8,128)(2,1)S(1)}, u32[]{:S(2)}, u32[]{:S(2)}) collective-permute-start(bf16[16,128,128]{2,1,0:T(8,128)(2,1)S(1)} %get-tuple-element.22), channel_id=1, source_target_pairs={{0,4},{1,61},{4,8},{5,1},{8,12},{9,5},{12,16},{13,9},{16,20},{17,1... | collective-permute-start | bytes 1572872 | tf_op jit(solution)/shard_map/ppermute | solution.py:259
  61.1 1.9 %collective-permute-start.4 = (bf16[16,128,128]{2,1,0:T(8,128)(2,1)S(1)}, bf16[16,128,128]{2,1,0:T(8,128)(2,1)S(1)}, u32[]{:S(2)}, u32[]{:S(2)}) collective-permute-start(bf16[16,128,128]{2,1,0:T(8,128)(2,1)S(1)} %get-tuple-element.23), channel_id=1, source_target_pairs={{0,1},{1,0},{2,3},{3,2},{4,5},{5,4},{6,7},{7,6},{8,9},{9,8},{10,11... | collective-permute-start | bytes 1572872 | tf_op jit(solution)/shard_map/ppermute | solution.py:259
  63.1 4.6 %collective-permute-done.3.halo_ref = bf16[16,128,128]{2,1,0:T(8,128)(2,1)S(1)} collective-permute-done((bf16[16,128,128]{2,1,0:T(8,128)(2,1)S(1)}, bf16[16,128,128]{2,1,0:T(8,128)(2,1)S(1)}, u32[]{:S(2)}, u32[]{:S(2)}) %collective-permute-start.3) | collective-permute-done | bytes 524320 | tf_op jit(solution)/shard_map/ppermute | solution.py:259
  67.7 0.1 halo_total.1.own_ref
  67.8 0.0 collective-permute-done.4.mate_ref
  67.8 0.1 total.1
  67.9 23.6 %all_to_all.11.in_ref = bf16[32,128,128]{2,1,0:T(8,128)(2,1)S(1)} all-to-all(bf16[32,128,128]{2,1,0:T(8,128)(2,1)S(1)} %total.1), channel_id=1, replica_groups=mesh['x_lo'=2,'y'=4,'z'=16,'x_hi'=2,'core'=2] {'x_hi','core','x_lo','y'}, dimensions={0} | all-to-all | bytes 2097152 | tf_op jit(solution)/shard_map/all_to_all | solution.py:366
  91.5 1.2 %unpack.1 = (bf16[128,1024]{1,0:T(8,128)(2,1)}, bf16[128,1024]{1,0:T(8,128)(2,1)}, bf16[128,1024]{1,0:T(8,128)(2,1)}, bf16[128,1024]{1,0:T(8,128)(2,1)}) custom-call(bf16[32,128,128]{2,1,0:T(8,128)(2,1)S(1)} %all_to_all.11.in_ref), custom_call_target="tpu_custom_call" | custom-call | tf_op jit(solution)/shard_map/unpack/pallas_call | solution.py:368
Async XLA Ops:
  0.6 44.4 %copy-start = (s32[512,8]{0,1:T(8,128)S(1)}, s32[512,8]{0,1:T(8,128)}, u32[]{:S(2)}) copy-start(s32[512,8]{0,1:T(8,128)} %param.9) | copy-start | bytes 49156
  30.1 14.9 %collective-permute-start = (bf16[16,128,128]{2,1,0:T(8,128)(2,1)S(1)}, bf16[16,128,128]{2,1,0:T(8,128)(2,1)S(1)}, u32[]{:S(2)}, u32[]{:S(2)}) collective-permute-start(bf16[16,128,128]{2,1,0:T(8,128)(2,1)S(1)} %get-tuple-element.15.own_ref), channel_id=1, source_target_pairs={{0,1},{1,0},{2,3},{3,2},{4,5},{5,4},{6,7},{7,6},{8,9},{9,8},{10,11... | collective-permute-start | bytes 1572872 | tf_op jit(solution)/shard_map/ppermute | solution.py:259
  32.2 12.9 %collective-permute-start.1 = (bf16[8,128,128]{2,1,0:T(8,128)(2,1)S(1)}, bf16[8,128,128]{2,1,0:T(8,128)(2,1)S(1)}, u32[]{:S(2)}, u32[]{:S(2)}) collective-permute-start(bf16[8,128,128]{2,1,0:T(8,128)(2,1)S(1)} %get-tuple-element.16), channel_id=1, source_target_pairs={{0,60},{1,5},{4,0},{5,9},{8,4},{9,13},{12,8},{13,17},{16,12},{17,2... | collective-permute-start | bytes 786440 | tf_op jit(solution)/shard_map/ppermute | solution.py:259
  34.1 17.0 %collective-permute-start.2 = (bf16[8,128,128]{2,1,0:T(8,128)(2,1)S(1)}, bf16[8,128,128]{2,1,0:T(8,128)(2,1)S(1)}, u32[]{:S(2)}, u32[]{:S(2)}) collective-permute-start(bf16[8,128,128]{2,1,0:T(8,128)(2,1)S(1)} %get-tuple-element.18), channel_id=1, source_target_pairs={{0,60},{1,5},{4,0},{5,9},{8,4},{9,13},{12,8},{13,17},{16,12},{17,2... | collective-permute-start | bytes 786440 | tf_op jit(solution)/shard_map/ppermute | solution.py:259
  57.5 10.2 %collective-permute-start.3 = (bf16[16,128,128]{2,1,0:T(8,128)(2,1)S(1)}, bf16[16,128,128]{2,1,0:T(8,128)(2,1)S(1)}, u32[]{:S(2)}, u32[]{:S(2)}) collective-permute-start(bf16[16,128,128]{2,1,0:T(8,128)(2,1)S(1)} %get-tuple-element.22), channel_id=1, source_target_pairs={{0,4},{1,61},{4,8},{5,1},{8,12},{9,5},{12,16},{13,9},{16,20},{17,1... | collective-permute-start | bytes 1572872 | tf_op jit(solution)/shard_map/ppermute | solution.py:259
  61.1 6.6 %collective-permute-start.4 = (bf16[16,128,128]{2,1,0:T(8,128)(2,1)S(1)}, bf16[16,128,128]{2,1,0:T(8,128)(2,1)S(1)}, u32[]{:S(2)}, u32[]{:S(2)}) collective-permute-start(bf16[16,128,128]{2,1,0:T(8,128)(2,1)S(1)} %get-tuple-element.23), channel_id=1, source_target_pairs={{0,1},{1,0},{2,3},{3,2},{4,5},{5,4},{6,7},{7,6},{8,9},{9,8},{10,11... | collective-permute-start | bytes 1572872 | tf_op jit(solution)/shard_map/ppermute | solution.py:259

commit v6 on v5

--- a/solution.py
+++ b/solution.py
@@ -110,6 +110,10 @@
     far_ref[...] = in_ref[pl.ds(kv_at + (1 - core) * QUARTER, QUARTER)]
 
 
+def copy_kernel(in_ref, out_ref):
+    out_ref[...] = in_ref[...]
+
+
 def near_kernel(list_hbm, qg_ref, own_ref, mate_ref, near_ref, qo_ref, sums, *scratch):
     sums[...] = jnp.zeros_like(sums)
     core = lax.axis_index("core")
@@ -297,7 +301,15 @@
     def inward(value):
         return moved(value, ("z", "core"), lambda z, c: ((z + (1 if c else depth - 1)) % depth, c))
 
-    near = inward(near_part)
+    near = pl.pallas_call(
+        copy_kernel,
+        out_shape=jax.ShapeDtypeStruct(quarter, jnp.bfloat16),
+        in_specs=[VMEM],
+        out_specs=VMEM,
+        compiler_params=PARAMS,
+        cost_estimate=pl.CostEstimate(flops=1 << 32, bytes_accessed=1 << 20, transcendentals=0),
+        name="near_copy",
+    )(inward(near_part))
     mate = to_mate(key_value)
     far = inward(far_part)
     scratch = [

time: 93.2 us -> 91.8 us (0.985)
  waiting for transfers between devices: 12.4 us -> 4.44 us
  starting transfers between devices: 12.8 us -> 19.6 us
    ppermute x5, waiting for transfers between devices: 12.4 us -> 4.44 us  [moved(): return lax.ppermute(value, axes, pairs)]
    ppermute x5, starting transfers between devices: 12.8 us -> 19.6 us  [moved(): return lax.ppermute(value, axes, pairs)]
where the time goes in v6:
time: 91.8 us; the launch traced here: 91.3 us
  blocking collectives  50.1 us (55%)
  starting transfers between devices  19.6 us (21%)
  Pallas kernels  16.4 us (18%)
  waiting for transfers between devices  4.44 us (5%)
    all_to_all x1, blocking collectives, per_device(): received = lax.all_to_all(packed, AXES, 0, 0, tiled=True)  26.9 us
    all_to_all x1, blocking collectives, per_device(): returned = lax.all_to_all(outgoing, AXES, 0, 0, tiled=True)  23.1 us
    ppermute x5, starting transfers between devices, moved(): return lax.ppermute(value, axes, pairs)  19.6 us
    pallas_call x1, Pallas kernels, per_device(): pl.pallas_call(far_kernel, out_shape=[jax.ShapeDtypeStruct(quarter, jnp.b...  6.29 us
    pallas_call x1, Pallas kernels, per_device(): pl.pallas_call(near_kernel, out_shape=[jax.ShapeDtypeStruct(quarter, jnp....  6.08 us
    ppermute x5, waiting for transfers between devices, moved(): return lax.ppermute(value, axes, pairs)  4.44 us
    pallas_call x1, Pallas kernels, per_device(): pl.pallas_call(pack_kernel, out_shape=plane, in_specs=[ANY] * 4, out_spec...  2.44 us
  transfers between devices with their start and end apart: 5, of which 2 were waited for; matrix products, arithmetic and copies ran while one was open for 0% of the time, Pallas kernels for 7%

profile of v6, /device:TPU:1, one launch (start us, length us, event | category | flops | bytes accessed | tf_op | source)
XLA Modules:
  0.0 91.3 jit_solution(13089915935993039433)
XLA Ops:
  0.6 2.4 %pack.1 = bf16[32,128,128]{2,1,0:T(8,128)(2,1)} custom-call(bf16[128,1024]{1,0:T(8,128)(2,1)} %q_hbm.1, bf16[128,1024]{1,0:T(8,128)(2,1)} %k_hbm.1, bf16[128,1024]{1,0:T(8,128)(2,1)} %v_hbm.1, bf16[128,1024]{1,0:T(8,128)(2,1)} %g_hbm.1), custom_call_target="tpu_custom_call" | custom-call | tf_op jit(solution)/shard_map/pack/pallas_call | solution.py:273
  3.1 26.9 %all_to_all.10.in_ref = bf16[32,128,128]{2,1,0:T(8,128)(2,1)S(1)} all-to-all(bf16[32,128,128]{2,1,0:T(8,128)(2,1)} %pack.1), channel_id=1, replica_groups=mesh['x_lo'=2,'y'=4,'z'=16,'x_hi'=2,'core'=2] {'x_hi','core','x_lo','y'}, dimensions={0} | all-to-all | bytes 2097152 | tf_op jit(solution)/shard_map/all_to_all | solution.py:287
  30.0 0.1 split.1
  30.1 1.9 %collective-permute-start.1 = (bf16[8,128,128]{2,1,0:T(8,128)(2,1)S(1)}, bf16[8,128,128]{2,1,0:T(8,128)(2,1)S(1)}, u32[]{:S(2)}, u32[]{:S(2)}) collective-permute-start(bf16[8,128,128]{2,1,0:T(8,128)(2,1)S(1)} %get-tuple-element.16), channel_id=1, source_target_pairs={{0,60},{1,5},{4,0},{5,9},{8,4},{9,13},{12,8},{13,17},{16,12},{17,2... | collective-permute-start | bytes 786440 | tf_op jit(solution)/shard_map/ppermute | solution.py:263
  32.0 9.5 %collective-permute-start = (bf16[16,128,128]{2,1,0:T(8,128)(2,1)S(1)}, bf16[16,128,128]{2,1,0:T(8,128)(2,1)S(1)}, u32[]{:S(2)}, u32[]{:S(2)}) collective-permute-start(bf16[16,128,128]{2,1,0:T(8,128)(2,1)S(1)} %get-tuple-element.15.own_ref), channel_id=1, source_target_pairs={{0,1},{1,0},{2,3},{3,2},{4,5},{5,4},{6,7},{7,6},{8,9},{9,8},{10,11... | collective-permute-start | bytes 1572872 | tf_op jit(solution)/shard_map/ppermute | solution.py:263
  41.6 0.0 copy-start
  41.6 1.9 %collective-permute-start.2 = (bf16[8,128,128]{2,1,0:T(8,128)(2,1)S(1)}, bf16[8,128,128]{2,1,0:T(8,128)(2,1)S(1)}, u32[]{:S(2)}, u32[]{:S(2)}) collective-permute-start(bf16[8,128,128]{2,1,0:T(8,128)(2,1)S(1)} %get-tuple-element.18), channel_id=1, source_target_pairs={{0,60},{1,5},{4,0},{5,9},{8,4},{9,13},{12,8},{13,17},{16,12},{17,2... | collective-permute-start | bytes 786440 | tf_op jit(solution)/shard_map/ppermute | solution.py:263
  43.5 0.0 collective-permute-done.1.in_ref
  43.6 0.0 collective-permute-done.mate_ref
  43.6 0.0 copy-done
  43.6 6.1 %near.1 = (bf16[8,128,128]{2,1,0:T(8,128)(2,1)S(1)}, f32[48,128,128]{2,1,0:T(8,128)S(1)}) custom-call(s32[8,512]{1,0:T(8,128)S(1)} %bitcast.1, bf16[16,128,128]{2,1,0:T(8,128)(2,1)S(1)} %get-tuple-element.14.qg_ref, bf16[16,128,128]{2,1,0:T(8,128)(2,1)S(1)} %get-tuple-element.15.own_ref, bf16[16,128,128]{2,1,0:T(8,128)(2,1)S(1)} %collective-permute-done.mate_ref, ...), custom_call_target="tpu_custom_call" | custom-call | flops 1610612736 | bytes 1048576 | tf_op jit(solution)/shard_map/near/pallas_call | solution.py:330
  49.7 0.3 collective-permute-done.2.far_ref
  49.9 6.3 %far.1 = (bf16[8,128,128]{2,1,0:T(8,128)(2,1)S(1)}, f32[16,128,128]{2,1,0:T(8,128)S(1)}, bf16[16,128,128]{2,1,0:T(8,128)(2,1)S(1)}, bf16[16,128,128]{2,1,0:T(8,128)(2,1)S(1)}) custom-call(s32[8,512]{1,0:T(8,128)S(1)} %bitcast.2, bf16[16,128,128]{2,1,0:T(8,128)(2,1)S(1)} %get-tuple-element.14.qg_ref, bf16[16,128,128]{2,1,0:T(8,128)(2,1)S(1)} %get-tuple-element.15.own_ref, ...), custom_call_target="tpu_custom_call" | custom-call | flops 1610612736 | bytes 1048576 | tf_op jit(solution)/shard_map/far/pallas_call | solution.py:343
  56.2 4.3 %collective-permute-start.3 = (bf16[16,128,128]{2,1,0:T(8,128)(2,1)S(1)}, bf16[16,128,128]{2,1,0:T(8,128)(2,1)S(1)}, u32[]{:S(2)}, u32[]{:S(2)}) collective-permute-start(bf16[16,128,128]{2,1,0:T(8,128)(2,1)S(1)} %get-tuple-element.22), channel_id=1, source_target_pairs={{0,4},{1,61},{4,8},{5,1},{8,12},{9,5},{12,16},{13,9},{16,20},{17,1... | collective-permute-start | bytes 1572872 | tf_op jit(solution)/shard_map/ppermute | solution.py:263
  60.6 1.9 %collective-permute-start.4 = (bf16[16,128,128]{2,1,0:T(8,128)(2,1)S(1)}, bf16[16,128,128]{2,1,0:T(8,128)(2,1)S(1)}, u32[]{:S(2)}, u32[]{:S(2)}) collective-permute-start(bf16[16,128,128]{2,1,0:T(8,128)(2,1)S(1)} %get-tuple-element.23), channel_id=1, source_target_pairs={{0,1},{1,0},{2,3},{3,2},{4,5},{5,4},{6,7},{7,6},{8,9},{9,8},{10,11... | collective-permute-start | bytes 1572872 | tf_op jit(solution)/shard_map/ppermute | solution.py:263
  62.5 4.2 %collective-permute-done.3.halo_ref = bf16[16,128,128]{2,1,0:T(8,128)(2,1)S(1)} collective-permute-done((bf16[16,128,128]{2,1,0:T(8,128)(2,1)S(1)}, bf16[16,128,128]{2,1,0:T(8,128)(2,1)S(1)}, u32[]{:S(2)}, u32[]{:S(2)}) %collective-permute-start.3) | collective-permute-done | bytes 524320 | tf_op jit(solution)/shard_map/ppermute | solution.py:263
  66.7 0.1 halo_total.1.own_ref
  66.8 0.0 collective-permute-done.4.mate_ref
  66.8 0.1 total.1
  66.9 23.1 %all_to_all.11.in_ref = bf16[32,128,128]{2,1,0:T(8,128)(2,1)S(1)} all-to-all(bf16[32,128,128]{2,1,0:T(8,128)(2,1)S(1)} %total.1), channel_id=1, replica_groups=mesh['x_lo'=2,'y'=4,'z'=16,'x_hi'=2,'core'=2] {'x_hi','core','x_lo','y'}, dimensions={0} | all-to-all | bytes 2097152 | tf_op jit(solution)/shard_map/all_to_all | solution.py:378
  90.1 1.2 %unpack.1 = (bf16[128,1024]{1,0:T(8,128)(2,1)}, bf16[128,1024]{1,0:T(8,128)(2,1)}, bf16[128,1024]{1,0:T(8,128)(2,1)}, bf16[128,1024]{1,0:T(8,128)(2,1)}) custom-call(bf16[32,128,128]{2,1,0:T(8,128)(2,1)S(1)} %all_to_all.11.in_ref), custom_call_target="tpu_custom_call" | custom-call | tf_op jit(solution)/shard_map/unpack/pallas_call | solution.py:380
  (1 shorter events, 0.0 us)
Async XLA Ops:
  30.1 13.4 %collective-permute-start.1 = (bf16[8,128,128]{2,1,0:T(8,128)(2,1)S(1)}, bf16[8,128,128]{2,1,0:T(8,128)(2,1)S(1)}, u32[]{:S(2)}, u32[]{:S(2)}) collective-permute-start(bf16[8,128,128]{2,1,0:T(8,128)(2,1)S(1)} %get-tuple-element.16), channel_id=1, source_target_pairs={{0,60},{1,5},{4,0},{5,9},{8,4},{9,13},{12,8},{13,17},{16,12},{17,2... | collective-permute-start | bytes 786440 | tf_op jit(solution)/shard_map/ppermute | solution.py:263
  32.0 11.5 %collective-permute-start = (bf16[16,128,128]{2,1,0:T(8,128)(2,1)S(1)}, bf16[16,128,128]{2,1,0:T(8,128)(2,1)S(1)}, u32[]{:S(2)}, u32[]{:S(2)}) collective-permute-start(bf16[16,128,128]{2,1,0:T(8,128)(2,1)S(1)} %get-tuple-element.15.own_ref), channel_id=1, source_target_pairs={{0,1},{1,0},{2,3},{3,2},{4,5},{5,4},{6,7},{7,6},{8,9},{9,8},{10,11... | collective-permute-start | bytes 1572872 | tf_op jit(solution)/shard_map/ppermute | solution.py:263
  41.6 2.0 %copy-start = (s32[512,8]{0,1:T(8,128)S(1)}, s32[512,8]{0,1:T(8,128)}, u32[]{:S(2)}) copy-start(s32[512,8]{0,1:T(8,128)} %param.9) | copy-start | bytes 49156
  41.6 8.3 %collective-permute-start.2 = (bf16[8,128,128]{2,1,0:T(8,128)(2,1)S(1)}, bf16[8,128,128]{2,1,0:T(8,128)(2,1)S(1)}, u32[]{:S(2)}, u32[]{:S(2)}) collective-permute-start(bf16[8,128,128]{2,1,0:T(8,128)(2,1)S(1)} %get-tuple-element.18), channel_id=1, source_target_pairs={{0,60},{1,5},{4,0},{5,9},{8,4},{9,13},{12,8},{13,17},{16,12},{17,2... | collective-permute-start | bytes 786440 | tf_op jit(solution)/shard_map/ppermute | solution.py:263
  56.2 10.4 %collective-permute-start.3 = (bf16[16,128,128]{2,1,0:T(8,128)(2,1)S(1)}, bf16[16,128,128]{2,1,0:T(8,128)(2,1)S(1)}, u32[]{:S(2)}, u32[]{:S(2)}) collective-permute-start(bf16[16,128,128]{2,1,0:T(8,128)(2,1)S(1)} %get-tuple-element.22), channel_id=1, source_target_pairs={{0,4},{1,61},{4,8},{5,1},{8,12},{9,5},{12,16},{13,9},{16,20},{17,1... | collective-permute-start | bytes 1572872 | tf_op jit(solution)/shard_map/ppermute | solution.py:263
  60.6 6.2 %collective-permute-start.4 = (bf16[16,128,128]{2,1,0:T(8,128)(2,1)S(1)}, bf16[16,128,128]{2,1,0:T(8,128)(2,1)S(1)}, u32[]{:S(2)}, u32[]{:S(2)}) collective-permute-start(bf16[16,128,128]{2,1,0:T(8,128)(2,1)S(1)} %get-tuple-element.23), channel_id=1, source_target_pairs={{0,1},{1,0},{2,3},{3,2},{4,5},{5,4},{6,7},{7,6},{8,9},{9,8},{10,11... | collective-permute-start | bytes 1572872 | tf_op jit(solution)/shard_map/ppermute | solution.py:263

commit v7 on v6

--- a/solution.py
+++ b/solution.py
@@ -19,6 +19,9 @@
 VMEM_LIMIT = 40 * 1024 * 1024
 KEYS = SLOTS * BLOCK
 CHUNK = 16
+PIECES = 4
+SPAN = KEYS // PIECES
+PAIR = SLOTS // PIECES
 LANES = 128
 PART = 256
 PARTS = HEADS * HEAD_SIZE // PART
@@ -29,6 +32,13 @@
     return jnp.concatenate(
         [left[:, start : start + HEAD_SIZE], right[:, start : start + HEAD_SIZE]], axis=1
     )
+
+
+def turned_pair(left, right, odd):
+    start = HEAD_SIZE if odd else 0
+    return jnp.concatenate(
+        [left[start : start + HEAD_SIZE], right[start : start + HEAD_SIZE]], axis=0
+    ).T
 
 
 def slot_of(head, core):
@@ -84,8 +94,8 @@
         even, odd = 2 * pair, 2 * pair + 1
         kv0, kv1 = in_ref[slot_of(even, x_hi)], in_ref[slot_of(odd, x_hi)]
         qo0, qo1 = in_ref[slot_of(even, 1 - x_hi)], in_ref[slot_of(odd, 1 - x_hi)]
-        dk_ref[:, columns] = lane_pair(kv0, kv1, 0)
-        dv_ref[:, columns] = lane_pair(kv0, kv1, 1)
+        dk_ref[:, columns] = turned_pair(kv0, kv1, 0)
+        dv_ref[:, columns] = turned_pair(kv0, kv1, 1)
         dq_ref[:, columns] = lane_pair(qo0, qo1, 0)
         o_ref[:, columns] = lane_pair(qo0, qo1, 1)
         if (pair + 1) * WIDTH % PART == 0:
@@ -175,9 +185,6 @@
 
     left = lax.broadcasted_iota(jnp.int32, (BLOCK, WIDTH), 1) < HEAD_SIZE
 
-    def listed_rows(i):
-        return jnp.concatenate([window[b] for b in blocks_of(i)], axis=0)
-
     def query_rows(i):
         qg = qg_ref[first + i]
         zero = jnp.zeros_like(qg)
@@ -185,11 +192,24 @@
             [jnp.where(left, qg * jnp.bfloat16(SCALING), zero), jnp.where(left, zero, qg)], axis=0
         )
 
+    top = lax.broadcasted_iota(jnp.int32, (WIDTH, BLOCK), 0) < HEAD_SIZE
+
+    def query_columns(i):
+        columns = qg_ref[first + i].T
+        zero = jnp.zeros_like(columns)
+        return jnp.concatenate(
+            [jnp.where(top, columns * jnp.bfloat16(SCALING), zero), jnp.where(top, zero, columns)],
+            axis=1,
+        )
+
     def products(i, both):
-        both[...] = lax.dot_general(
-            query_rows(i), listed_rows(i), (((1,), (1,)), ((), ())),
-            preferred_element_type=jnp.float32,
-        )
+        rows, blocks = query_rows(i), blocks_of(i)
+        for k in range(PIECES):
+            kv = jnp.concatenate([window[b] for b in blocks[k * PAIR : (k + 1) * PAIR]], axis=0)
+            both[:, k * SPAN : (k + 1) * SPAN] = lax.dot_general(
+                rows, kv, (((1,), (1,)), ((), ())), preferred_element_type=jnp.float32
+            )
+            yield
 
     def weigh(i, both, pair):
         live = [table[i, s] >= 0 for s in range(SLOTS)]
@@ -208,31 +228,50 @@
             dscore = terms - probs * jnp.sum(terms, axis=1, keepdims=True)
             pair[r : r + CHUNK] = dscore.astype(jnp.bfloat16)
             pair[BLOCK + r : BLOCK + r + CHUNK] = probs.astype(jnp.bfloat16)
+            if (r // CHUNK + 1) % (BLOCK // CHUNK // PIECES) == 0:
+                yield
 
     def results(i, pair):
-        stacked = pair[...]
-        mixed = jnp.dot(stacked, listed_rows(i), preferred_element_type=jnp.float32)
-        qo_ref[i] = jnp.where(left, mixed[:BLOCK] * SCALING, mixed[BLOCK:]).astype(jnp.bfloat16)
-        grads = lax.dot_general(
-            stacked, query_rows(i), (((0,), (0,)), ((), ())), preferred_element_type=jnp.float32
-        )
-        for s, block in enumerate(blocks_of(i)):
-            accum[block] += grads[s * BLOCK : (s + 1) * BLOCK]
-
-    products(0, both_even)
+        blocks = blocks_of(i)
+        columns = query_columns(i)
+        mixed = None
+        for k in range(PIECES):
+            stacked = pair[:, k * SPAN : (k + 1) * SPAN]
+            here = blocks[k * PAIR : (k + 1) * PAIR]
+            kv = jnp.concatenate([window[b] for b in here], axis=0)
+            part = jnp.dot(stacked, kv, preferred_element_type=jnp.float32)
+            mixed = part if mixed is None else mixed + part
+            grads = jnp.dot(columns, stacked, preferred_element_type=jnp.float32)
+            for s, block in enumerate(here):
+                accum[block] += grads[:, s * BLOCK : (s + 1) * BLOCK]
+            if k == PIECES - 1:
+                qo_ref[i] = jnp.where(left, mixed[:BLOCK] * SCALING, mixed[BLOCK:]).astype(
+                    jnp.bfloat16
+                )
+            yield
+
+    def beside(*stages):
+        for _ in zip(*stages):
+            pass
+
+    beside(products(0, both_even))
 
     def step(j, carry):
         even, odd = 2 * j, 2 * j + 1
-        products(odd, both_odd)
-        weigh(even, both_even, pair_even)
-        results(jnp.maximum(even - 1, 0), pair_odd)
-        products(jnp.minimum(even + 2, QUARTER - 1), both_even)
-        weigh(odd, both_odd, pair_odd)
-        results(even, pair_even)
+        beside(
+            products(odd, both_odd),
+            weigh(even, both_even, pair_even),
+            results(jnp.maximum(even - 1, 0), pair_odd),
+        )
+        beside(
+            products(jnp.minimum(even + 2, QUARTER - 1), both_even),
+            weigh(odd, both_odd, pair_odd),
+            results(even, pair_even),
+        )
         return carry
 
     lax.fori_loop(0, QUARTER // 2, step, 0)
-    results(QUARTER - 1, pair_odd)
+    beside(results(QUARTER - 1, pair_odd))
 
 
 def halo_sum_kernel(own_ref, halo_ref, out_ref):

time: 91.8 us -> 90.7 us (0.988)
  Pallas kernels: 16.4 us -> 15.3 us
  waiting for transfers between devices: 4.44 us -> 5.41 us
    ppermute x5, waiting for transfers between devices: 4.44 us -> 5.41 us  [moved(): return lax.ppermute(value, axes, pairs)]
  transfers between devices with their start and end apart: 5 -> 5, of which waited for: 2 -> 2; matrix products, arithmetic and copies ran while one was open for 0% -> 0% of each run, Pallas kernels for 7% -> 6%
where the time goes in v7:
time: 90.7 us; the launch traced here: 90.2 us
  blocking collectives  49.7 us (55%)
  starting transfers between devices  19 us (21%)
  Pallas kernels  15.3 us (17%)
  waiting for transfers between devices  5.41 us (6%)
    all_to_all x1, blocking collectives, per_device(): received = lax.all_to_all(packed, AXES, 0, 0, tiled=True)  26.9 us
    all_to_all x1, blocking collectives, per_device(): returned = lax.all_to_all(outgoing, AXES, 0, 0, tiled=True)  22.8 us
    ppermute x5, starting transfers between devices, moved(): return lax.ppermute(value, axes, pairs)  19 us
    pallas_call x1, Pallas kernels, per_device(): pl.pallas_call(far_kernel, out_shape=[jax.ShapeDtypeStruct(quarter, jnp.b...  5.69 us
    pallas_call x1, Pallas kernels, per_device(): pl.pallas_call(near_kernel, out_shape=[jax.ShapeDtypeStruct(quarter, jnp....  5.48 us
    ppermute x5, waiting for transfers between devices, moved(): return lax.ppermute(value, axes, pairs)  5.41 us
    pallas_call x1, Pallas kernels, per_device(): pl.pallas_call(pack_kernel, out_shape=plane, in_specs=[ANY] * 4, out_spec...  2.44 us
  transfers between devices with their start and end apart: 5, of which 2 were waited for; matrix products, arithmetic and copies ran while one was open for 0% of the time, Pallas kernels for 6%

profile of v7, /device:TPU:1, one launch (start us, length us, event | category | flops | bytes accessed | tf_op | source)
XLA Modules:
  0.0 90.2 jit_solution(10289750429254101722)
XLA Ops:
  0.6 2.4 %pack.1 = bf16[32,128,128]{2,1,0:T(8,128)(2,1)} custom-call(bf16[128,1024]{1,0:T(8,128)(2,1)} %q_hbm.1, bf16[128,1024]{1,0:T(8,128)(2,1)} %k_hbm.1, bf16[128,1024]{1,0:T(8,128)(2,1)} %v_hbm.1, bf16[128,1024]{1,0:T(8,128)(2,1)} %g_hbm.1), custom_call_target="tpu_custom_call" | custom-call | tf_op jit(solution)/shard_map/pack/pallas_call | solution.py:312
  3.1 26.9 %all_to_all.10.in_ref = bf16[32,128,128]{2,1,0:T(8,128)(2,1)S(1)} all-to-all(bf16[32,128,128]{2,1,0:T(8,128)(2,1)} %pack.1), channel_id=1, replica_groups=mesh['x_lo'=2,'y'=4,'z'=16,'x_hi'=2,'core'=2] {'x_hi','core','x_lo','y'}, dimensions={0} | all-to-all | bytes 2097152 | tf_op jit(solution)/shard_map/all_to_all | solution.py:326
  30.0 0.1 split.1
  30.1 1.9 %collective-permute-start.1 = (bf16[8,128,128]{2,1,0:T(8,128)(2,1)S(1)}, bf16[8,128,128]{2,1,0:T(8,128)(2,1)S(1)}, u32[]{:S(2)}, u32[]{:S(2)}) collective-permute-start(bf16[8,128,128]{2,1,0:T(8,128)(2,1)S(1)} %get-tuple-element.16), channel_id=1, source_target_pairs={{0,60},{1,5},{4,0},{5,9},{8,4},{9,13},{12,8},{13,17},{16,12},{17,2... | collective-permute-start | bytes 786440 | tf_op jit(solution)/shard_map/ppermute | solution.py:302
  32.0 9.5 %collective-permute-start = (bf16[16,128,128]{2,1,0:T(8,128)(2,1)S(1)}, bf16[16,128,128]{2,1,0:T(8,128)(2,1)S(1)}, u32[]{:S(2)}, u32[]{:S(2)}) collective-permute-start(bf16[16,128,128]{2,1,0:T(8,128)(2,1)S(1)} %get-tuple-element.15.own_ref), channel_id=1, source_target_pairs={{0,1},{1,0},{2,3},{3,2},{4,5},{5,4},{6,7},{7,6},{8,9},{9,8},{10,11... | collective-permute-start | bytes 1572872 | tf_op jit(solution)/shard_map/ppermute | solution.py:302
  41.6 0.0 copy-start
  41.6 1.9 %collective-permute-start.2 = (bf16[8,128,128]{2,1,0:T(8,128)(2,1)S(1)}, bf16[8,128,128]{2,1,0:T(8,128)(2,1)S(1)}, u32[]{:S(2)}, u32[]{:S(2)}) collective-permute-start(bf16[8,128,128]{2,1,0:T(8,128)(2,1)S(1)} %get-tuple-element.18), channel_id=1, source_target_pairs={{0,60},{1,5},{4,0},{5,9},{8,4},{9,13},{12,8},{13,17},{16,12},{17,2... | collective-permute-start | bytes 786440 | tf_op jit(solution)/shard_map/ppermute | solution.py:302
  43.5 0.0 collective-permute-done.1.in_ref
  43.6 0.0 collective-permute-done.mate_ref
  43.6 0.0 copy-done
  43.6 5.5 %near.1 = (bf16[8,128,128]{2,1,0:T(8,128)(2,1)S(1)}, f32[48,128,128]{2,1,0:T(8,128)S(1)}) custom-call(s32[8,512]{1,0:T(8,128)S(1)} %bitcast.1, bf16[16,128,128]{2,1,0:T(8,128)(2,1)S(1)} %get-tuple-element.14.qg_ref, bf16[16,128,128]{2,1,0:T(8,128)(2,1)S(1)} %get-tuple-element.15.own_ref, bf16[16,128,128]{2,1,0:T(8,128)(2,1)S(1)} %collective-permute-done.mate_ref, ...), custom_call_target="tpu_custom_call" | custom-call | flops 1610612736 | bytes 1048576 | tf_op jit(solution)/shard_map/near/pallas_call | solution.py:369
  49.1 0.8 collective-permute-done.2.far_ref
  49.9 5.7 %far.1 = (bf16[8,128,128]{2,1,0:T(8,128)(2,1)S(1)}, f32[16,128,128]{2,1,0:T(8,128)S(1)}, bf16[16,128,128]{2,1,0:T(8,128)(2,1)S(1)}, bf16[16,128,128]{2,1,0:T(8,128)(2,1)S(1)}) custom-call(s32[8,512]{1,0:T(8,128)S(1)} %bitcast.2, bf16[16,128,128]{2,1,0:T(8,128)(2,1)S(1)} %get-tuple-element.14.qg_ref, bf16[16,128,128]{2,1,0:T(8,128)(2,1)S(1)} %get-tuple-element.15.own_ref, ...), custom_call_target="tpu_custom_call" | custom-call | flops 1610612736 | bytes 1048576 | tf_op jit(solution)/shard_map/far/pallas_call | solution.py:382
  55.6 3.7 %collective-permute-start.3 = (bf16[16,128,128]{2,1,0:T(8,128)(2,1)S(1)}, bf16[16,128,128]{2,1,0:T(8,128)(2,1)S(1)}, u32[]{:S(2)}, u32[]{:S(2)}) collective-permute-start(bf16[16,128,128]{2,1,0:T(8,128)(2,1)S(1)} %get-tuple-element.22), channel_id=1, source_target_pairs={{0,4},{1,61},{4,8},{5,1},{8,12},{9,5},{12,16},{13,9},{16,20},{17,1... | collective-permute-start | bytes 1572872 | tf_op jit(solution)/shard_map/ppermute | solution.py:302
  59.4 1.9 %collective-permute-start.4 = (bf16[16,128,128]{2,1,0:T(8,128)(2,1)S(1)}, bf16[16,128,128]{2,1,0:T(8,128)(2,1)S(1)}, u32[]{:S(2)}, u32[]{:S(2)}) collective-permute-start(bf16[16,128,128]{2,1,0:T(8,128)(2,1)S(1)} %get-tuple-element.23), channel_id=1, source_target_pairs={{0,1},{1,0},{2,3},{3,2},{4,5},{5,4},{6,7},{7,6},{8,9},{9,8},{10,11... | collective-permute-start | bytes 1572872 | tf_op jit(solution)/shard_map/ppermute | solution.py:302
  61.3 4.6 %collective-permute-done.3.halo_ref = bf16[16,128,128]{2,1,0:T(8,128)(2,1)S(1)} collective-permute-done((bf16[16,128,128]{2,1,0:T(8,128)(2,1)S(1)}, bf16[16,128,128]{2,1,0:T(8,128)(2,1)S(1)}, u32[]{:S(2)}, u32[]{:S(2)}) %collective-permute-start.3) | collective-permute-done | bytes 524320 | tf_op jit(solution)/shard_map/ppermute | solution.py:302
  65.8 0.1 halo_total.1.own_ref
  65.9 0.0 collective-permute-done.4.mate_ref
  66.0 0.1 total.1
  66.1 22.8 %all_to_all.11.in_ref = bf16[32,128,128]{2,1,0:T(8,128)(2,1)S(1)} all-to-all(bf16[32,128,128]{2,1,0:T(8,128)(2,1)S(1)} %total.1), channel_id=1, replica_groups=mesh['x_lo'=2,'y'=4,'z'=16,'x_hi'=2,'core'=2] {'x_hi','core','x_lo','y'}, dimensions={0} | all-to-all | bytes 2097152 | tf_op jit(solution)/shard_map/all_to_all | solution.py:417
  88.8 1.3 %unpack.1 = (bf16[128,1024]{1,0:T(8,128)(2,1)}, bf16[128,1024]{1,0:T(8,128)(2,1)}, bf16[128,1024]{1,0:T(8,128)(2,1)}, bf16[128,1024]{1,0:T(8,128)(2,1)}) custom-call(bf16[32,128,128]{2,1,0:T(8,128)(2,1)S(1)} %all_to_all.11.in_ref), custom_call_target="tpu_custom_call" | custom-call | tf_op jit(solution)/shard_map/unpack/pallas_call | solution.py:419
  (1 shorter events, 0.0 us)
Async XLA Ops:
  30.1 13.4 %collective-permute-start.1 = (bf16[8,128,128]{2,1,0:T(8,128)(2,1)S(1)}, bf16[8,128,128]{2,1,0:T(8,128)(2,1)S(1)}, u32[]{:S(2)}, u32[]{:S(2)}) collective-permute-start(bf16[8,128,128]{2,1,0:T(8,128)(2,1)S(1)} %get-tuple-element.16), channel_id=1, source_target_pairs={{0,60},{1,5},{4,0},{5,9},{8,4},{9,13},{12,8},{13,17},{16,12},{17,2... | collective-permute-start | bytes 786440 | tf_op jit(solution)/shard_map/ppermute | solution.py:302
  32.0 11.5 %collective-permute-start = (bf16[16,128,128]{2,1,0:T(8,128)(2,1)S(1)}, bf16[16,128,128]{2,1,0:T(8,128)(2,1)S(1)}, u32[]{:S(2)}, u32[]{:S(2)}) collective-permute-start(bf16[16,128,128]{2,1,0:T(8,128)(2,1)S(1)} %get-tuple-element.15.own_ref), channel_id=1, source_target_pairs={{0,1},{1,0},{2,3},{3,2},{4,5},{5,4},{6,7},{7,6},{8,9},{9,8},{10,11... | collective-permute-start | bytes 1572872 | tf_op jit(solution)/shard_map/ppermute | solution.py:302
  41.6 2.0 %copy-start = (s32[512,8]{0,1:T(8,128)S(1)}, s32[512,8]{0,1:T(8,128)}, u32[]{:S(2)}) copy-start(s32[512,8]{0,1:T(8,128)} %param.9) | copy-start | bytes 49156
  41.6 8.3 %collective-permute-start.2 = (bf16[8,128,128]{2,1,0:T(8,128)(2,1)S(1)}, bf16[8,128,128]{2,1,0:T(8,128)(2,1)S(1)}, u32[]{:S(2)}, u32[]{:S(2)}) collective-permute-start(bf16[8,128,128]{2,1,0:T(8,128)(2,1)S(1)} %get-tuple-element.18), channel_id=1, source_target_pairs={{0,60},{1,5},{4,0},{5,9},{8,4},{9,13},{12,8},{13,17},{16,12},{17,2... | collective-permute-start | bytes 786440 | tf_op jit(solution)/shard_map/ppermute | solution.py:302
  55.6 10.2 %collective-permute-start.3 = (bf16[16,128,128]{2,1,0:T(8,128)(2,1)S(1)}, bf16[16,128,128]{2,1,0:T(8,128)(2,1)S(1)}, u32[]{:S(2)}, u32[]{:S(2)}) collective-permute-start(bf16[16,128,128]{2,1,0:T(8,128)(2,1)S(1)} %get-tuple-element.22), channel_id=1, source_target_pairs={{0,4},{1,61},{4,8},{5,1},{8,12},{9,5},{12,16},{13,9},{16,20},{17,1... | collective-permute-start | bytes 1572872 | tf_op jit(solution)/shard_map/ppermute | solution.py:302
  59.4 6.6 %collective-permute-start.4 = (bf16[16,128,128]{2,1,0:T(8,128)(2,1)S(1)}, bf16[16,128,128]{2,1,0:T(8,128)(2,1)S(1)}, u32[]{:S(2)}, u32[]{:S(2)}) collective-permute-start(bf16[16,128,128]{2,1,0:T(8,128)(2,1)S(1)} %get-tuple-element.23), channel_id=1, source_target_pairs={{0,1},{1,0},{2,3},{3,2},{4,5},{5,4},{6,7},{7,6},{8,9},{9,8},{10,11... | collective-permute-start | bytes 1572872 | tf_op jit(solution)/shard_map/ppermute | solution.py:302

commit v8 on v7

--- a/solution.py
+++ b/solution.py
@@ -298,7 +298,9 @@
     pairs = []
     for source in range(int(np.prod(sizes))):
         spot = [int(t) for t in np.unravel_index(source, sizes)]
-        pairs.append((source, int(np.ravel_multi_index(target(*spot), sizes))))
+        goal = target(*spot)
+        if all(0 <= g < size for g, size in zip(goal, sizes)):
+            pairs.append((source, int(np.ravel_multi_index(goal, sizes))))
     return lax.ppermute(value, axes, pairs)
 
 
@@ -307,7 +309,6 @@
 
 
 def per_device(queries, key_rows, value_rows, cotangent, block_list):
-    depth = lax.axis_size("z")
     plane = jax.ShapeDtypeStruct((PLANE, BLOCK, WIDTH), jnp.bfloat16)
     packed = pl.pallas_call(
         pack_kernel,
@@ -338,7 +339,7 @@
     )(received)
 
     def inward(value):
-        return moved(value, ("z", "core"), lambda z, c: ((z + (1 if c else depth - 1)) % depth, c))
+        return moved(value, ("z", "core"), lambda z, c: (z + (1 if c else -1), c))
 
     near = pl.pallas_call(
         copy_kernel,
@@ -395,9 +396,7 @@
         name="far",
     )(block_list.T, query_grad_rows, key_value, mate, near, far, near_sums)
     mate_sum = to_mate(mate_part)
-    halo_sum = moved(
-        halo_part, ("z", "core"), lambda z, c: ((z + (depth - 1 if c else 1)) % depth, c)
-    )
+    halo_sum = moved(halo_part, ("z", "core"), lambda z, c: (z + (-1 if c else 1), c))
     own_sum = pl.pallas_call(
         halo_sum_kernel,
         out_shape=jax.ShapeDtypeStruct(half, jnp.float32),

time: 90.7 us -> 83.1 us (0.916)
  the two profiles are of different devices: /device:TPU:1 before, /device:TPU:97 now
where the time goes in v8:
time: 83.1 us; the launch traced here: 82.6 us
  blocking collectives  45.2 us (54%)
  starting transfers between devices  16.2 us (19%)
  Pallas kernels  15.3 us (18%)
  waiting for transfers between devices  5.2 us (6%)
    all_to_all x1, blocking collectives, per_device(): received = lax.all_to_all(packed, AXES, 0, 0, tiled=True)  24.1 us
    all_to_all x1, blocking collectives, per_device(): returned = lax.all_to_all(outgoing, AXES, 0, 0, tiled=True)  21.1 us
    ppermute x5, starting transfers between devices, moved(): return lax.ppermute(value, axes, pairs)  16.2 us
    pallas_call x1, Pallas kernels, per_device(): pl.pallas_call(far_kernel, out_shape=[jax.ShapeDtypeStruct(quarter, jnp.b...  5.7 us
    pallas_call x1, Pallas kernels, per_device(): pl.pallas_call(near_kernel, out_shape=[jax.ShapeDtypeStruct(quarter, jnp....  5.46 us
    ppermute x5, waiting for transfers between devices, moved(): return lax.ppermute(value, axes, pairs)  5.2 us
    pallas_call x1, Pallas kernels, per_device(): pl.pallas_call(pack_kernel, out_shape=plane, in_specs=[ANY] * 4, out_spec...  2.44 us
  transfers between devices with their start and end apart: 5, of which 1 were waited for; matrix products, arithmetic and copies ran while one was open for 0% of the time, Pallas kernels for 7%

profile of v8, /device:TPU:97, one launch (start us, length us, event | category | flops | bytes accessed | tf_op | source)
XLA Modules:
  0.0 82.6 jit_solution(12565476508974564992)
XLA Ops:
  0.6 2.4 %pack.1 = bf16[32,128,128]{2,1,0:T(8,128)(2,1)} custom-call(bf16[128,1024]{1,0:T(8,128)(2,1)} %q_hbm.1, bf16[128,1024]{1,0:T(8,128)(2,1)} %k_hbm.1, bf16[128,1024]{1,0:T(8,128)(2,1)} %v_hbm.1, bf16[128,1024]{1,0:T(8,128)(2,1)} %g_hbm.1), custom_call_target="tpu_custom_call" | custom-call | tf_op jit(solution)/shard_map/pack/pallas_call | solution.py:313
  3.1 24.1 %all_to_all.10.in_ref = bf16[32,128,128]{2,1,0:T(8,128)(2,1)S(1)} all-to-all(bf16[32,128,128]{2,1,0:T(8,128)(2,1)} %pack.1), channel_id=1, replica_groups=mesh['x_lo'=2,'y'=4,'z'=16,'x_hi'=2,'core'=2] {'x_hi','core','x_lo','y'}, dimensions={0} | all-to-all | bytes 2097152 | tf_op jit(solution)/shard_map/all_to_all | solution.py:327
  27.2 0.1 split.1
  27.3 4.8 %collective-permute-start.1 = (bf16[8,128,128]{2,1,0:T(8,128)(2,1)S(1)}, bf16[8,128,128]{2,1,0:T(8,128)(2,1)S(1)}, u32[]{:S(2)}, u32[]{:S(2)}) collective-permute-start(bf16[8,128,128]{2,1,0:T(8,128)(2,1)S(1)} %get-tuple-element.16), channel_id=1, source_target_pairs={{1,5},{4,0},{5,9},{8,4},{9,13},{12,8},{13,17},{16,12},{17,21},{20,... | collective-permute-start | bytes 786440 | tf_op jit(solution)/shard_map/ppermute | solution.py:304
  32.1 1.9 %collective-permute-start = (bf16[16,128,128]{2,1,0:T(8,128)(2,1)S(1)}, bf16[16,128,128]{2,1,0:T(8,128)(2,1)S(1)}, u32[]{:S(2)}, u32[]{:S(2)}) collective-permute-start(bf16[16,128,128]{2,1,0:T(8,128)(2,1)S(1)} %get-tuple-element.15.own_ref), channel_id=1, source_target_pairs={{0,1},{1,0},{2,3},{3,2},{4,5},{5,4},{6,7},{7,6},{8,9},{9,8},{10,11... | collective-permute-start | bytes 1572872 | tf_op jit(solution)/shard_map/ppermute | solution.py:304
  34.0 0.0 copy-start
  34.0 3.5 %collective-permute-start.2 = (bf16[8,128,128]{2,1,0:T(8,128)(2,1)S(1)}, bf16[8,128,128]{2,1,0:T(8,128)(2,1)S(1)}, u32[]{:S(2)}, u32[]{:S(2)}) collective-permute-start(bf16[8,128,128]{2,1,0:T(8,128)(2,1)S(1)} %get-tuple-element.18), channel_id=1, source_target_pairs={{1,5},{4,0},{5,9},{8,4},{9,13},{12,8},{13,17},{16,12},{17,21},{20,... | collective-permute-start | bytes 786440 | tf_op jit(solution)/shard_map/ppermute | solution.py:304
  37.6 0.0 collective-permute-done.1.in_ref
  37.6 0.0 collective-permute-done.mate_ref
  37.6 0.0 copy-done
  37.6 5.5 %near.1 = (bf16[8,128,128]{2,1,0:T(8,128)(2,1)S(1)}, f32[48,128,128]{2,1,0:T(8,128)S(1)}) custom-call(s32[8,512]{1,0:T(8,128)S(1)} %bitcast.1, bf16[16,128,128]{2,1,0:T(8,128)(2,1)S(1)} %get-tuple-element.14.qg_ref, bf16[16,128,128]{2,1,0:T(8,128)(2,1)S(1)} %get-tuple-element.15.own_ref, bf16[16,128,128]{2,1,0:T(8,128)(2,1)S(1)} %collective-permute-done.mate_ref, ...), custom_call_target="tpu_custom_call" | custom-call | flops 1610612736 | bytes 1048576 | tf_op jit(solution)/shard_map/near/pallas_call | solution.py:370
  43.1 0.0 collective-permute-done.2.far_ref
  43.1 5.7 %far.1 = (bf16[8,128,128]{2,1,0:T(8,128)(2,1)S(1)}, f32[16,128,128]{2,1,0:T(8,128)S(1)}, bf16[16,128,128]{2,1,0:T(8,128)(2,1)S(1)}, bf16[16,128,128]{2,1,0:T(8,128)(2,1)S(1)}) custom-call(s32[8,512]{1,0:T(8,128)S(1)} %bitcast.2, bf16[16,128,128]{2,1,0:T(8,128)(2,1)S(1)} %get-tuple-element.14.qg_ref, bf16[16,128,128]{2,1,0:T(8,128)(2,1)S(1)} %get-tuple-element.15.own_ref, ...), custom_call_target="tpu_custom_call" | custom-call | flops 1610612736 | bytes 1048576 | tf_op jit(solution)/shard_map/far/pallas_call | solution.py:383
  48.8 1.9 %collective-permute-start.3 = (bf16[16,128,128]{2,1,0:T(8,128)(2,1)S(1)}, bf16[16,128,128]{2,1,0:T(8,128)(2,1)S(1)}, u32[]{:S(2)}, u32[]{:S(2)}) collective-permute-start(bf16[16,128,128]{2,1,0:T(8,128)(2,1)S(1)} %get-tuple-element.22), channel_id=1, source_target_pairs={{0,4},{4,8},{5,1},{8,12},{9,5},{12,16},{13,9},{16,20},{17,13},{20,... | collective-permute-start | bytes 1572872 | tf_op jit(solution)/shard_map/ppermute | solution.py:304
  50.7 4.0 %collective-permute-start.4 = (bf16[16,128,128]{2,1,0:T(8,128)(2,1)S(1)}, bf16[16,128,128]{2,1,0:T(8,128)(2,1)S(1)}, u32[]{:S(2)}, u32[]{:S(2)}) collective-permute-start(bf16[16,128,128]{2,1,0:T(8,128)(2,1)S(1)} %get-tuple-element.23), channel_id=1, source_target_pairs={{0,1},{1,0},{2,3},{3,2},{4,5},{5,4},{6,7},{7,6},{8,9},{9,8},{10,11... | collective-permute-start | bytes 1572872 | tf_op jit(solution)/shard_map/ppermute | solution.py:304
  54.8 5.2 %collective-permute-done.3.halo_ref = bf16[16,128,128]{2,1,0:T(8,128)(2,1)S(1)} collective-permute-done((bf16[16,128,128]{2,1,0:T(8,128)(2,1)S(1)}, bf16[16,128,128]{2,1,0:T(8,128)(2,1)S(1)}, u32[]{:S(2)}, u32[]{:S(2)}) %collective-permute-start.3) | collective-permute-done | bytes 524320 | tf_op jit(solution)/shard_map/ppermute | solution.py:304
  59.9 0.1 halo_total.1.own_ref
  60.0 0.0 collective-permute-done.4.mate_ref
  60.0 0.1 total.1
  60.2 21.1 %all_to_all.11.in_ref = bf16[32,128,128]{2,1,0:T(8,128)(2,1)S(1)} all-to-all(bf16[32,128,128]{2,1,0:T(8,128)(2,1)S(1)} %total.1), channel_id=1, replica_groups=mesh['x_lo'=2,'y'=4,'z'=16,'x_hi'=2,'core'=2] {'x_hi','core','x_lo','y'}, dimensions={0} | all-to-all | bytes 2097152 | tf_op jit(solution)/shard_map/all_to_all | solution.py:416
  81.3 1.3 %unpack.1 = (bf16[128,1024]{1,0:T(8,128)(2,1)}, bf16[128,1024]{1,0:T(8,128)(2,1)}, bf16[128,1024]{1,0:T(8,128)(2,1)}, bf16[128,1024]{1,0:T(8,128)(2,1)}) custom-call(bf16[32,128,128]{2,1,0:T(8,128)(2,1)S(1)} %all_to_all.11.in_ref), custom_call_target="tpu_custom_call" | custom-call | tf_op jit(solution)/shard_map/unpack/pallas_call | solution.py:418
  (1 shorter events, 0.0 us)
Async XLA Ops:
  27.3 10.3 %collective-permute-start.1 = (bf16[8,128,128]{2,1,0:T(8,128)(2,1)S(1)}, bf16[8,128,128]{2,1,0:T(8,128)(2,1)S(1)}, u32[]{:S(2)}, u32[]{:S(2)}) collective-permute-start(bf16[8,128,128]{2,1,0:T(8,128)(2,1)S(1)} %get-tuple-element.16), channel_id=1, source_target_pairs={{1,5},{4,0},{5,9},{8,4},{9,13},{12,8},{13,17},{16,12},{17,21},{20,... | collective-permute-start | bytes 786440 | tf_op jit(solution)/shard_map/ppermute | solution.py:304
  32.1 5.5 %collective-permute-start = (bf16[16,128,128]{2,1,0:T(8,128)(2,1)S(1)}, bf16[16,128,128]{2,1,0:T(8,128)(2,1)S(1)}, u32[]{:S(2)}, u32[]{:S(2)}) collective-permute-start(bf16[16,128,128]{2,1,0:T(8,128)(2,1)S(1)} %get-tuple-element.15.own_ref), channel_id=1, source_target_pairs={{0,1},{1,0},{2,3},{3,2},{4,5},{5,4},{6,7},{7,6},{8,9},{9,8},{10,11... | collective-permute-start | bytes 1572872 | tf_op jit(solution)/shard_map/ppermute | solution.py:304
  34.0 3.6 %copy-start = (s32[512,8]{0,1:T(8,128)S(1)}, s32[512,8]{0,1:T(8,128)}, u32[]{:S(2)}) copy-start(s32[512,8]{0,1:T(8,128)} %param.9) | copy-start | bytes 49156
  34.0 9.1 %collective-permute-start.2 = (bf16[8,128,128]{2,1,0:T(8,128)(2,1)S(1)}, bf16[8,128,128]{2,1,0:T(8,128)(2,1)S(1)}, u32[]{:S(2)}, u32[]{:S(2)}) collective-permute-start(bf16[8,128,128]{2,1,0:T(8,128)(2,1)S(1)} %get-tuple-element.18), channel_id=1, source_target_pairs={{1,5},{4,0},{5,9},{8,4},{9,13},{12,8},{13,17},{16,12},{17,21},{20,... | collective-permute-start | bytes 786440 | tf_op jit(solution)/shard_map/ppermute | solution.py:304
  48.8 11.1 %collective-permute-start.3 = (bf16[16,128,128]{2,1,0:T(8,128)(2,1)S(1)}, bf16[16,128,128]{2,1,0:T(8,128)(2,1)S(1)}, u32[]{:S(2)}, u32[]{:S(2)}) collective-permute-start(bf16[16,128,128]{2,1,0:T(8,128)(2,1)S(1)} %get-tuple-element.22), channel_id=1, source_target_pairs={{0,4},{4,8},{5,1},{8,12},{9,5},{12,16},{13,9},{16,20},{17,13},{20,... | collective-permute-start | bytes 1572872 | tf_op jit(solution)/shard_map/ppermute | solution.py:304
  50.7 9.3 %collective-permute-start.4 = (bf16[16,128,128]{2,1,0:T(8,128)(2,1)S(1)}, bf16[16,128,128]{2,1,0:T(8,128)(2,1)S(1)}, u32[]{:S(2)}, u32[]{:S(2)}) collective-permute-start(bf16[16,128,128]{2,1,0:T(8,128)(2,1)S(1)} %get-tuple-element.23), channel_id=1, source_target_pairs={{0,1},{1,0},{2,3},{3,2},{4,5},{5,4},{6,7},{7,6},{8,9},{9,8},{10,11... | collective-permute-start | bytes 1572872 | tf_op jit(solution)/shard_map/ppermute | solution.py:304

commit v9 on v8

--- a/solution.py
+++ b/solution.py
@@ -165,7 +165,6 @@
     window[HALF : 2 * HALF] = mate_ref[...]
     for side, halo_ref in zip((core, 1 - core), halo_refs):
         window[pl.ds(halo_at + side * QUARTER, QUARTER)] = halo_ref[...]
-    pair_odd[...] = jnp.zeros_like(pair_odd)
     copy.wait()
 
     def note(i, carry):
@@ -250,28 +249,17 @@
                 )
             yield
 
-    def beside(*stages):
+    both, pair = (both_even, both_odd), (pair_even, pair_odd)
+    for i in range(-1, QUARTER + 1):
+        stages = []
+        if i + 1 < QUARTER:
+            stages.append(products(i + 1, both[(i + 1) % 2]))
+        if 0 <= i < QUARTER:
+            stages.append(weigh(i, both[i % 2], pair[i % 2]))
+        if i > 0:
+            stages.append(results(i - 1, pair[(i - 1) % 2]))
         for _ in zip(*stages):
             pass
-
-    beside(products(0, both_even))
-
-    def step(j, carry):
-        even, odd = 2 * j, 2 * j + 1
-        beside(
-            products(odd, both_odd),
-            weigh(even, both_even, pair_even),
-            results(jnp.maximum(even - 1, 0), pair_odd),
-        )
-        beside(
-            products(jnp.minimum(even + 2, QUARTER - 1), both_even),
-            weigh(odd, both_odd, pair_odd),
-            results(even, pair_even),
-        )
-        return carry
-
-    lax.fori_loop(0, QUARTER // 2, step, 0)
-    beside(results(QUARTER - 1, pair_odd))
 
 
 def halo_sum_kernel(own_ref, halo_ref, out_ref):

time: 83.1 us -> 82.3 us (level)
  the two profiles are of different devices: /device:TPU:97 before, /device:TPU:225 now
where the time goes in v9:
time: 82.3 us; the launch traced here: 81.9 us
  blocking collectives  46.9 us (57%)
  starting transfers between devices  16.1 us (20%)
  Pallas kernels  13.7 us (17%)
  waiting for transfers between devices  4.35 us (5%)
    all_to_all x1, blocking collectives, per_device(): received = lax.all_to_all(packed, AXES, 0, 0, tiled=True)  24.1 us
    all_to_all x1, blocking collectives, per_device(): returned = lax.all_to_all(outgoing, AXES, 0, 0, tiled=True)  22.8 us
    ppermute x5, starting transfers between devices, moved(): return lax.ppermute(value, axes, pairs)  16.1 us
    pallas_call x1, Pallas kernels, per_device(): pl.pallas_call(far_kernel, out_shape=[jax.ShapeDtypeStruct(quarter, jnp.b...  4.93 us
    pallas_call x1, Pallas kernels, per_device(): pl.pallas_call(near_kernel, out_shape=[jax.ShapeDtypeStruct(quarter, jnp....  4.67 us
    ppermute x5, waiting for transfers between devices, moved(): return lax.ppermute(value, axes, pairs)  4.35 us
    pallas_call x1, Pallas kernels, per_device(): pl.pallas_call(pack_kernel, out_shape=plane, in_specs=[ANY] * 4, out_spec...  2.44 us
  transfers between devices with their start and end apart: 5, of which 1 were waited for; matrix products, arithmetic and copies ran while one was open for 0% of the time, Pallas kernels for 6%

profile of v9, /device:TPU:225, one launch (start us, length us, event | category | flops | bytes accessed | tf_op | source)
XLA Modules:
  0.0 81.9 jit_solution(3987963884012231270)
XLA Ops:
  0.6 2.4 %pack.1 = bf16[32,128,128]{2,1,0:T(8,128)(2,1)} custom-call(bf16[128,1024]{1,0:T(8,128)(2,1)} %q_hbm.1, bf16[128,1024]{1,0:T(8,128)(2,1)} %k_hbm.1, bf16[128,1024]{1,0:T(8,128)(2,1)} %v_hbm.1, bf16[128,1024]{1,0:T(8,128)(2,1)} %g_hbm.1), custom_call_target="tpu_custom_call" | custom-call | tf_op jit(solution)/shard_map/pack/pallas_call | solution.py:301
  3.1 24.1 %all_to_all.10.in_ref = bf16[32,128,128]{2,1,0:T(8,128)(2,1)S(1)} all-to-all(bf16[32,128,128]{2,1,0:T(8,128)(2,1)} %pack.1), channel_id=1, replica_groups=mesh['x_lo'=2,'y'=4,'z'=16,'x_hi'=2,'core'=2] {'x_hi','core','x_lo','y'}, dimensions={0} | all-to-all | bytes 2097152 | tf_op jit(solution)/shard_map/all_to_all | solution.py:315
  27.2 0.1 split.1
  27.3 4.8 %collective-permute-start.1 = (bf16[8,128,128]{2,1,0:T(8,128)(2,1)S(1)}, bf16[8,128,128]{2,1,0:T(8,128)(2,1)S(1)}, u32[]{:S(2)}, u32[]{:S(2)}) collective-permute-start(bf16[8,128,128]{2,1,0:T(8,128)(2,1)S(1)} %get-tuple-element.16), channel_id=1, source_target_pairs={{1,5},{4,0},{5,9},{8,4},{9,13},{12,8},{13,17},{16,12},{17,21},{20,... | collective-permute-start | bytes 786440 | tf_op jit(solution)/shard_map/ppermute | solution.py:292
  32.1 1.9 %collective-permute-start = (bf16[16,128,128]{2,1,0:T(8,128)(2,1)S(1)}, bf16[16,128,128]{2,1,0:T(8,128)(2,1)S(1)}, u32[]{:S(2)}, u32[]{:S(2)}) collective-permute-start(bf16[16,128,128]{2,1,0:T(8,128)(2,1)S(1)} %get-tuple-element.15.own_ref), channel_id=1, source_target_pairs={{0,1},{1,0},{2,3},{3,2},{4,5},{5,4},{6,7},{7,6},{8,9},{9,8},{10,11... | collective-permute-start | bytes 1572872 | tf_op jit(solution)/shard_map/ppermute | solution.py:292
  34.0 0.0 copy-start
  34.0 2.6 %collective-permute-start.2 = (bf16[8,128,128]{2,1,0:T(8,128)(2,1)S(1)}, bf16[8,128,128]{2,1,0:T(8,128)(2,1)S(1)}, u32[]{:S(2)}, u32[]{:S(2)}) collective-permute-start(bf16[8,128,128]{2,1,0:T(8,128)(2,1)S(1)} %get-tuple-element.18), channel_id=1, source_target_pairs={{1,5},{4,0},{5,9},{8,4},{9,13},{12,8},{13,17},{16,12},{17,21},{20,... | collective-permute-start | bytes 786440 | tf_op jit(solution)/shard_map/ppermute | solution.py:292
  36.7 0.0 collective-permute-done.1.in_ref
  36.7 0.0 collective-permute-done.mate_ref
  36.7 0.0 copy-done
  36.7 4.7 %near.1 = (bf16[8,128,128]{2,1,0:T(8,128)(2,1)S(1)}, f32[48,128,128]{2,1,0:T(8,128)S(1)}) custom-call(s32[8,512]{1,0:T(8,128)S(1)} %bitcast.1, bf16[16,128,128]{2,1,0:T(8,128)(2,1)S(1)} %get-tuple-element.14.qg_ref, bf16[16,128,128]{2,1,0:T(8,128)(2,1)S(1)} %get-tuple-element.15.own_ref, bf16[16,128,128]{2,1,0:T(8,128)(2,1)S(1)} %collective-permute-done.mate_ref, ...), custom_call_target="tpu_custom_call" | custom-call | flops 1610612736 | bytes 1048576 | tf_op jit(solution)/shard_map/near/pallas_call | solution.py:358
  41.4 0.0 collective-permute-done.2.far_ref
  41.4 4.9 %far.1 = (bf16[8,128,128]{2,1,0:T(8,128)(2,1)S(1)}, f32[16,128,128]{2,1,0:T(8,128)S(1)}, bf16[16,128,128]{2,1,0:T(8,128)(2,1)S(1)}, bf16[16,128,128]{2,1,0:T(8,128)(2,1)S(1)}) custom-call(s32[8,512]{1,0:T(8,128)S(1)} %bitcast.2, bf16[16,128,128]{2,1,0:T(8,128)(2,1)S(1)} %get-tuple-element.14.qg_ref, bf16[16,128,128]{2,1,0:T(8,128)(2,1)S(1)} %get-tuple-element.15.own_ref, ...), custom_call_target="tpu_custom_call" | custom-call | flops 1610612736 | bytes 1048576 | tf_op jit(solution)/shard_map/far/pallas_call | solution.py:371
  46.4 2.6 %collective-permute-start.3 = (bf16[16,128,128]{2,1,0:T(8,128)(2,1)S(1)}, bf16[16,128,128]{2,1,0:T(8,128)(2,1)S(1)}, u32[]{:S(2)}, u32[]{:S(2)}) collective-permute-start(bf16[16,128,128]{2,1,0:T(8,128)(2,1)S(1)} %get-tuple-element.22), channel_id=1, source_target_pairs={{0,4},{4,8},{5,1},{8,12},{9,5},{12,16},{13,9},{16,20},{17,13},{20,... | collective-permute-start | bytes 1572872 | tf_op jit(solution)/shard_map/ppermute | solution.py:292
  49.0 4.2 %collective-permute-start.4 = (bf16[16,128,128]{2,1,0:T(8,128)(2,1)S(1)}, bf16[16,128,128]{2,1,0:T(8,128)(2,1)S(1)}, u32[]{:S(2)}, u32[]{:S(2)}) collective-permute-start(bf16[16,128,128]{2,1,0:T(8,128)(2,1)S(1)} %get-tuple-element.23), channel_id=1, source_target_pairs={{0,1},{1,0},{2,3},{3,2},{4,5},{5,4},{6,7},{7,6},{8,9},{9,8},{10,11... | collective-permute-start | bytes 1572872 | tf_op jit(solution)/shard_map/ppermute | solution.py:292
  53.2 4.3 %collective-permute-done.3.halo_ref = bf16[16,128,128]{2,1,0:T(8,128)(2,1)S(1)} collective-permute-done((bf16[16,128,128]{2,1,0:T(8,128)(2,1)S(1)}, bf16[16,128,128]{2,1,0:T(8,128)(2,1)S(1)}, u32[]{:S(2)}, u32[]{:S(2)}) %collective-permute-start.3) | collective-permute-done | bytes 524320 | tf_op jit(solution)/shard_map/ppermute | solution.py:292
  57.5 0.1 halo_total.1.own_ref
  57.6 0.0 collective-permute-done.4.mate_ref
  57.6 0.1 total.1
  57.7 22.8 %all_to_all.11.in_ref = bf16[32,128,128]{2,1,0:T(8,128)(2,1)S(1)} all-to-all(bf16[32,128,128]{2,1,0:T(8,128)(2,1)S(1)} %total.1), channel_id=1, replica_groups=mesh['x_lo'=2,'y'=4,'z'=16,'x_hi'=2,'core'=2] {'x_hi','core','x_lo','y'}, dimensions={0} | all-to-all | bytes 2097152 | tf_op jit(solution)/shard_map/all_to_all | solution.py:404
  80.5 1.3 %unpack.1 = (bf16[128,1024]{1,0:T(8,128)(2,1)}, bf16[128,1024]{1,0:T(8,128)(2,1)}, bf16[128,1024]{1,0:T(8,128)(2,1)}, bf16[128,1024]{1,0:T(8,128)(2,1)}) custom-call(bf16[32,128,128]{2,1,0:T(8,128)(2,1)S(1)} %all_to_all.11.in_ref), custom_call_target="tpu_custom_call" | custom-call | tf_op jit(solution)/shard_map/unpack/pallas_call | solution.py:406
  (1 shorter events, 0.0 us)
Async XLA Ops:
  27.3 9.4 %collective-permute-start.1 = (bf16[8,128,128]{2,1,0:T(8,128)(2,1)S(1)}, bf16[8,128,128]{2,1,0:T(8,128)(2,1)S(1)}, u32[]{:S(2)}, u32[]{:S(2)}) collective-permute-start(bf16[8,128,128]{2,1,0:T(8,128)(2,1)S(1)} %get-tuple-element.16), channel_id=1, source_target_pairs={{1,5},{4,0},{5,9},{8,4},{9,13},{12,8},{13,17},{16,12},{17,21},{20,... | collective-permute-start | bytes 786440 | tf_op jit(solution)/shard_map/ppermute | solution.py:292
  32.1 4.6 %collective-permute-start = (bf16[16,128,128]{2,1,0:T(8,128)(2,1)S(1)}, bf16[16,128,128]{2,1,0:T(8,128)(2,1)S(1)}, u32[]{:S(2)}, u32[]{:S(2)}) collective-permute-start(bf16[16,128,128]{2,1,0:T(8,128)(2,1)S(1)} %get-tuple-element.15.own_ref), channel_id=1, source_target_pairs={{0,1},{1,0},{2,3},{3,2},{4,5},{5,4},{6,7},{7,6},{8,9},{9,8},{10,11... | collective-permute-start | bytes 1572872 | tf_op jit(solution)/shard_map/ppermute | solution.py:292
  34.0 2.7 %copy-start = (s32[512,8]{0,1:T(8,128)S(1)}, s32[512,8]{0,1:T(8,128)}, u32[]{:S(2)}) copy-start(s32[512,8]{0,1:T(8,128)} %param.9) | copy-start | bytes 49156
  34.0 7.4 %collective-permute-start.2 = (bf16[8,128,128]{2,1,0:T(8,128)(2,1)S(1)}, bf16[8,128,128]{2,1,0:T(8,128)(2,1)S(1)}, u32[]{:S(2)}, u32[]{:S(2)}) collective-permute-start(bf16[8,128,128]{2,1,0:T(8,128)(2,1)S(1)} %get-tuple-element.18), channel_id=1, source_target_pairs={{1,5},{4,0},{5,9},{8,4},{9,13},{12,8},{13,17},{16,12},{17,21},{20,... | collective-permute-start | bytes 786440 | tf_op jit(solution)/shard_map/ppermute | solution.py:292
  46.4 11.1 %collective-permute-start.3 = (bf16[16,128,128]{2,1,0:T(8,128)(2,1)S(1)}, bf16[16,128,128]{2,1,0:T(8,128)(2,1)S(1)}, u32[]{:S(2)}, u32[]{:S(2)}) collective-permute-start(bf16[16,128,128]{2,1,0:T(8,128)(2,1)S(1)} %get-tuple-element.22), channel_id=1, source_target_pairs={{0,4},{4,8},{5,1},{8,12},{9,5},{12,16},{13,9},{16,20},{17,13},{20,... | collective-permute-start | bytes 1572872 | tf_op jit(solution)/shard_map/ppermute | solution.py:292
  49.0 8.6 %collective-permute-start.4 = (bf16[16,128,128]{2,1,0:T(8,128)(2,1)S(1)}, bf16[16,128,128]{2,1,0:T(8,128)(2,1)S(1)}, u32[]{:S(2)}, u32[]{:S(2)}) collective-permute-start(bf16[16,128,128]{2,1,0:T(8,128)(2,1)S(1)} %get-tuple-element.23), channel_id=1, source_target_pairs={{0,1},{1,0},{2,3},{3,2},{4,5},{5,4},{6,7},{7,6},{8,9},{9,8},{10,11... | collective-permute-start | bytes 1572872 | tf_op jit(solution)/shard_map/ppermute | solution.py:292

commit v10 on v9

--- a/solution.py
+++ b/solution.py
@@ -89,24 +89,22 @@
 ):
     x_hi = lax.axis_index("x_hi")
     copies = []
-    for pair in range(HEADS // 2):
-        columns = slice(pair * WIDTH, (pair + 1) * WIDTH)
-        even, odd = 2 * pair, 2 * pair + 1
-        kv0, kv1 = in_ref[slot_of(even, x_hi)], in_ref[slot_of(odd, x_hi)]
-        qo0, qo1 = in_ref[slot_of(even, 1 - x_hi)], in_ref[slot_of(odd, 1 - x_hi)]
-        dk_ref[:, columns] = turned_pair(kv0, kv1, 0)
-        dv_ref[:, columns] = turned_pair(kv0, kv1, 1)
-        dq_ref[:, columns] = lane_pair(qo0, qo1, 0)
-        o_ref[:, columns] = lane_pair(qo0, qo1, 1)
-        if (pair + 1) * WIDTH % PART == 0:
-            p = pair * WIDTH // PART
-            part = slice(p * PART, (p + 1) * PART)
-            for n, (source, target) in enumerate(
-                ((o_ref, o_hbm), (dq_ref, dq_hbm), (dk_ref, dk_hbm), (dv_ref, dv_hbm))
-            ):
-                copy = pltpu.make_async_copy(source.at[:, part], target.at[:, part], sems.at[p, n])
-                copy.start()
-                copies.append(copy)
+    for n, (ref, hbm, core, odd, joined) in enumerate(
+        (
+            (dk_ref, dk_hbm, x_hi, 0, turned_pair),
+            (dv_ref, dv_hbm, x_hi, 1, turned_pair),
+            (dq_ref, dq_hbm, 1 - x_hi, 0, lane_pair),
+            (o_ref, o_hbm, 1 - x_hi, 1, lane_pair),
+        )
+    ):
+        for pair in range(HEADS // 2):
+            columns = slice(pair * WIDTH, (pair + 1) * WIDTH)
+            ref[:, columns] = joined(
+                in_ref[slot_of(2 * pair, core)], in_ref[slot_of(2 * pair + 1, core)], odd
+            )
+        copy = pltpu.make_async_copy(ref, hbm, sems.at[n])
+        copy.start()
+        copies.append(copy)
     for copy in copies:
         copy.wait()
 
@@ -167,14 +165,11 @@
         window[pl.ds(halo_at + side * QUARTER, QUARTER)] = halo_ref[...]
     copy.wait()
 
-    def note(i, carry):
+    for i in range(QUARTER):
         for s in range(SLOTS):
             block = listed[s, first_query - at + i]
             dead = (block == first_query + i) if s else False
             table[i, s] = jnp.where(dead, -1, block - first_key)
-        return carry
-
-    lax.fori_loop(0, QUARTER, note, 0)
 
     def blocks_of(i):
         return [
@@ -409,7 +404,7 @@
         in_specs=[VMEM],
         out_specs=[ANY] * 4,
         scratch_shapes=[pltpu.VMEM(queries.shape, jnp.bfloat16)] * 4
-        + [pltpu.SemaphoreType.DMA((PARTS, 4))],
+        + [pltpu.SemaphoreType.DMA((4,))],
         compiler_params=PARAMS,
         name="unpack",
     )(returned)

time: 82.3 us -> 81.9 us (level)
  transfers between devices with their start and end apart: 5 -> 5, of which waited for: 1 -> 2; matrix products, arithmetic and copies ran while one was open for 0% -> 0% of each run, Pallas kernels for 6% -> 6%
where the time goes in v10:
time: 81.9 us; the launch traced here: 81.5 us
  blocking collectives  46.9 us (57%)
  starting transfers between devices  16 us (20%)
  Pallas kernels  13.2 us (16%)
  waiting for transfers between devices  4.62 us (6%)
    all_to_all x1, blocking collectives, per_device(): received = lax.all_to_all(packed, AXES, 0, 0, tiled=True)  24.1 us
    all_to_all x1, blocking collectives, per_device(): returned = lax.all_to_all(outgoing, AXES, 0, 0, tiled=True)  22.8 us
    ppermute x5, starting transfers between devices, moved(): return lax.ppermute(value, axes, pairs)  16 us
    pallas_call x1, Pallas kernels, per_device(): pl.pallas_call(far_kernel, out_shape=[jax.ShapeDtypeStruct(quarter, jnp.b...  4.78 us
    ppermute x5, waiting for transfers between devices, moved(): return lax.ppermute(value, axes, pairs)  4.62 us
    pallas_call x1, Pallas kernels, per_device(): pl.pallas_call(near_kernel, out_shape=[jax.ShapeDtypeStruct(quarter, jnp....  4.53 us
    pallas_call x1, Pallas kernels, per_device(): pl.pallas_call(pack_kernel, out_shape=plane, in_specs=[ANY] * 4, out_spec...  2.44 us
  transfers between devices with their start and end apart: 5, of which 2 were waited for; matrix products, arithmetic and copies ran while one was open for 0% of the time, Pallas kernels for 6%

profile of v10, /device:TPU:225, one launch (start us, length us, event | category | flops | bytes accessed | tf_op | source)
XLA Modules:
  0.0 81.5 jit_solution(9966672475106226113)
XLA Ops:
  0.6 2.4 %pack.1 = bf16[32,128,128]{2,1,0:T(8,128)(2,1)} custom-call(bf16[128,1024]{1,0:T(8,128)(2,1)} %q_hbm.1, bf16[128,1024]{1,0:T(8,128)(2,1)} %k_hbm.1, bf16[128,1024]{1,0:T(8,128)(2,1)} %v_hbm.1, bf16[128,1024]{1,0:T(8,128)(2,1)} %g_hbm.1), custom_call_target="tpu_custom_call" | custom-call | tf_op jit(solution)/shard_map/pack/pallas_call | solution.py:296
  3.1 24.1 %all_to_all.10.in_ref = bf16[32,128,128]{2,1,0:T(8,128)(2,1)S(1)} all-to-all(bf16[32,128,128]{2,1,0:T(8,128)(2,1)} %pack.1), channel_id=1, replica_groups=mesh['x_lo'=2,'y'=4,'z'=16,'x_hi'=2,'core'=2] {'x_hi','core','x_lo','y'}, dimensions={0} | all-to-all | bytes 2097152 | tf_op jit(solution)/shard_map/all_to_all | solution.py:310
  27.2 0.1 split.1
  27.3 4.8 %collective-permute-start.1 = (bf16[8,128,128]{2,1,0:T(8,128)(2,1)S(1)}, bf16[8,128,128]{2,1,0:T(8,128)(2,1)S(1)}, u32[]{:S(2)}, u32[]{:S(2)}) collective-permute-start(bf16[8,128,128]{2,1,0:T(8,128)(2,1)S(1)} %get-tuple-element.16), channel_id=1, source_target_pairs={{1,5},{4,0},{5,9},{8,4},{9,13},{12,8},{13,17},{16,12},{17,21},{20,... | collective-permute-start | bytes 786440 | tf_op jit(solution)/shard_map/ppermute | solution.py:287
  32.1 1.9 %collective-permute-start = (bf16[16,128,128]{2,1,0:T(8,128)(2,1)S(1)}, bf16[16,128,128]{2,1,0:T(8,128)(2,1)S(1)}, u32[]{:S(2)}, u32[]{:S(2)}) collective-permute-start(bf16[16,128,128]{2,1,0:T(8,128)(2,1)S(1)} %get-tuple-element.15.own_ref), channel_id=1, source_target_pairs={{0,1},{1,0},{2,3},{3,2},{4,5},{5,4},{6,7},{7,6},{8,9},{9,8},{10,11... | collective-permute-start | bytes 1572872 | tf_op jit(solution)/shard_map/ppermute | solution.py:287
  34.0 0.0 copy-start
  34.0 2.6 %collective-permute-start.2 = (bf16[8,128,128]{2,1,0:T(8,128)(2,1)S(1)}, bf16[8,128,128]{2,1,0:T(8,128)(2,1)S(1)}, u32[]{:S(2)}, u32[]{:S(2)}) collective-permute-start(bf16[8,128,128]{2,1,0:T(8,128)(2,1)S(1)} %get-tuple-element.18), channel_id=1, source_target_pairs={{1,5},{4,0},{5,9},{8,4},{9,13},{12,8},{13,17},{16,12},{17,21},{20,... | collective-permute-start | bytes 786440 | tf_op jit(solution)/shard_map/ppermute | solution.py:287
  36.7 0.0 collective-permute-done.1.in_ref
  36.7 0.0 collective-permute-done.mate_ref
  36.7 0.0 copy-done
  36.7 4.5 %near.1 = (bf16[8,128,128]{2,1,0:T(8,128)(2,1)S(1)}, f32[48,128,128]{2,1,0:T(8,128)S(1)}) custom-call(s32[8,512]{1,0:T(8,128)S(1)} %bitcast.1, bf16[16,128,128]{2,1,0:T(8,128)(2,1)S(1)} %get-tuple-element.14.qg_ref, bf16[16,128,128]{2,1,0:T(8,128)(2,1)S(1)} %get-tuple-element.15.own_ref, bf16[16,128,128]{2,1,0:T(8,128)(2,1)S(1)} %collective-permute-done.mate_ref, ...), custom_call_target="tpu_custom_call" | custom-call | flops 1610612736 | bytes 1048576 | tf_op jit(solution)/shard_map/near/pallas_call | solution.py:353
  41.3 0.2 collective-permute-done.2.far_ref
  41.4 4.8 %far.1 = (bf16[8,128,128]{2,1,0:T(8,128)(2,1)S(1)}, f32[16,128,128]{2,1,0:T(8,128)S(1)}, bf16[16,128,128]{2,1,0:T(8,128)(2,1)S(1)}, bf16[16,128,128]{2,1,0:T(8,128)(2,1)S(1)}) custom-call(s32[8,512]{1,0:T(8,128)S(1)} %bitcast.2, bf16[16,128,128]{2,1,0:T(8,128)(2,1)S(1)} %get-tuple-element.14.qg_ref, bf16[16,128,128]{2,1,0:T(8,128)(2,1)S(1)} %get-tuple-element.15.own_ref, ...), custom_call_target="tpu_custom_call" | custom-call | flops 1610612736 | bytes 1048576 | tf_op jit(solution)/shard_map/far/pallas_call | solution.py:366
  46.2 2.5 %collective-permute-start.3 = (bf16[16,128,128]{2,1,0:T(8,128)(2,1)S(1)}, bf16[16,128,128]{2,1,0:T(8,128)(2,1)S(1)}, u32[]{:S(2)}, u32[]{:S(2)}) collective-permute-start(bf16[16,128,128]{2,1,0:T(8,128)(2,1)S(1)} %get-tuple-element.22), channel_id=1, source_target_pairs={{0,4},{4,8},{5,1},{8,12},{9,5},{12,16},{13,9},{16,20},{17,13},{20,... | collective-permute-start | bytes 1572872 | tf_op jit(solution)/shard_map/ppermute | solution.py:287
  48.7 4.2 %collective-permute-start.4 = (bf16[16,128,128]{2,1,0:T(8,128)(2,1)S(1)}, bf16[16,128,128]{2,1,0:T(8,128)(2,1)S(1)}, u32[]{:S(2)}, u32[]{:S(2)}) collective-permute-start(bf16[16,128,128]{2,1,0:T(8,128)(2,1)S(1)} %get-tuple-element.23), channel_id=1, source_target_pairs={{0,1},{1,0},{2,3},{3,2},{4,5},{5,4},{6,7},{7,6},{8,9},{9,8},{10,11... | collective-permute-start | bytes 1572872 | tf_op jit(solution)/shard_map/ppermute | solution.py:287
  52.9 4.5 %collective-permute-done.3.halo_ref = bf16[16,128,128]{2,1,0:T(8,128)(2,1)S(1)} collective-permute-done((bf16[16,128,128]{2,1,0:T(8,128)(2,1)S(1)}, bf16[16,128,128]{2,1,0:T(8,128)(2,1)S(1)}, u32[]{:S(2)}, u32[]{:S(2)}) %collective-permute-start.3) | collective-permute-done | bytes 524320 | tf_op jit(solution)/shard_map/ppermute | solution.py:287
  57.3 0.1 halo_total.1.own_ref
  57.4 0.0 collective-permute-done.4.mate_ref
  57.4 0.1 total.1
  57.6 22.8 %all_to_all.11.in_ref = bf16[32,128,128]{2,1,0:T(8,128)(2,1)S(1)} all-to-all(bf16[32,128,128]{2,1,0:T(8,128)(2,1)S(1)} %total.1), channel_id=1, replica_groups=mesh['x_lo'=2,'y'=4,'z'=16,'x_hi'=2,'core'=2] {'x_hi','core','x_lo','y'}, dimensions={0} | all-to-all | bytes 2097152 | tf_op jit(solution)/shard_map/all_to_all | solution.py:399
  80.4 1.1 %unpack.1 = (bf16[128,1024]{1,0:T(8,128)(2,1)}, bf16[128,1024]{1,0:T(8,128)(2,1)}, bf16[128,1024]{1,0:T(8,128)(2,1)}, bf16[128,1024]{1,0:T(8,128)(2,1)}) custom-call(bf16[32,128,128]{2,1,0:T(8,128)(2,1)S(1)} %all_to_all.11.in_ref), custom_call_target="tpu_custom_call" | custom-call | tf_op jit(solution)/shard_map/unpack/pallas_call | solution.py:401
  (1 shorter events, 0.0 us)
Async XLA Ops:
  27.3 9.4 %collective-permute-start.1 = (bf16[8,128,128]{2,1,0:T(8,128)(2,1)S(1)}, bf16[8,128,128]{2,1,0:T(8,128)(2,1)S(1)}, u32[]{:S(2)}, u32[]{:S(2)}) collective-permute-start(bf16[8,128,128]{2,1,0:T(8,128)(2,1)S(1)} %get-tuple-element.16), channel_id=1, source_target_pairs={{1,5},{4,0},{5,9},{8,4},{9,13},{12,8},{13,17},{16,12},{17,21},{20,... | collective-permute-start | bytes 786440 | tf_op jit(solution)/shard_map/ppermute | solution.py:287
  32.1 4.6 %collective-permute-start = (bf16[16,128,128]{2,1,0:T(8,128)(2,1)S(1)}, bf16[16,128,128]{2,1,0:T(8,128)(2,1)S(1)}, u32[]{:S(2)}, u32[]{:S(2)}) collective-permute-start(bf16[16,128,128]{2,1,0:T(8,128)(2,1)S(1)} %get-tuple-element.15.own_ref), channel_id=1, source_target_pairs={{0,1},{1,0},{2,3},{3,2},{4,5},{5,4},{6,7},{7,6},{8,9},{9,8},{10,11... | collective-permute-start | bytes 1572872 | tf_op jit(solution)/shard_map/ppermute | solution.py:287
  34.0 2.7 %copy-start = (s32[512,8]{0,1:T(8,128)S(1)}, s32[512,8]{0,1:T(8,128)}, u32[]{:S(2)}) copy-start(s32[512,8]{0,1:T(8,128)} %param.9) | copy-start | bytes 49156
  34.0 7.4 %collective-permute-start.2 = (bf16[8,128,128]{2,1,0:T(8,128)(2,1)S(1)}, bf16[8,128,128]{2,1,0:T(8,128)(2,1)S(1)}, u32[]{:S(2)}, u32[]{:S(2)}) collective-permute-start(bf16[8,128,128]{2,1,0:T(8,128)(2,1)S(1)} %get-tuple-element.18), channel_id=1, source_target_pairs={{1,5},{4,0},{5,9},{8,4},{9,13},{12,8},{13,17},{16,12},{17,21},{20,... | collective-permute-start | bytes 786440 | tf_op jit(solution)/shard_map/ppermute | solution.py:287
  46.2 11.1 %collective-permute-start.3 = (bf16[16,128,128]{2,1,0:T(8,128)(2,1)S(1)}, bf16[16,128,128]{2,1,0:T(8,128)(2,1)S(1)}, u32[]{:S(2)}, u32[]{:S(2)}) collective-permute-start(bf16[16,128,128]{2,1,0:T(8,128)(2,1)S(1)} %get-tuple-element.22), channel_id=1, source_target_pairs={{0,4},{4,8},{5,1},{8,12},{9,5},{12,16},{13,9},{16,20},{17,13},{20,... | collective-permute-start | bytes 1572872 | tf_op jit(solution)/shard_map/ppermute | solution.py:287
  48.7 8.7 %collective-permute-start.4 = (bf16[16,128,128]{2,1,0:T(8,128)(2,1)S(1)}, bf16[16,128,128]{2,1,0:T(8,128)(2,1)S(1)}, u32[]{:S(2)}, u32[]{:S(2)}) collective-permute-start(bf16[16,128,128]{2,1,0:T(8,128)(2,1)S(1)} %get-tuple-element.23), channel_id=1, source_target_pairs={{0,1},{1,0},{2,3},{3,2},{4,5},{5,4},{6,7},{7,6},{8,9},{9,8},{10,11... | collective-permute-start | bytes 1572872 | tf_op jit(solution)/shard_map/ppermute | solution.py:287

commit v11 on v9

--- a/solution.py
+++ b/solution.py
@@ -335,7 +335,7 @@
         in_specs=[VMEM],
         out_specs=VMEM,
         compiler_params=PARAMS,
-        cost_estimate=pl.CostEstimate(flops=1 << 32, bytes_accessed=1 << 20, transcendentals=0),
+        cost_estimate=pl.CostEstimate(flops=1 << 33, bytes_accessed=1 << 20, transcendentals=0),
         name="near_copy",
     )(inward(near_part))
     mate = to_mate(key_value)

time: 82.3 us -> 82.8 us (level)
  the two profiles are of different devices: /device:TPU:225 before, /device:TPU:1 now
where the time goes in v11:
time: 82.8 us; the launch traced here: 81.2 us
  blocking collectives  47.8 us (58%)
  Pallas kernels  13.7 us (17%)
  starting transfers between devices  12.9 us (16%)
  waiting for transfers between devices  6.04 us (7%)
    all_to_all x1, blocking collectives, per_device(): received = lax.all_to_all(packed, AXES, 0, 0, tiled=True)  26.9 us
    all_to_all x1, blocking collectives, per_device(): returned = lax.all_to_all(outgoing, AXES, 0, 0, tiled=True)  20.8 us
    ppermute x5, starting transfers between devices, moved(): return lax.ppermute(value, axes, pairs)  12.9 us
    ppermute x5, waiting for transfers between devices, moved(): return lax.ppermute(value, axes, pairs)  6.04 us
    pallas_call x1, Pallas kernels, per_device(): pl.pallas_call(far_kernel, out_shape=[jax.ShapeDtypeStruct(quarter, jnp.b...  4.93 us
    pallas_call x1, Pallas kernels, per_device(): pl.pallas_call(near_kernel, out_shape=[jax.ShapeDtypeStruct(quarter, jnp....  4.67 us
    pallas_call x1, Pallas kernels, per_device(): pl.pallas_call(pack_kernel, out_shape=plane, in_specs=[ANY] * 4, out_spec...  2.44 us
  transfers between devices with their start and end apart: 5, of which 2 were waited for; matrix products, arithmetic and copies ran while one was open for 0% of the time, Pallas kernels for 6%

profile of v11, /device:TPU:1, one launch (start us, length us, event | category | flops | bytes accessed | tf_op | source)
XLA Modules:
  0.0 81.2 jit_solution(14483093215997675158)
XLA Ops:
  0.6 2.4 %pack.1 = bf16[32,128,128]{2,1,0:T(8,128)(2,1)} custom-call(bf16[128,1024]{1,0:T(8,128)(2,1)} %q_hbm.1, bf16[128,1024]{1,0:T(8,128)(2,1)} %k_hbm.1, bf16[128,1024]{1,0:T(8,128)(2,1)} %v_hbm.1, bf16[128,1024]{1,0:T(8,128)(2,1)} %g_hbm.1), custom_call_target="tpu_custom_call" | custom-call | tf_op jit(solution)/shard_map/pack/pallas_call | solution.py:301
  3.1 26.9 %all_to_all.10.in_ref = bf16[32,128,128]{2,1,0:T(8,128)(2,1)S(1)} all-to-all(bf16[32,128,128]{2,1,0:T(8,128)(2,1)} %pack.1), channel_id=1, replica_groups=mesh['x_lo'=2,'y'=4,'z'=16,'x_hi'=2,'core'=2] {'x_hi','core','x_lo','y'}, dimensions={0} | all-to-all | bytes 2097152 | tf_op jit(solution)/shard_map/all_to_all | solution.py:315
  30.0 0.1 split.1
  30.1 1.6 %collective-permute-start.1 = (bf16[8,128,128]{2,1,0:T(8,128)(2,1)S(1)}, bf16[8,128,128]{2,1,0:T(8,128)(2,1)S(1)}, u32[]{:S(2)}, u32[]{:S(2)}) collective-permute-start(bf16[8,128,128]{2,1,0:T(8,128)(2,1)S(1)} %get-tuple-element.16), channel_id=1, source_target_pairs={{1,5},{4,0},{5,9},{8,4},{9,13},{12,8},{13,17},{16,12},{17,21},{20,... | collective-permute-start | bytes 786440 | tf_op jit(solution)/shard_map/ppermute | solution.py:292
  31.7 3.5 %collective-permute-start.2 = (bf16[8,128,128]{2,1,0:T(8,128)(2,1)S(1)}, bf16[8,128,128]{2,1,0:T(8,128)(2,1)S(1)}, u32[]{:S(2)}, u32[]{:S(2)}) collective-permute-start(bf16[8,128,128]{2,1,0:T(8,128)(2,1)S(1)} %get-tuple-element.18), channel_id=1, source_target_pairs={{1,5},{4,0},{5,9},{8,4},{9,13},{12,8},{13,17},{16,12},{17,21},{20,... | collective-permute-start | bytes 786440 | tf_op jit(solution)/shard_map/ppermute | solution.py:292
  35.3 0.0 copy-start
  35.3 1.9 %collective-permute-start = (bf16[16,128,128]{2,1,0:T(8,128)(2,1)S(1)}, bf16[16,128,128]{2,1,0:T(8,128)(2,1)S(1)}, u32[]{:S(2)}, u32[]{:S(2)}) collective-permute-start(bf16[16,128,128]{2,1,0:T(8,128)(2,1)S(1)} %get-tuple-element.15.own_ref), channel_id=1, source_target_pairs={{0,1},{1,0},{2,3},{3,2},{4,5},{5,4},{6,7},{7,6},{8,9},{9,8},{10,11... | collective-permute-start | bytes 1572872 | tf_op jit(solution)/shard_map/ppermute | solution.py:292
  37.2 0.0 collective-permute-done.1.in_ref
  37.2 1.8 %collective-permute-done.mate_ref = bf16[16,128,128]{2,1,0:T(8,128)(2,1)S(1)} collective-permute-done((bf16[16,128,128]{2,1,0:T(8,128)(2,1)S(1)}, bf16[16,128,128]{2,1,0:T(8,128)(2,1)S(1)}, u32[]{:S(2)}, u32[]{:S(2)}) %collective-permute-start) | collective-permute-done | bytes 524320 | tf_op jit(solution)/shard_map/ppermute | solution.py:292
  39.1 0.0 copy-done
  39.1 4.7 %near.1 = (bf16[8,128,128]{2,1,0:T(8,128)(2,1)S(1)}, f32[48,128,128]{2,1,0:T(8,128)S(1)}) custom-call(s32[8,512]{1,0:T(8,128)S(1)} %bitcast.1, bf16[16,128,128]{2,1,0:T(8,128)(2,1)S(1)} %get-tuple-element.14.qg_ref, bf16[16,128,128]{2,1,0:T(8,128)(2,1)S(1)} %get-tuple-element.15.own_ref, bf16[16,128,128]{2,1,0:T(8,128)(2,1)S(1)} %collective-permute-done.mate_ref, ...), custom_call_target="tpu_custom_call" | custom-call | flops 1610612736 | bytes 1048576 | tf_op jit(solution)/shard_map/near/pallas_call | solution.py:358
  43.7 0.0 collective-permute-done.2.far_ref
  43.8 4.9 %far.1 = (bf16[8,128,128]{2,1,0:T(8,128)(2,1)S(1)}, f32[16,128,128]{2,1,0:T(8,128)S(1)}, bf16[16,128,128]{2,1,0:T(8,128)(2,1)S(1)}, bf16[16,128,128]{2,1,0:T(8,128)(2,1)S(1)}) custom-call(s32[8,512]{1,0:T(8,128)S(1)} %bitcast.2, bf16[16,128,128]{2,1,0:T(8,128)(2,1)S(1)} %get-tuple-element.14.qg_ref, bf16[16,128,128]{2,1,0:T(8,128)(2,1)S(1)} %get-tuple-element.15.own_ref, ...), custom_call_target="tpu_custom_call" | custom-call | flops 1610612736 | bytes 1048576 | tf_op jit(solution)/shard_map/far/pallas_call | solution.py:371
  48.7 1.3 %collective-permute-start.3 = (bf16[16,128,128]{2,1,0:T(8,128)(2,1)S(1)}, bf16[16,128,128]{2,1,0:T(8,128)(2,1)S(1)}, u32[]{:S(2)}, u32[]{:S(2)}) collective-permute-start(bf16[16,128,128]{2,1,0:T(8,128)(2,1)S(1)} %get-tuple-element.22), channel_id=1, source_target_pairs={{0,4},{4,8},{5,1},{8,12},{9,5},{12,16},{13,9},{16,20},{17,13},{20,... | collective-permute-start | bytes 1572872 | tf_op jit(solution)/shard_map/ppermute | solution.py:292
  50.0 4.6 %collective-permute-start.4 = (bf16[16,128,128]{2,1,0:T(8,128)(2,1)S(1)}, bf16[16,128,128]{2,1,0:T(8,128)(2,1)S(1)}, u32[]{:S(2)}, u32[]{:S(2)}) collective-permute-start(bf16[16,128,128]{2,1,0:T(8,128)(2,1)S(1)} %get-tuple-element.23), channel_id=1, source_target_pairs={{0,1},{1,0},{2,3},{3,2},{4,5},{5,4},{6,7},{7,6},{8,9},{9,8},{10,11... | collective-permute-start | bytes 1572872 | tf_op jit(solution)/shard_map/ppermute | solution.py:292
  54.6 4.2 %collective-permute-done.3.halo_ref = bf16[16,128,128]{2,1,0:T(8,128)(2,1)S(1)} collective-permute-done((bf16[16,128,128]{2,1,0:T(8,128)(2,1)S(1)}, bf16[16,128,128]{2,1,0:T(8,128)(2,1)S(1)}, u32[]{:S(2)}, u32[]{:S(2)}) %collective-permute-start.3) | collective-permute-done | bytes 524320 | tf_op jit(solution)/shard_map/ppermute | solution.py:292
  58.8 0.1 halo_total.1.own_ref
  58.9 0.0 collective-permute-done.4.mate_ref
  58.9 0.1 total.1
  59.0 20.8 %all_to_all.11.in_ref = bf16[32,128,128]{2,1,0:T(8,128)(2,1)S(1)} all-to-all(bf16[32,128,128]{2,1,0:T(8,128)(2,1)S(1)} %total.1), channel_id=1, replica_groups=mesh['x_lo'=2,'y'=4,'z'=16,'x_hi'=2,'core'=2] {'x_hi','core','x_lo','y'}, dimensions={0} | all-to-all | bytes 2097152 | tf_op jit(solution)/shard_map/all_to_all | solution.py:404
  79.9 1.3 %unpack.1 = (bf16[128,1024]{1,0:T(8,128)(2,1)}, bf16[128,1024]{1,0:T(8,128)(2,1)}, bf16[128,1024]{1,0:T(8,128)(2,1)}, bf16[128,1024]{1,0:T(8,128)(2,1)}) custom-call(bf16[32,128,128]{2,1,0:T(8,128)(2,1)S(1)} %all_to_all.11.in_ref), custom_call_target="tpu_custom_call" | custom-call | tf_op jit(solution)/shard_map/unpack/pallas_call | solution.py:406
  (1 shorter events, 0.0 us)
Async XLA Ops:
  30.1 7.1 %collective-permute-start.1 = (bf16[8,128,128]{2,1,0:T(8,128)(2,1)S(1)}, bf16[8,128,128]{2,1,0:T(8,128)(2,1)S(1)}, u32[]{:S(2)}, u32[]{:S(2)}) collective-permute-start(bf16[8,128,128]{2,1,0:T(8,128)(2,1)S(1)} %get-tuple-element.16), channel_id=1, source_target_pairs={{1,5},{4,0},{5,9},{8,4},{9,13},{12,8},{13,17},{16,12},{17,21},{20,... | collective-permute-start | bytes 786440 | tf_op jit(solution)/shard_map/ppermute | solution.py:292
  31.7 12.1 %collective-permute-start.2 = (bf16[8,128,128]{2,1,0:T(8,128)(2,1)S(1)}, bf16[8,128,128]{2,1,0:T(8,128)(2,1)S(1)}, u32[]{:S(2)}, u32[]{:S(2)}) collective-permute-start(bf16[8,128,128]{2,1,0:T(8,128)(2,1)S(1)} %get-tuple-element.18), channel_id=1, source_target_pairs={{1,5},{4,0},{5,9},{8,4},{9,13},{12,8},{13,17},{16,12},{17,21},{20,... | collective-permute-start | bytes 786440 | tf_op jit(solution)/shard_map/ppermute | solution.py:292
  35.3 3.8 %copy-start = (s32[512,8]{0,1:T(8,128)S(1)}, s32[512,8]{0,1:T(8,128)}, u32[]{:S(2)}) copy-start(s32[512,8]{0,1:T(8,128)} %param.9) | copy-start | bytes 49156
  35.3 3.8 %collective-permute-start = (bf16[16,128,128]{2,1,0:T(8,128)(2,1)S(1)}, bf16[16,128,128]{2,1,0:T(8,128)(2,1)S(1)}, u32[]{:S(2)}, u32[]{:S(2)}) collective-permute-start(bf16[16,128,128]{2,1,0:T(8,128)(2,1)S(1)} %get-tuple-element.15.own_ref), channel_id=1, source_target_pairs={{0,1},{1,0},{2,3},{3,2},{4,5},{5,4},{6,7},{7,6},{8,9},{9,8},{10,11... | collective-permute-start | bytes 1572872 | tf_op jit(solution)/shard_map/ppermute | solution.py:292
  48.7 10.1 %collective-permute-start.3 = (bf16[16,128,128]{2,1,0:T(8,128)(2,1)S(1)}, bf16[16,128,128]{2,1,0:T(8,128)(2,1)S(1)}, u32[]{:S(2)}, u32[]{:S(2)}) collective-permute-start(bf16[16,128,128]{2,1,0:T(8,128)(2,1)S(1)} %get-tuple-element.22), channel_id=1, source_target_pairs={{0,4},{4,8},{5,1},{8,12},{9,5},{12,16},{13,9},{16,20},{17,13},{20,... | collective-permute-start | bytes 1572872 | tf_op jit(solution)/shard_map/ppermute | solution.py:292
  50.0 8.9 %collective-permute-start.4 = (bf16[16,128,128]{2,1,0:T(8,128)(2,1)S(1)}, bf16[16,128,128]{2,1,0:T(8,128)(2,1)S(1)}, u32[]{:S(2)}, u32[]{:S(2)}) collective-permute-start(bf16[16,128,128]{2,1,0:T(8,128)(2,1)S(1)} %get-tuple-element.23), channel_id=1, source_target_pairs={{0,1},{1,0},{2,3},{3,2},{4,5},{5,4},{6,7},{7,6},{8,9},{9,8},{10,11... | collective-permute-start | bytes 1572872 | tf_op jit(solution)/shard_map/ppermute | solution.py:292
